TPU v7x, 32 devices: a whole 2x2x4 slice. The times are simulated.
32 devices in a mesh: seq: 16 (over z, x, core), fsdp: 2 (over y).
Axes of the slice: x: 2, y: 2, z: 4, core: 2. Of those that a mesh axis runs over, the one named last changes fastest.
Arguments:
- queries: bfloat16 [2, 2048, 2048], P('fsdp', 'seq'), may hold values from -6 to 6
- key_vectors: bfloat16 [2, 2048, 2048], P('fsdp', 'seq'), may hold values from -6 to 6
- value_vectors: bfloat16 [2, 2048, 2048], P('fsdp', 'seq'), may hold values from -6 to 6
- out_grad: bfloat16 [2, 2048, 2048], P('fsdp', 'seq'), may hold values from -6 to 6
- out_weight: bfloat16 [2048, 2048], P(None, 'fsdp'), may hold values from -0.125 to 0.125
Outputs:
- query_grad: bfloat16 [2, 2048, 2048], P('fsdp', 'seq')
- key_grad: bfloat16 [2, 2048, 2048], P('fsdp', 'seq')
- value_grad: bfloat16 [2, 2048, 2048], P('fsdp', 'seq')
- weight_grad: float32 [2048, 2048], P('seq', 'fsdp')
All inputs are finite; a program needn't handle non-finite values.
Results may differ from a plain program's by a relative error of at most 0.005.
Values may be sent and summed in bfloat16 or wider, within the bound.
No kernel may reach another device: no remote copies, remote signals or barrier semaphores. Data moves between devices by JAX's collectives and lax.ppermute only.
A program may use at most 192 MiB of HBM per device.

v0:
```python
import math

import jax
import jax.numpy as jnp
from jax import lax
from jax.sharding import PartitionSpec as P

HEADS = 16
HEAD_DIM = 128
BLOCK = 128


def carried_in(value, axis, combine, identity, reverse):
    length, here = (lax.axis_size(axis), lax.axis_index(axis))
    everything = lax.all_gather(value, axis)
    start = jnp.broadcast_to(jnp.asarray(identity, value.dtype), value.shape)

    def lap(k, before):
        at = length - 1 - k if reverse else k
        reached = at > here if reverse else at < here
        new = combine(before, everything[at])
        return jnp.where(reached, new, before)

    return lax.fori_loop(0, length, lap, start)


def add_states(earlier, after_dev):
    return earlier + after_dev


def attend(queries, key_vectors, value_vectors, grads, factor):
    batches, tokens, head_count, head_width = queries.shape
    blocks = tokens // BLOCK
    shape_five = (batches, blocks, BLOCK, head_count, head_width)
    query_wide = queries.reshape(shape_five)
    keys_wide = key_vectors.reshape(shape_five)
    values_wide = value_vectors.reshape(shape_five)
    grads_wide = grads.reshape(shape_five)
    single = jnp.float32
    higher = lax.Precision.HIGH
    key_value = jnp.einsum(
        "bnshd,bnshe->bnhde", keys_wide, values_wide, preferred_element_type=single
    )
    query_cot = jnp.einsum(
        "bnthd,bnthe->bnhde", query_wide, grads_wide, preferred_element_type=single
    )
    key_value_dev = jnp.sum(key_value, 1)
    query_cot_dev = jnp.sum(query_cot, 1)
    nothing = jnp.zeros_like(key_value_dev)
    earlier = carried_in(key_value_dev, "seq", add_states, nothing, False)
    after_dev = carried_in(query_cot_dev, "seq", add_states, nothing, True)
    s_before = earlier[:, None] + jnp.cumsum(key_value, 1) - key_value
    g_after = after_dev[:, None] + query_cot_dev[:, None] - jnp.cumsum(query_cot, 1)
    row_index = lax.broadcasted_iota(jnp.int32, (BLOCK, BLOCK), 0)
    col_index = lax.broadcasted_iota(jnp.int32, (BLOCK, BLOCK), 1)
    causal = (row_index >= col_index).astype(jnp.float32)
    scores = jnp.einsum("bnthd,bnshd->bnhts", query_wide, keys_wide, preferred_element_type=single)
    scores = (scores * causal).astype(jnp.bfloat16)
    mixing = jnp.einsum(
        "bnthe,bnshe->bnhts", grads_wide, values_wide, preferred_element_type=single
    )
    mixing = (mixing * causal).astype(jnp.bfloat16)
    attended = jnp.einsum(
        "bnthd,bnhde->bnthe", query_wide.astype(single), s_before, precision=higher
    )
    attended = attended + jnp.einsum(
        "bnhts,bnshe->bnthe", scores, values_wide, preferred_element_type=single
    )
    query_grad = jnp.einsum(
        "bnthe,bnhde->bnthd", grads_wide.astype(single), s_before, precision=higher
    )
    query_grad = query_grad + jnp.einsum(
        "bnhts,bnshd->bnthd", mixing, keys_wide, preferred_element_type=single
    )
    key_grad = jnp.einsum(
        "bnshe,bnhde->bnshd", values_wide.astype(single), g_after, precision=higher
    )
    key_grad = key_grad + jnp.einsum(
        "bnhts,bnthd->bnshd", mixing, query_wide, preferred_element_type=single
    )
    value_grad = jnp.einsum(
        "bnshd,bnhde->bnshe", keys_wide.astype(single), g_after, precision=higher
    )
    value_grad = value_grad + jnp.einsum(
        "bnhts,bnthe->bnshe", scores, grads_wide, preferred_element_type=single
    )
    flat = (batches, tokens, head_count * head_width)
    return (
        factor * attended.reshape(flat),
        factor * query_grad.reshape(flat),
        factor * key_grad.reshape(flat),
        factor * value_grad.reshape(flat),
    )


def split_heads(values_in, head_count):
    return values_in.reshape(values_in.shape[0], values_in.shape[1], head_count, HEAD_DIM)


def body(queries, key_vectors, value_vectors, out_grad, out_weight):
    seq_devices = lax.axis_size("seq")
    fsdp_devices = lax.axis_size("fsdp")
    tokens = queries.shape[1]
    factor = 1.0 / math.sqrt(HEAD_DIM * tokens * seq_devices)
    grad_factor = 1.0 / math.sqrt(fsdp_devices * tokens * seq_devices)
    group_count = HEADS // fsdp_devices
    grads_all = lax.all_gather(out_grad, "fsdp", axis=0, tiled=True)
    grad_attn = jnp.einsum(
        "btd,dc->btc", grads_all, out_weight, preferred_element_type=jnp.float32
    ).astype(jnp.bfloat16)
    moved = (
        lax.all_to_all(queries, "fsdp", split_axis=2, concat_axis=0, tiled=True),
        lax.all_to_all(key_vectors, "fsdp", split_axis=2, concat_axis=0, tiled=True),
        lax.all_to_all(value_vectors, "fsdp", split_axis=2, concat_axis=0, tiled=True),
    )
    attended, query_grad, key_grad, value_grad = attend(
        split_heads(moved[0], group_count),
        split_heads(moved[1], group_count),
        split_heads(moved[2], group_count),
        split_heads(grad_attn, group_count),
        factor,
    )
    returned = (
        lax.all_to_all(
            query_grad.astype(jnp.bfloat16), "fsdp", split_axis=0, concat_axis=2, tiled=True
        ),
        lax.all_to_all(
            key_grad.astype(jnp.bfloat16), "fsdp", split_axis=0, concat_axis=2, tiled=True
        ),
        lax.all_to_all(
            value_grad.astype(jnp.bfloat16), "fsdp", split_axis=0, concat_axis=2, tiled=True
        ),
    )
    attended_low = attended.astype(jnp.bfloat16)
    weight_grad = (
        lax.psum_scatter(
            lax.dot_general(
                grads_all,
                attended_low,
                (((0, 1), (0, 1)), ((), ())),
                preferred_element_type=jnp.float32,
            ),
            "seq",
            scatter_dimension=0,
            tiled=True,
        )
        * grad_factor
    )
    return (returned[0], returned[1], returned[2], weight_grad)


def solution(mesh):
    in_specs = (
        P("fsdp", "seq", None),
        P("fsdp", "seq", None),
        P("fsdp", "seq", None),
        P("fsdp", "seq", None),
        P(None, "fsdp"),
    )
    out_specs = (
        P("fsdp", "seq", None),
        P("fsdp", "seq", None),
        P("fsdp", "seq", None),
        P("seq", "fsdp"),
    )
    return jax.shard_map(body, mesh=mesh, in_specs=in_specs, out_specs=out_specs, check_vma=False)
```

profile of v0, /device:TPU:8, one launch (start us, length us, event | category | flops | bytes accessed | tf_op | source)
XLA Modules:
  0.0 426.4 jit_solution(18435053537939295249)
XLA Ops:
  7.9 2.4 copy.72
  10.8 11.5 %reduce = bf16[2048,128]{1,0:T(8,128)(2,1)S(1)} reduce(bf16[2048,1,128]{2,1,0:T(2,128)(2,1)S(1)} %bitcast.144, bf16[]{:T(256)} %broadcast.48), dimensions={1}, to_apply=%bitcast.92.reduce_sub_computation | reduce | bytes 1048578
  23.2 3.5 all-to-all-start
  26.7 2.4 copy.73
  29.1 11.5 %reduce.1 = bf16[2048,128]{1,0:T(8,128)(2,1)S(1)} reduce(bf16[2048,1,128]{2,1,0:T(2,128)(2,1)S(1)} %bitcast.146, bf16[]{:T(256)} %broadcast.48), dimensions={1}, to_apply=%bitcast.94.reduce_sub_computation | reduce | bytes 1048578
  41.5 3.5 all-to-all-start.1
  45.6 7.6 %all-to-all-done.1 = bf16[2,2,65536]{2,1,0:T(2,128)(2,1)S(1)} async-done(((bf16[2,2,65536]{2,1,0:T(2,128)(2,1)}), bf16[2,2,65536]{2,1,0:T(2,128)(2,1)S(1)}, u32[]{:S(2)}, u32[]{:S(2)}) %all-to-all-start.1) | async-done | bytes 524320 | tf_op jit(solution)/shard_map/all_to_all | solution.py:114
  57.1 11.5 %reduce.2 = bf16[2048,128]{1,0:T(8,128)(2,1)S(1)} reduce(bf16[2048,1,128]{2,1,0:T(2,128)(2,1)S(1)} %bitcast.145, bf16[]{:T(256)} %broadcast.48), dimensions={1}, to_apply=%bitcast.96.reduce_sub_computation | reduce | bytes 1048578
  68.8 9.8 %all_to_all.99 = bf16[2,2,65536]{2,1,0:T(2,128)(2,1)S(1)} all-to-all(bf16[2,2,65536]{2,1,0:T(2,128)(2,1)S(1)} %reshape.157), channel_id=1, replica_groups=mesh['seq'=16,'fsdp'=2] {'fsdp'}, dimensions={0} | all-to-all | bytes 1048576 | tf_op jit(solution)/shard_map/all_to_all | solution.py:112
  79.2 4.0 fusion.15
  85.4 2.5 fusion.14
  87.9 93.6 %all-gather.8.cloned.1.call-done = f32[32,8,128,128]{3,2,1,0:T(8,128)} async-done(((f32[2,8,128,128]{3,2,1,0:T(8,128)}), f32[32,8,128,128]{3,2,1,0:T(8,128)}) %all-gather.8.cloned.1.call-update) | async-done | bytes 16777232 | tf_op jit(solution)/shard_map/all_gather | solution.py:15
  181.5 26.0 %while.30 = (s32[]{:T(128)}, f32[2,8,128,128]{3,2,1,0:T(8,128)S(1)}, s32[]{:T(128)}, f32[16,2,8,128,128]{4,3,2,1,0:T(8,128)}, s32[]{:T(128)}, /*index=5*/s32[]{:T(128)}) while((s32[]{:T(128)}, f32[2,8,128,128]{3,2,1,0:T(8,128)S(1)}, s32[]{:T(128)}, f32[16,2,8,128,128]{4,3,2,1,0:T(8,128)}, s32[]{:T(128)}, /*index=5*/s32[]{:T(128)}) %tuple.92), condition=%wide.region_1.0_spmd.clone, body=%wide.region_0.0_spmd.clone.sunk | while | flops 786436 | bytes 3145821 | solution.py:24
  211.0 5.7 %convolution_bitcast_fusion = f32[2048,1024]{0,1:T(8,128)} fusion(bf16[2,128,1024]{1,2,0:T(8,128)(2,1)S(1)} %bitcast.147, bf16[2,128,2048]{2,1,0:T(8,128)(2,1)} %all-gather.6.cloned.1.call-done), kind=kOutput, calls=%fused_computation.2 | convolution fusion | flops 1073741824 | bytes 9961472 | tf_op jit(solution)/shard_map/dot_general | solution.py:137
  220.4 2.3 fusion.9
  222.7 4.4 %all-to-all-start.2 = ((bf16[2,128,1024]{1,2,0:T(8,128)(2,1)}), bf16[2,128,1024]{1,2,0:T(8,128)(2,1)}, u32[]{:S(2)}, u32[]{:S(2)}) async-start(bf16[2,128,1024]{1,2,0:T(8,128)(2,1)} %bitcast.11), calls=%async_computation.2 | async-start | bytes 1048576 | tf_op jit(solution)/shard_map/all_to_all | solution.py:124
  227.1 81.6 %all-gather.10.cloned.1.call-done = f32[32,8,128,128]{3,2,1,0:T(8,128)} async-done(((f32[2,8,128,128]{3,2,1,0:T(8,128)}), f32[32,8,128,128]{3,2,1,0:T(8,128)}) %all-gather.10.cloned.1.call-update) | async-done | bytes 16777232 | tf_op jit(solution)/shard_map/all_gather | solution.py:15
  308.8 26.9 %while.31 = (s32[]{:T(128)}, f32[2,8,128,128]{3,2,1,0:T(8,128)S(1)}, s32[]{:T(128)}, f32[16,2,8,128,128]{4,3,2,1,0:T(8,128)}, s32[]{:T(128)}, /*index=5*/s32[]{:T(128)}, s32[]{:T(128)}, s32[]{:T(128)}) while((s32[]{:T(128)}, f32[2,8,128,128]{3,2,1,0:T(8,128)S(1)}, s32[]{:T(128)}, f32[16,2,8,128,128]{4,3,2,1,0:T(8,128)}, s32[]{:T(128)}, ...), condition=%wide.region_3.4_spmd.clone, body=%wide.region_2.3_spmd.clone.sunk | while | flops 786440 | bytes 3145883 | solution.py:24
  338.8 3.0 fusion.21
  344.0 3.5 all-to-all-start.5
  349.9 6.3 %all-to-all-done.5 = bf16[2,128,1024]{1,2,0:T(8,128)(2,1)S(1)} async-done(((bf16[2,128,1024]{1,2,0:T(8,128)(2,1)}), bf16[2,128,1024]{1,2,0:T(8,128)(2,1)S(1)}, u32[]{:S(2)}, u32[]{:S(2)}) %all-to-all-start.5) | async-done | bytes 524320 | tf_op jit(solution)/shard_map/all_to_all | solution.py:130
  356.1 3.5 all-to-all-start.4
  362.7 4.8 %all-to-all-done.4 = bf16[2,128,1024]{1,2,0:T(8,128)(2,1)S(1)} async-done(((bf16[2,128,1024]{1,2,0:T(8,128)(2,1)}), bf16[2,128,1024]{1,2,0:T(8,128)(2,1)S(1)}, u32[]{:S(2)}, u32[]{:S(2)}) %all-to-all-start.4) | async-done | bytes 524320 | tf_op jit(solution)/shard_map/all_to_all | solution.py:127
  368.5 49.3 %reduce-scatter.2.cloned.1.call-done = f32[128,1024]{0,1:T(8,128)} async-done(((f32[2048,1024]{0,1:T(8,128)}), f32[128,1024]{0,1:T(8,128)}) %reduce-scatter.2.cloned.1.call-update) | async-done | bytes 524304 | tf_op jit(solution)/shard_map/reduce_scatter | solution.py:136
  (96 shorter events, 83.3 us)
Async XLA Ops:
  7.2 72.0 %all-gather.6.cloned.1.call-start = ((), (), s32[]{:S(2)}) async-start(), calls=%async_computation.7 | async-start | bytes 1572864 | tf_op jit(solution)/shard_map/all_gather | solution.py:107
  22.3 34.0 %copy-start.10 = (bf16[1,128,2048]{2,1,0:T(8,128)(2,1)S(1)}, bf16[1,128,2048]{2,1,0:T(8,128)(2,1)}, u32[]{:S(2)}) copy-start(bf16[1,128,2048]{2,1,0:T(8,128)(2,1)} %param.9) | copy-start | bytes 1572868
  23.2 18.3 %all-to-all-start = ((bf16[2,2,65536]{2,1,0:T(2,128)(2,1)}), bf16[2,2,65536]{2,1,0:T(2,128)(2,1)S(1)}, u32[]{:S(2)}, u32[]{:S(2)}) async-start(bf16[2,2,65536]{2,1,0:T(2,128)(2,1)} %reshape.153), calls=%async_computation | async-start | bytes 1048576 | tf_op jit(solution)/shard_map/all_to_all | solution.py:113
  41.5 11.7 %all-to-all-start.1 = ((bf16[2,2,65536]{2,1,0:T(2,128)(2,1)}), bf16[2,2,65536]{2,1,0:T(2,128)(2,1)S(1)}, u32[]{:S(2)}, u32[]{:S(2)}) async-start(bf16[2,2,65536]{2,1,0:T(2,128)(2,1)} %reshape.155), calls=%async_computation.1 | async-start | bytes 1048576 | tf_op jit(solution)/shard_map/all_to_all | solution.py:114
  45.0 136.5 %all-gather.8.cloned.1.call-start = ((), (), s32[]{:S(2)}) async-start(), calls=%async_computation.9 | async-start | bytes 17825792 | tf_op jit(solution)/shard_map/all_gather | solution.py:15
  45.6 37.6 %copy-start.1 = (bf16[1,128,2048]{1,2,0:T(8,128)(2,1)}, bf16[1,128,2048]{1,2,0:T(8,128)(2,1)S(1)}, u32[]{:S(2)}) copy-start(bf16[1,128,2048]{1,2,0:T(8,128)(2,1)S(1)} %copy.108) | copy-start | bytes 1572868
  53.8 0.8 copy-start.3
  56.1 252.7 %all-gather.10.cloned.1.call-start = ((), (), s32[]{:S(2)}) async-start(), calls=%async_computation.10 | async-start | bytes 17825792 | tf_op jit(solution)/shard_map/all_gather | solution.py:15
  79.2 6.2 %copy-start.5 = (bf16[1,128,2048]{1,2,0:T(8,128)(2,1)}, bf16[1,128,2048]{1,2,0:T(8,128)(2,1)S(1)}, u32[]{:S(2)}) copy-start(bf16[1,128,2048]{1,2,0:T(8,128)(2,1)S(1)} %copy.110) | copy-start | bytes 1572868
  83.5 1.9 copy-start.7
  85.3 332.6 %reduce-scatter.2.cloned.1.call-start = ((), (), s32[]{:S(2)}) async-start(), calls=%async_computation.8 | async-start | bytes 8912896 | tf_op jit(solution)/shard_map/reduce_scatter | solution.py:136
  85.4 122.1 %copy-start = (f32[2,8,128,128]{3,2,1,0:T(8,128)S(1)}, f32[2,8,128,128]{3,2,1,0:T(8,128)}, u32[]{:S(2)}) copy-start(f32[2,8,128,128]{3,2,1,0:T(8,128)} %fusion.23) | copy-start | bytes 3145732
  218.3 2.0 copy-start.8
  222.7 121.3 %all-to-all-start.2 = ((bf16[2,128,1024]{1,2,0:T(8,128)(2,1)}), bf16[2,128,1024]{1,2,0:T(8,128)(2,1)}, u32[]{:S(2)}, u32[]{:S(2)}) async-start(bf16[2,128,1024]{1,2,0:T(8,128)(2,1)} %bitcast.11), calls=%async_computation.2 | async-start | bytes 1048576 | tf_op jit(solution)/shard_map/all_to_all | solution.py:124
  308.8 28.2 %copy-start.2 = (bf16[1,128,2048]{1,2,0:T(8,128)(2,1)S(1)}, bf16[1,128,2048]{1,2,0:T(8,128)(2,1)}, u32[]{:S(2)}) copy-start(bf16[1,128,2048]{1,2,0:T(8,128)(2,1)} %copy-done.1) | copy-start | bytes 1572868
  308.8 30.0 %copy-start.4 = (bf16[1,128,2048]{1,2,0:T(8,128)(2,1)S(1)}, bf16[1,128,2048]{1,2,0:T(8,128)(2,1)}, u32[]{:S(2)}) copy-start(bf16[1,128,2048]{1,2,0:T(8,128)(2,1)} %copy-done.3) | copy-start | bytes 1572868
  337.0 10.5 %copy-start.6 = (bf16[1,128,2048]{1,2,0:T(8,128)(2,1)S(1)}, bf16[1,128,2048]{1,2,0:T(8,128)(2,1)}, u32[]{:S(2)}) copy-start(bf16[1,128,2048]{1,2,0:T(8,128)(2,1)} %copy-done.5) | copy-start | bytes 1572868
  337.0 10.5 %copy-start.9 = (bf16[2,8,128,128]{3,2,1,0:T(8,128)(2,1)S(1)}, bf16[2,8,128,128]{3,2,1,0:T(8,128)(2,1)}, u32[]{:S(2)}) copy-start(bf16[2,8,128,128]{3,2,1,0:T(8,128)(2,1)} %copy-done.8) | copy-start | bytes 1572868
  344.0 12.1 %all-to-all-start.5 = ((bf16[2,128,1024]{1,2,0:T(8,128)(2,1)}), bf16[2,128,1024]{1,2,0:T(8,128)(2,1)S(1)}, u32[]{:S(2)}, u32[]{:S(2)}) async-start(bf16[2,128,1024]{1,2,0:T(8,128)(2,1)} %bitcast.29), calls=%async_computation.5 | async-start | bytes 1048576 | tf_op jit(solution)/shard_map/all_to_all | solution.py:130
  356.1 11.4 %all-to-all-start.4 = ((bf16[2,128,1024]{1,2,0:T(8,128)(2,1)}), bf16[2,128,1024]{1,2,0:T(8,128)(2,1)S(1)}, u32[]{:S(2)}, u32[]{:S(2)}) async-start(bf16[2,128,1024]{1,2,0:T(8,128)(2,1)} %bitcast.23), calls=%async_computation.4 | async-start | bytes 1048576 | tf_op jit(solution)/shard_map/all_to_all | solution.py:127
Sparse Core Ops, SparseCore 0:
  9.5 24.8 all-gather.5
  56.2 125.2 all-gather.7
  183.7 125.0 all-gather.9
  312.7 105.1 reduce-scatter.1
where the time goes:
time: 430 us; the launch traced here: 426 us
  waiting for transfers between devices  244 us (57%)
  other arithmetic  87.8 us (20%)
  matrix products  32.8 us (8%)
  starting transfers between devices  18.7 us (4%)
  local copies, waits for them, and re-layouts  18.3 us (4%)
  between operations  14.1 us (3%)
  blocking collectives  9.78 us (2%)
    all_gather x2, waiting for transfers between devices, carried_in(): everything = lax.all_gather(value, axis)  175 us
    select_n x32, other arithmetic, lap(): return jnp.where(reached, new, before)  52.1 us
    reduce_scatter x1, waiting for transfers between devices, body(): lax.psum_scatter(lax.dot_general(grads_all, attended_low, (((0, 1), (0, 1...  49.3 us
    unnamed x5, other arithmetic  34.6 us
    unnamed x36, local copies, waits for them, and re-layouts  11.4 us
    all_to_all x1, blocking collectives, body(): lax.all_to_all(queries, 'fsdp', split_axis=2, concat_axis=0, tiled=True)  9.78 us
  transfers between devices with their start and end apart: 9, of which 6 were waited for; matrix products, arithmetic and copies ran while one was open for 32% of the time, Pallas kernels for 0%

commit v1 on v0

v1 whole, which is shorter than its diff:
```python
import math

import jax
import jax.numpy as jnp
from jax import lax
from jax.experimental import pallas as pl
from jax.experimental.pallas import tpu as pltpu
from jax.sharding import PartitionSpec as P

HEADS = 16
HEAD_DIM = 128
BLOCK = 128
PLANE = 4
SLOTS = HEADS // PLANE
F32 = jnp.float32
BF16 = jnp.bfloat16
VMEM_LIMIT = 40 * 1024 * 1024


def dot(a, b, contract_a, contract_b):
    dims = (((contract_a,), (contract_b,)), ((), ()))
    return lax.dot_general(a, b, dims, preferred_element_type=F32)


def call(kernel, ids, arrays, outs):
    vmem = pl.BlockSpec(memory_space=pltpu.VMEM)
    return pl.pallas_call(
        kernel,
        out_shape=[jax.ShapeDtypeStruct(shape, dtype) for shape, dtype in outs],
        in_specs=[pl.BlockSpec(memory_space=pltpu.SMEM)] + [vmem] * len(arrays),
        out_specs=[vmem] * len(outs),
        compiler_params=pltpu.CompilerParams(vmem_limit_bytes=VMEM_LIMIT),
    )(ids, *arrays)


def columns(head):
    return pl.ds(pl.multiple_of(head * HEAD_DIM, HEAD_DIM), HEAD_DIM)


def state_kernel(ids, a_ref, b_ref, mine_ref, send_ref):
    x, c = (ids[1], ids[2])
    for other, out in ((0, mine_ref), (1, send_ref)):
        for far in range(2):
            for slot in range(SLOTS):
                head = 4 * slot + 2 * (x ^ far) + (c ^ other)
                state = dot(a_ref[0, :, columns(head)], b_ref[0, :, columns(head)], 0, 0)
                out[far, slot] = state.astype(out.dtype)


def grad_state_kernel(pieces, ids, a_ref, *refs):
    f = ids[3]
    whole_ref, mine_ref, send_ref = refs[pieces:]
    width = refs[0].shape[1]
    for r in range(pieces):
        at = lax.rem(f + r, pieces) * width
        whole_ref[0, :, pl.ds(pl.multiple_of(at, HEAD_DIM), width)] = refs[r][...]
    state_kernel(ids, a_ref, whole_ref, mine_ref, send_ref)


def masked(scores):
    rows = lax.broadcasted_iota(jnp.int32, (BLOCK, BLOCK), 0)
    cols = lax.broadcasted_iota(jnp.int32, (BLOCK, BLOCK), 1)
    return jnp.where(rows >= cols, scores, 0.0).astype(BF16)


def each_head(ids, body):
    x, c = (ids[1], ids[2])
    for other in range(2):
        for far in range(2):
            for slot in range(SLOTS):
                head = 4 * slot + 2 * (x ^ far) + (c ^ other)
                body(other, far, slot, columns(head))


def attended_kernel(pieces, factor, ids, q_ref, k_ref, v_ref, own_ref, got_ref, *outs):
    f, x, c = (ids[3], ids[1], ids[2])
    per = HEADS // pieces
    for r in range(pieces):
        for other, s_ref in ((0, own_ref), (1, got_ref)):
            for t in range(per // 2):
                inner = 2 * t + (c ^ other)
                head = lax.rem(f + r, pieces) * per + inner
                far = ((head >> 1) & 1) ^ x
                cols = columns(head)
                q, k, v = (q_ref[0, :, cols], k_ref[0, :, cols], v_ref[0, :, cols])
                scores = masked(dot(q, k, 1, 1))
                out = dot(q, s_ref[far, head >> 2], 1, 0) + dot(scores, v, 1, 0)
                outs[r][:, columns(inner)] = (factor * out).astype(BF16)


def query_grad_kernel(factor, ids, g_ref, k_ref, v_ref, own_ref, got_ref, out_ref):
    def body(other, far, slot, cols):
        g, k, v = (g_ref[0, :, cols], k_ref[0, :, cols], v_ref[0, :, cols])
        mixing = masked(dot(g, v, 1, 1))
        state = (own_ref, got_ref)[other][far, slot]
        out = dot(g, state, 1, 1) + dot(mixing, k, 1, 0)
        out_ref[0, :, cols] = (factor * out).astype(BF16)

    each_head(ids, body)


def key_value_grad_kernel(
    factor, ids, q_ref, k_ref, v_ref, g_ref, own_ref, got_ref, key_ref, value_ref
):
    def body(other, far, slot, cols):
        q, k = (q_ref[0, :, cols], k_ref[0, :, cols])
        v, g = (v_ref[0, :, cols], g_ref[0, :, cols])
        state = (own_ref, got_ref)[other][far, slot]
        mixing = masked(dot(g, v, 1, 1))
        scores = masked(dot(q, k, 1, 1))
        key = dot(v, state, 1, 1) + dot(mixing, q, 0, 0)
        value = dot(k, state, 1, 0) + dot(scores, g, 0, 0)
        key_ref[0, :, cols] = (factor * key).astype(BF16)
        value_ref[0, :, cols] = (factor * value).astype(BF16)

    each_head(ids, body)


def swap(value, distance, count):
    return lax.ppermute(value, "seq", [(i, i ^ distance) for i in range(count)])


def scan(mine, send, ids, count, reverse):
    x, c = (ids[1], ids[2])
    first_x = (1 - x if reverse else x).astype(F32)
    first_c = (1 - c if reverse else c).astype(F32)
    levels = count // PLANE
    pair = swap(send, 1, count).astype(F32)
    chip = mine + pair
    across = swap(chip[1].astype(BF16), 2, count).astype(F32)
    plane = (chip[0] + across).astype(BF16)
    before = jnp.zeros(plane.shape, F32)
    for step in range(1, levels):
        move = -PLANE * step if reverse else PLANE * step
        route = [(i, i + move) for i in range(count) if 0 <= i + move < count]
        before = before + lax.ppermute(plane, "seq", route).astype(F32)
    near = before + first_x * across
    far = swap((before + (1.0 - first_x) * chip[0]).astype(BF16), 2, count)
    chip_before = jnp.stack([near, far.astype(F32)])
    got = swap((chip_before + (1.0 - first_c) * mine).astype(BF16), 1, count)
    own = (chip_before + first_c * pair).astype(BF16)
    return own, got


def shift(value, r, count):
    return lax.ppermute(value, "fsdp", [(i, (i + r) % count) for i in range(count)])


def body(queries, key_vectors, value_vectors, out_grad, out_weight):
    seq_devices = lax.axis_size("seq")
    fsdp_devices = lax.axis_size("fsdp")
    batches, tokens, width = queries.shape
    rows = out_grad.shape[2] // seq_devices
    levels = seq_devices // PLANE
    piece = out_weight.shape[1]
    factor = 1.0 / math.sqrt(HEAD_DIM * tokens * seq_devices)
    grad_factor = 1.0 / math.sqrt(fsdp_devices * tokens * seq_devices)
    me = lax.axis_index("seq")
    ids = jnp.stack([me // PLANE, (me >> 1) & 1, me & 1, lax.axis_index("fsdp")]).astype(jnp.int32)
    half = (2, SLOTS, HEAD_DIM, HEAD_DIM)

    mine, send = call(state_kernel, ids, (key_vectors, value_vectors), [(half, F32), (half, BF16)])
    grads_all = [out_grad[0]] + [shift(out_grad[0], r, fsdp_devices) for r in range(1, fsdp_devices)]
    s_own, s_got = scan(mine, send, ids, seq_devices, False)

    attn_pieces = []
    for r in range(fsdp_devices):
        part = dot(grads_all[r], out_weight, 1, 0).astype(BF16)
        attn_pieces.append(part if r == 0 else shift(part, -r, fsdp_devices))

    def grad_states(ids, *refs):
        grad_state_kernel(fsdp_devices, ids, *refs)

    grad_attn, g_mine, g_send = call(
        grad_states,
        ids,
        (queries, *attn_pieces),
        [(queries.shape, BF16), (half, F32), (half, BF16)],
    )
    g_own, g_got = scan(g_mine, g_send, ids, seq_devices, True)

    def attended_heads(ids, *refs):
        attended_kernel(fsdp_devices, factor, ids, *refs)

    attended = call(
        attended_heads,
        ids,
        (queries, key_vectors, value_vectors, s_own, s_got),
        [((tokens, piece), BF16)] * fsdp_devices,
    )
    attended_all = [attended[0]] + [
        shift(attended[r], r, fsdp_devices) for r in range(1, fsdp_devices)
    ]

    def query_grads(ids, *refs):
        query_grad_kernel(factor, ids, *refs)

    (query_grad,) = call(
        query_grads,
        ids,
        (grad_attn, key_vectors, value_vectors, s_own, s_got),
        [(queries.shape, BF16)],
    )

    def key_value_grads(ids, *refs):
        key_value_grad_kernel(factor, ids, *refs)

    key_grad, value_grad = call(
        key_value_grads,
        ids,
        (queries, key_vectors, value_vectors, grad_attn, g_own, g_got),
        [(queries.shape, BF16)] * 2,
    )

    features = jnp.concatenate(grads_all).reshape(-1, levels, PLANE, rows)
    features = jnp.roll(features, -ids[0], axis=1)
    member = me % PLANE
    parts = [
        lax.dynamic_index_in_dim(features, member ^ j, 2, keepdims=False).reshape(-1, levels * rows)
        for j in range(PLANE)
    ]
    grads_plane = [parts[0]] + [swap(parts[j], j, seq_devices) for j in range(1, PLANE)]
    near = jnp.concatenate(attended_all)
    across = swap(near, 2, seq_devices)
    pair = swap(near, 1, seq_devices)
    diagonal = swap(across, 1, seq_devices)
    partial = dot(
        jnp.concatenate(grads_plane), jnp.concatenate([near, pair, across, diagonal]), 0, 0
    )
    weight_grad = partial[:rows]
    for r in range(1, levels):
        route = [(i, (i + PLANE * r) % seq_devices) for i in range(seq_devices)]
        chunk = partial[r * rows : (r + 1) * rows].astype(BF16)
        weight_grad = weight_grad + lax.ppermute(chunk, "seq", route).astype(F32)
    return (query_grad, key_grad, value_grad, weight_grad * grad_factor)


def solution(mesh):
    in_specs = (
        P("fsdp", "seq", None),
        P("fsdp", "seq", None),
        P("fsdp", "seq", None),
        P("fsdp", "seq", None),
        P(None, "fsdp"),
    )
    out_specs = (
        P("fsdp", "seq", None),
        P("fsdp", "seq", None),
        P("fsdp", "seq", None),
        P("seq", "fsdp"),
    )
    return jax.shard_map(body, mesh=mesh, in_specs=in_specs, out_specs=out_specs, check_vma=False)
```

time: 430 us -> 111 us (0.26)
  waiting for transfers between devices: 244 us -> 52.4 us
  other arithmetic: 87.8 us -> 4.52 us
  matrix products: 32.8 us -> 4.94 us
  between operations: 14.1 us -> 1.05 us
  local copies, waits for them, and re-layouts: 18.3 us -> 5.67 us
  Pallas kernels: 0 us -> 12.3 us
  starting transfers between devices: 18.7 us -> 29.9 us
  blocking collectives: 9.78 us -> 0 us
    all_gather x3 -> x0, waiting for transfers between devices: 175 us -> none  [the longest x2 175 us: carried_in(): everything = lax.all_gather(value, axis)]
    ppermute x0 -> x26, waiting for transfers between devices: none -> 52.4 us  [the longest x14 18.9 us: swap(): return lax.ppermute(value, 'seq', [(i, i ^ distance) for i in range(count)])]
    select_n x32 -> x0, other arithmetic: 52.1 us -> none  [lap(): return jnp.where(reached, new, before)]
    reduce_scatter x1 -> x0, waiting for transfers between devices: 49.3 us -> none  [body(): lax.psum_scatter(lax.dot_general(grads_all, attended_low, (((0, 1), (0, 1...]
    unnamed x5 -> x0, other arithmetic: 34.6 us -> none
    ppermute x0 -> x26, starting transfers between devices: none -> 29.9 us  [the longest x6 10.3 us: scan(): before = before + lax.ppermute(plane, 'seq', route).astype(F32)]
    dot_general x14 -> x3, matrix products: 32.8 us -> 4.94 us  [dot(): return lax.dot_general(a, b, dims, preferred_element_type=F32)]
    all_to_all x5 -> x0, waiting for transfers between devices: 18.7 us -> none  [the longest x1 7.59 us: body(): lax.all_to_all(value_vectors, 'fsdp', split_axis=2, concat_axis=0, tiled=...]
  transfers between devices with their start and end apart: 9 -> 26, of which waited for: 6 -> 14; matrix products, arithmetic and copies ran while one was open for 32% -> 9% of each run, Pallas kernels for 0% -> 10%
where the time goes in v1:
time: 111 us
  waiting for transfers between devices  52.4 us (47%)
  starting transfers between devices  29.9 us (27%)
  Pallas kernels  12.3 us (11%)
  local copies, waits for them, and re-layouts  5.67 us (5%)
  matrix products  4.94 us (4%)
  other arithmetic  4.52 us (4%)
    ppermute x14, waiting for transfers between devices, swap(): return lax.ppermute(value, 'seq', [(i, i ^ distance) for i in range(count)])  18.9 us
    ppermute x6, waiting for transfers between devices, scan(): before = before + lax.ppermute(plane, 'seq', route).astype(F32)  15.1 us
    ppermute x3, waiting for transfers between devices, body(): weight_grad = weight_grad + lax.ppermute(chunk, 'seq', route).astype(F32)  12.9 us
    pallas_call x5, Pallas kernels, call(): pl.pallas_call(kernel, out_shape=[jax.ShapeDtypeStruct(shape, dtype) for...  12.3 us
    ppermute x6, starting transfers between devices, scan(): before = before + lax.ppermute(plane, 'seq', route).astype(F32)  10.3 us
    ppermute x14, starting transfers between devices, swap(): return lax.ppermute(value, 'seq', [(i, i ^ distance) for i in range(count)])  9.2 us
    ppermute x3, starting transfers between devices, body(): weight_grad = weight_grad + lax.ppermute(chunk, 'seq', route).astype(F32)  5.6 us
    ppermute x3, waiting for transfers between devices, shift(): lax.ppermute(value, 'fsdp', [(i, (i + r) % count) for i in range(count)])  5.52 us
  transfers between devices with their start and end apart: 26, of which 14 were waited for; matrix products, arithmetic and copies ran while one was open for 9% of the time, Pallas kernels for 10%

profile of v1, /device:TPU:8, one launch (start us, length us, event | category | flops | bytes accessed | tf_op | source)
XLA Modules:
  0.0 110.8 jit_solution(15974407209010522365)
XLA Ops:
  3.9 1.5 %collective-permute-done.2 = bf16[2,4,128,128]{3,2,1,0:T(8,128)(2,1)S(1)} collective-permute-done((bf16[2,4,128,128]{3,2,1,0:T(8,128)(2,1)S(1)}, bf16[2,4,128,128]{3,2,1,0:T(8,128)(2,1)S(1)}, u32[]{:S(2)}, u32[]{:S(2)}) %collective-permute-start.2) | collective-permute-done | bytes 262176 | tf_op jit(solution)/shard_map/ppermute | solution.py:120
  6.1 1.5 %collective-permute-start.3 = (bf16[4,128,128]{2,1,0:T(8,128)(2,1)S(1)}, bf16[4,128,128]{2,1,0:T(8,128)(2,1)S(1)}, u32[]{:S(2)}, u32[]{:S(2)}) collective-permute-start(bf16[4,128,128]{2,1,0:T(8,128)(2,1)S(1)} %fusion.22), channel_id=1, source_target_pairs={{0,4},{2,6},{4,0},{6,2},{8,12},{10,14},{12,8},{14,10},{16,20},{18,... | collective-permute-start | bytes 393224 | tf_op jit(solution)/shard_map/ppermute | solution.py:120
  7.9 1.6 %collective-permute-start = (bf16[128,2048]{0,1:T(8,128)(2,1)S(1)}, bf16[128,2048]{0,1:T(8,128)(2,1)S(1)}, u32[]{:S(2)}, u32[]{:S(2)}) collective-permute-start(bf16[128,2048]{0,1:T(8,128)(2,1)S(1)} %bitcast.45), channel_id=1, source_target_pairs={{0,1},{1,0},{2,3},{3,2},{4,5},{5,4},{6,7},{7,6},{8,9},{9,8},{10,11... | collective-permute-start | bytes 1572872 | tf_op jit(solution)/shard_map/ppermute | solution.py:146
  9.5 2.2 %collective-permute-done.3 = bf16[4,128,128]{2,1,0:T(8,128)(2,1)S(1)} collective-permute-done((bf16[4,128,128]{2,1,0:T(8,128)(2,1)S(1)}, bf16[4,128,128]{2,1,0:T(8,128)(2,1)S(1)}, u32[]{:S(2)}, u32[]{:S(2)}) %collective-permute-start.3) | collective-permute-done | bytes 131104 | tf_op jit(solution)/shard_map/ppermute | solution.py:120
  11.7 3.5 %collective-permute-start.4 = (bf16[4,128,128]{2,1,0:T(8,128)(2,1)S(1)}, bf16[4,128,128]{2,1,0:T(8,128)(2,1)S(1)}, u32[]{:S(2)}, u32[]{:S(2)}) collective-permute-start(bf16[4,128,128]{2,1,0:T(8,128)(2,1)S(1)} %fusion.16), channel_id=1, source_target_pairs={{0,8},{2,10},{4,12},{6,14},{8,16},{10,18},{12,20},{14,22},{16,24},... | collective-permute-start | bytes 393224 | tf_op jit(solution)/shard_map/ppermute | solution.py:136
  15.2 2.3 %collective-permute-start.5 = (bf16[4,128,128]{2,1,0:T(8,128)(2,1)S(1)}, bf16[4,128,128]{2,1,0:T(8,128)(2,1)S(1)}, u32[]{:S(2)}, u32[]{:S(2)}) collective-permute-start(bf16[4,128,128]{2,1,0:T(8,128)(2,1)S(1)} %fusion.16), channel_id=1, source_target_pairs={{0,16},{2,18},{4,20},{6,22},{8,24},{10,26},{12,28},{14,30},{1,17},... | collective-permute-start | bytes 393224 | tf_op jit(solution)/shard_map/ppermute | solution.py:136
  18.6 7.5 %collective-permute-done.5 = bf16[4,128,128]{2,1,0:T(8,128)(2,1)S(1)} collective-permute-done((bf16[4,128,128]{2,1,0:T(8,128)(2,1)S(1)}, bf16[4,128,128]{2,1,0:T(8,128)(2,1)S(1)}, u32[]{:S(2)}, u32[]{:S(2)}) %collective-permute-start.5) | collective-permute-done | bytes 131104 | tf_op jit(solution)/shard_map/ppermute | solution.py:136
  26.9 1.5 %collective-permute-start.7 = (bf16[4,128,128]{2,1,0:T(8,128)(2,1)}, bf16[4,128,128]{2,1,0:T(8,128)(2,1)S(1)}, u32[]{:S(2)}, u32[]{:S(2)}) collective-permute-start(bf16[4,128,128]{2,1,0:T(8,128)(2,1)} %get-tuple-element.36), channel_id=1, source_target_pairs={{0,4},{2,6},{4,0},{6,2},{8,12},{10,14},{12,8},{14,10},{16,20},{18,... | collective-permute-start | bytes 393224 | tf_op jit(solution)/shard_map/ppermute | solution.py:120
  29.2 2.9 %convolution_convert_fusion = bf16[128,1024]{1,0:T(8,128)(2,1)S(1)} fusion(bf16[128,2048]{0,1:T(8,128)(2,1)S(1)} %collective-permute-done, bf16[2048,1024]{1,0:T(8,128)(2,1)} %param.9), kind=kOutput, calls=%fused_computation.1 | convolution fusion | flops 537001984 | bytes 4980736 | tf_op jit(solution)/shard_map/dot_general | solution.py:22
  32.2 1.6 %collective-permute-start.1 = (bf16[128,1024]{1,0:T(8,128)(2,1)S(1)}, bf16[128,1024]{1,0:T(8,128)(2,1)S(1)}, u32[]{:S(2)}, u32[]{:S(2)}) collective-permute-start(bf16[128,1024]{1,0:T(8,128)(2,1)S(1)} %convolution_convert_fusion), channel_id=1, source_target_pairs={{0,1},{1,0},{2,3},{3,2},{4,5},{5,4},{6,7},{7,6},{8,9},{9,8},{10,11... | collective-permute-start | bytes 786440 | tf_op jit(solution)/shard_map/ppermute | solution.py:146
  34.5 4.6 %collective-permute-done.1.refs_2_ = bf16[128,1024]{1,0:T(8,128)(2,1)S(1)} collective-permute-done((bf16[128,1024]{1,0:T(8,128)(2,1)S(1)}, bf16[128,1024]{1,0:T(8,128)(2,1)S(1)}, u32[]{:S(2)}, u32[]{:S(2)}) %collective-permute-start.1) | collective-permute-done | bytes 262176 | tf_op jit(solution)/shard_map/ppermute | solution.py:146
  40.4 2.0 %add_convert_fusion.1 = (bf16[2,4,128,128]{3,2,1,0:T(8,128)(2,1)}, bf16[2,4,128,128]{3,2,1,0:T(8,128)(2,1)S(1)}) fusion(f32[2,4,128,128]{3,2,1,0:T(8,128)S(1)} %get-tuple-element.14, f32[1,4,128,128]{3,2,1,0:T(8,128)S(1)} %bitcast_convert_fusion.1, f32[1,4,128,128]{3,2,1,0:T(8,128)} %get-tuple-element.35, f32[]{:T(128)S(6)} %sub.28, ...), kind=kLoop, calls=%fused_computation.27 | loop fusion | flops 1048576 | bytes 1835016 | tf_op jit(solution)/shard_map/convert_element_type | solution.py:140
  46.7 1.6 %collective-permute-start.19 = (bf16[128,1024]{1,0:T(8,128)(2,1)S(1)}, bf16[128,1024]{1,0:T(8,128)(2,1)S(1)}, u32[]{:S(2)}, u32[]{:S(2)}) collective-permute-start(bf16[128,1024]{1,0:T(8,128)(2,1)S(1)} %get-tuple-element.21), channel_id=1, source_target_pairs={{0,1},{1,0},{2,3},{3,2},{4,5},{5,4},{6,7},{7,6},{8,9},{9,8},{10,11... | collective-permute-start | bytes 786440 | tf_op jit(solution)/shard_map/ppermute | solution.py:146
  48.4 1.6 %collective-permute-done.10 = bf16[4,128,128]{2,1,0:T(8,128)(2,1)S(1)} collective-permute-done((bf16[4,128,128]{2,1,0:T(8,128)(2,1)}, bf16[4,128,128]{2,1,0:T(8,128)(2,1)S(1)}, u32[]{:S(2)}, u32[]{:S(2)}) %collective-permute-start.10) | collective-permute-done | bytes 131104 | tf_op jit(solution)/shard_map/ppermute | solution.py:120
  50.1 1.9 %collective-permute-start.11 = (bf16[4,128,128]{2,1,0:T(8,128)(2,1)S(1)}, bf16[4,128,128]{2,1,0:T(8,128)(2,1)S(1)}, u32[]{:S(2)}, u32[]{:S(2)}) collective-permute-start(bf16[4,128,128]{2,1,0:T(8,128)(2,1)S(1)} %fusion.19), channel_id=1, source_target_pairs={{8,0},{10,2},{12,4},{14,6},{16,8},{18,10},{20,12},{22,14},{24,16},... | collective-permute-start | bytes 393224 | tf_op jit(solution)/shard_map/ppermute | solution.py:136
  56.4 7.2 %collective-permute-done.11 = bf16[4,128,128]{2,1,0:T(8,128)(2,1)S(1)} collective-permute-done((bf16[4,128,128]{2,1,0:T(8,128)(2,1)S(1)}, bf16[4,128,128]{2,1,0:T(8,128)(2,1)S(1)}, u32[]{:S(2)}, u32[]{:S(2)}) %collective-permute-start.11) | collective-permute-done | bytes 131104 | tf_op jit(solution)/shard_map/ppermute | solution.py:136
  66.1 6.6 %collective-permute-done.14 = bf16[4,128,128]{2,1,0:T(8,128)(2,1)S(1)} collective-permute-done((bf16[4,128,128]{2,1,0:T(8,128)(2,1)S(1)}, bf16[4,128,128]{2,1,0:T(8,128)(2,1)S(1)}, u32[]{:S(2)}, u32[]{:S(2)}) %collective-permute-start.14) | collective-permute-done | bytes 131104 | tf_op jit(solution)/shard_map/ppermute | solution.py:120
  76.6 4.7 %collective-permute-done.18 = bf16[256,512]{0,1:T(8,128)(2,1)S(1)} collective-permute-done((bf16[256,512]{0,1:T(8,128)(2,1)S(1)}, bf16[256,512]{0,1:T(8,128)(2,1)S(1)}, u32[]{:S(2)}, u32[]{:S(2)}) %collective-permute-start.18) | collective-permute-done | bytes 262176 | tf_op jit(solution)/shard_map/ppermute | solution.py:120
  83.8 2.4 %collective-permute-start.24 = (bf16[128,1024]{1,0:T(8,128)(2,1)S(1)}, bf16[128,1024]{1,0:T(8,128)(2,1)S(1)}, u32[]{:S(2)}, u32[]{:S(2)}) collective-permute-start(bf16[128,1024]{1,0:T(8,128)(2,1)S(1)} %get-tuple-element.28), channel_id=1, source_target_pairs={{0,16},{2,18},{4,20},{6,22},{8,24},{10,26},{12,28},{14,30},{16,0},... | collective-permute-start | bytes 786440 | tf_op jit(solution)/shard_map/ppermute | solution.py:234
  86.3 1.9 %collective-permute-start.25 = (bf16[128,1024]{1,0:T(8,128)(2,1)S(1)}, bf16[128,1024]{1,0:T(8,128)(2,1)S(1)}, u32[]{:S(2)}, u32[]{:S(2)}) collective-permute-start(bf16[128,1024]{1,0:T(8,128)(2,1)S(1)} %get-tuple-element.27), channel_id=1, source_target_pairs={{0,24},{2,26},{4,28},{6,30},{8,0},{10,2},{12,4},{14,6},{16,8},{18,... | collective-permute-start | bytes 786440 | tf_op jit(solution)/shard_map/ppermute | solution.py:234
  88.2 3.2 %shard_map.86 = bf16[1,128,2048]{2,1,0:T(8,128)(2,1)} custom-call(s32[4]{0:T(128)S(1)} %pad_add_fusion.ids, bf16[1,128,2048]{2,1,0:T(8,128)(2,1)S(1)} %get-tuple-element.13.refs_0_.refs_3_, bf16[1,128,2048]{2,1,0:T(8,128)(2,1)S(1)} %copy-done.1, bf16[1,128,2048]{2,1,0:T(8,128)(2,1)S(1)} %copy-done.3, bf16[2,4,128,128]{3,2,1,0:T(8,128)(2,1)S(1)} %get-tuple-element.32.refs_3_, ...), custom_call_target="tpu_custom_call" | custom-call | tf_op jit(solution)/shard_map/pallas_call | solution.py:27
  91.4 5.6 %shard_map.87 = (bf16[1,128,2048]{2,1,0:T(8,128)(2,1)}, bf16[1,128,2048]{2,1,0:T(8,128)(2,1)}) custom-call(s32[4]{0:T(128)S(1)} %pad_add_fusion.ids, bf16[1,128,2048]{2,1,0:T(8,128)(2,1)S(1)} %copy-done.4, bf16[1,128,2048]{2,1,0:T(8,128)(2,1)S(1)} %copy-done.1, bf16[1,128,2048]{2,1,0:T(8,128)(2,1)S(1)} %copy-done.3, ...), custom_call_target="tpu_custom_call" | custom-call | tf_op jit(solution)/shard_map/pallas_call | solution.py:27
  97.0 9.7 %collective-permute-done.24 = bf16[128,1024]{1,0:T(8,128)(2,1)S(1)} collective-permute-done((bf16[128,1024]{1,0:T(8,128)(2,1)S(1)}, bf16[128,1024]{1,0:T(8,128)(2,1)S(1)}, u32[]{:S(2)}, u32[]{:S(2)}) %collective-permute-start.24) | collective-permute-done | bytes 262176 | tf_op jit(solution)/shard_map/ppermute | solution.py:234
  106.8 3.1 %collective-permute-done.25 = bf16[128,1024]{1,0:T(8,128)(2,1)S(1)} collective-permute-done((bf16[128,1024]{1,0:T(8,128)(2,1)S(1)}, bf16[128,1024]{1,0:T(8,128)(2,1)S(1)}, u32[]{:S(2)}, u32[]{:S(2)}) %collective-permute-start.25) | collective-permute-done | bytes 262176 | tf_op jit(solution)/shard_map/ppermute | solution.py:234
  (91 shorter events, 27.5 us)
Async XLA Ops:
  6.1 5.5 %collective-permute-start.3 = (bf16[4,128,128]{2,1,0:T(8,128)(2,1)S(1)}, bf16[4,128,128]{2,1,0:T(8,128)(2,1)S(1)}, u32[]{:S(2)}, u32[]{:S(2)}) collective-permute-start(bf16[4,128,128]{2,1,0:T(8,128)(2,1)S(1)} %fusion.22), channel_id=1, source_target_pairs={{0,4},{2,6},{4,0},{6,2},{8,12},{10,14},{12,8},{14,10},{16,20},{18,... | collective-permute-start | bytes 393224 | tf_op jit(solution)/shard_map/ppermute | solution.py:120
  7.9 20.5 %collective-permute-start = (bf16[128,2048]{0,1:T(8,128)(2,1)S(1)}, bf16[128,2048]{0,1:T(8,128)(2,1)S(1)}, u32[]{:S(2)}, u32[]{:S(2)}) collective-permute-start(bf16[128,2048]{0,1:T(8,128)(2,1)S(1)} %bitcast.45), channel_id=1, source_target_pairs={{0,1},{1,0},{2,3},{3,2},{4,5},{5,4},{6,7},{7,6},{8,9},{9,8},{10,11... | collective-permute-start | bytes 1572872 | tf_op jit(solution)/shard_map/ppermute | solution.py:146
  11.7 6.9 %collective-permute-start.4 = (bf16[4,128,128]{2,1,0:T(8,128)(2,1)S(1)}, bf16[4,128,128]{2,1,0:T(8,128)(2,1)S(1)}, u32[]{:S(2)}, u32[]{:S(2)}) collective-permute-start(bf16[4,128,128]{2,1,0:T(8,128)(2,1)S(1)} %fusion.16), channel_id=1, source_target_pairs={{0,8},{2,10},{4,12},{6,14},{8,16},{10,18},{12,20},{14,22},{16,24},... | collective-permute-start | bytes 393224 | tf_op jit(solution)/shard_map/ppermute | solution.py:136
  15.2 10.9 %collective-permute-start.5 = (bf16[4,128,128]{2,1,0:T(8,128)(2,1)S(1)}, bf16[4,128,128]{2,1,0:T(8,128)(2,1)S(1)}, u32[]{:S(2)}, u32[]{:S(2)}) collective-permute-start(bf16[4,128,128]{2,1,0:T(8,128)(2,1)S(1)} %fusion.16), channel_id=1, source_target_pairs={{0,16},{2,18},{4,20},{6,22},{8,24},{10,26},{12,28},{14,30},{1,17},... | collective-permute-start | bytes 393224 | tf_op jit(solution)/shard_map/ppermute | solution.py:136
  17.5 8.6 %collective-permute-start.6 = (bf16[4,128,128]{2,1,0:T(8,128)(2,1)S(1)}, bf16[4,128,128]{2,1,0:T(8,128)(2,1)S(1)}, u32[]{:S(2)}, u32[]{:S(2)}) collective-permute-start(bf16[4,128,128]{2,1,0:T(8,128)(2,1)S(1)} %fusion.16), channel_id=1, source_target_pairs={{0,24},{2,26},{4,28},{6,30},{1,25},{3,27},{5,29},{7,31}} | collective-permute-start | bytes 393224 | tf_op jit(solution)/shard_map/ppermute | solution.py:136
  26.9 13.4 %collective-permute-start.7 = (bf16[4,128,128]{2,1,0:T(8,128)(2,1)}, bf16[4,128,128]{2,1,0:T(8,128)(2,1)S(1)}, u32[]{:S(2)}, u32[]{:S(2)}) collective-permute-start(bf16[4,128,128]{2,1,0:T(8,128)(2,1)} %get-tuple-element.36), channel_id=1, source_target_pairs={{0,4},{2,6},{4,0},{6,2},{8,12},{10,14},{12,8},{14,10},{16,20},{18,... | collective-permute-start | bytes 393224 | tf_op jit(solution)/shard_map/ppermute | solution.py:120
  32.2 7.0 %collective-permute-start.1 = (bf16[128,1024]{1,0:T(8,128)(2,1)S(1)}, bf16[128,1024]{1,0:T(8,128)(2,1)S(1)}, u32[]{:S(2)}, u32[]{:S(2)}) collective-permute-start(bf16[128,1024]{1,0:T(8,128)(2,1)S(1)} %convolution_convert_fusion), channel_id=1, source_target_pairs={{0,1},{1,0},{2,3},{3,2},{4,5},{5,4},{6,7},{7,6},{8,9},{9,8},{10,11... | collective-permute-start | bytes 786440 | tf_op jit(solution)/shard_map/ppermute | solution.py:146
  42.3 2.9 %collective-permute-start.8 = (bf16[2,4,128,128]{3,2,1,0:T(8,128)(2,1)}, bf16[2,4,128,128]{3,2,1,0:T(8,128)(2,1)S(1)}, u32[]{:S(2)}, u32[]{:S(2)}) collective-permute-start(bf16[2,4,128,128]{3,2,1,0:T(8,128)(2,1)} %get-tuple-element.31), channel_id=1, source_target_pairs={{0,2},{2,0},{4,6},{6,4},{8,10},{10,8},{12,14},{14,12},{16,18},{18,... | collective-permute-start | bytes 786440 | tf_op jit(solution)/shard_map/ppermute | solution.py:120
  44.3 5.7 %collective-permute-start.10 = (bf16[4,128,128]{2,1,0:T(8,128)(2,1)}, bf16[4,128,128]{2,1,0:T(8,128)(2,1)S(1)}, u32[]{:S(2)}, u32[]{:S(2)}) collective-permute-start(bf16[4,128,128]{2,1,0:T(8,128)(2,1)} %fusion.23), channel_id=1, source_target_pairs={{0,4},{2,6},{4,0},{6,2},{8,12},{10,14},{12,8},{14,10},{16,20},{18,... | collective-permute-start | bytes 393224 | tf_op jit(solution)/shard_map/ppermute | solution.py:120
  46.7 8.1 %collective-permute-start.19 = (bf16[128,1024]{1,0:T(8,128)(2,1)S(1)}, bf16[128,1024]{1,0:T(8,128)(2,1)S(1)}, u32[]{:S(2)}, u32[]{:S(2)}) collective-permute-start(bf16[128,1024]{1,0:T(8,128)(2,1)S(1)} %get-tuple-element.21), channel_id=1, source_target_pairs={{0,1},{1,0},{2,3},{3,2},{4,5},{5,4},{6,7},{7,6},{8,9},{9,8},{10,11... | collective-permute-start | bytes 786440 | tf_op jit(solution)/shard_map/ppermute | solution.py:146
  50.1 13.6 %collective-permute-start.11 = (bf16[4,128,128]{2,1,0:T(8,128)(2,1)S(1)}, bf16[4,128,128]{2,1,0:T(8,128)(2,1)S(1)}, u32[]{:S(2)}, u32[]{:S(2)}) collective-permute-start(bf16[4,128,128]{2,1,0:T(8,128)(2,1)S(1)} %fusion.19), channel_id=1, source_target_pairs={{8,0},{10,2},{12,4},{14,6},{16,8},{18,10},{20,12},{22,14},{24,16},... | collective-permute-start | bytes 393224 | tf_op jit(solution)/shard_map/ppermute | solution.py:136
  52.0 11.7 %collective-permute-start.12 = (bf16[4,128,128]{2,1,0:T(8,128)(2,1)S(1)}, bf16[4,128,128]{2,1,0:T(8,128)(2,1)S(1)}, u32[]{:S(2)}, u32[]{:S(2)}) collective-permute-start(bf16[4,128,128]{2,1,0:T(8,128)(2,1)S(1)} %fusion.19), channel_id=1, source_target_pairs={{16,0},{18,2},{20,4},{22,6},{24,8},{26,10},{28,12},{30,14},{17,1},... | collective-permute-start | bytes 393224 | tf_op jit(solution)/shard_map/ppermute | solution.py:136
  53.3 10.4 %collective-permute-start.13 = (bf16[4,128,128]{2,1,0:T(8,128)(2,1)S(1)}, bf16[4,128,128]{2,1,0:T(8,128)(2,1)S(1)}, u32[]{:S(2)}, u32[]{:S(2)}) collective-permute-start(bf16[4,128,128]{2,1,0:T(8,128)(2,1)S(1)} %fusion.19), channel_id=1, source_target_pairs={{24,0},{26,2},{28,4},{30,6},{25,1},{27,3},{29,5},{31,7}} | collective-permute-start | bytes 393224 | tf_op jit(solution)/shard_map/ppermute | solution.py:136
  54.9 17.7 %collective-permute-start.21 = (bf16[256,1024]{1,0:T(8,128)(2,1)S(1)}, bf16[256,1024]{1,0:T(8,128)(2,1)S(1)}, u32[]{:S(2)}, u32[]{:S(2)}) collective-permute-start(bf16[256,1024]{1,0:T(8,128)(2,1)S(1)} %get-tuple-element.37), channel_id=1, source_target_pairs={{0,4},{2,6},{4,0},{6,2},{8,12},{10,14},{12,8},{14,10},{16,20},{18,... | collective-permute-start | bytes 1572872 | tf_op jit(solution)/shard_map/ppermute | solution.py:120
  56.3 17.7 %collective-permute-start.20 = (bf16[256,1024]{1,0:T(8,128)(2,1)S(1)}, bf16[256,1024]{1,0:T(8,128)(2,1)S(1)}, u32[]{:S(2)}, u32[]{:S(2)}) collective-permute-start(bf16[256,1024]{1,0:T(8,128)(2,1)S(1)} %get-tuple-element.37), channel_id=1, source_target_pairs={{0,2},{2,0},{4,6},{6,4},{8,10},{10,8},{12,14},{14,12},{16,18},{18,... | collective-permute-start | bytes 1572872 | tf_op jit(solution)/shard_map/ppermute | solution.py:120
  63.7 8.9 %collective-permute-start.14 = (bf16[4,128,128]{2,1,0:T(8,128)(2,1)S(1)}, bf16[4,128,128]{2,1,0:T(8,128)(2,1)S(1)}, u32[]{:S(2)}, u32[]{:S(2)}) collective-permute-start(bf16[4,128,128]{2,1,0:T(8,128)(2,1)S(1)} %get-tuple-element.34), channel_id=1, source_target_pairs={{0,4},{2,6},{4,0},{6,2},{8,12},{10,14},{12,8},{14,10},{16,20},{18,... | collective-permute-start | bytes 393224 | tf_op jit(solution)/shard_map/ppermute | solution.py:120
  64.8 10.6 %collective-permute-start.16 = (bf16[256,512]{0,1:T(8,128)(2,1)S(1)}, bf16[256,512]{0,1:T(8,128)(2,1)S(1)}, u32[]{:S(2)}, u32[]{:S(2)}) collective-permute-start(bf16[256,512]{0,1:T(8,128)(2,1)S(1)} %bitcast.50), channel_id=1, source_target_pairs={{0,2},{2,0},{4,6},{6,4},{8,10},{10,8},{12,14},{14,12},{16,18},{18,... | collective-permute-start | bytes 786440 | tf_op jit(solution)/shard_map/ppermute | solution.py:120
  64.9 11.7 %collective-permute-start.17 = (bf16[256,512]{0,1:T(8,128)(2,1)S(1)}, bf16[256,512]{0,1:T(8,128)(2,1)S(1)}, u32[]{:S(2)}, u32[]{:S(2)}) collective-permute-start(bf16[256,512]{0,1:T(8,128)(2,1)S(1)} %bitcast.49), channel_id=1, source_target_pairs={{0,4},{2,6},{4,0},{6,2},{8,12},{10,14},{12,8},{14,10},{16,20},{18,... | collective-permute-start | bytes 786440 | tf_op jit(solution)/shard_map/ppermute | solution.py:120
  72.6 8.7 %collective-permute-start.18 = (bf16[256,512]{0,1:T(8,128)(2,1)S(1)}, bf16[256,512]{0,1:T(8,128)(2,1)S(1)}, u32[]{:S(2)}, u32[]{:S(2)}) collective-permute-start(bf16[256,512]{0,1:T(8,128)(2,1)S(1)} %bitcast.48), channel_id=1, source_target_pairs={{0,6},{2,4},{4,2},{6,0},{8,14},{10,12},{12,10},{14,8},{16,22},{18,... | collective-permute-start | bytes 786440 | tf_op jit(solution)/shard_map/ppermute | solution.py:120
  72.6 2.7 %collective-permute-start.22 = (bf16[256,1024]{1,0:T(8,128)(2,1)S(1)}, bf16[256,1024]{1,0:T(8,128)(2,1)S(1)}, u32[]{:S(2)}, u32[]{:S(2)}) collective-permute-start(bf16[256,1024]{1,0:T(8,128)(2,1)S(1)} %collective-permute-done.21), channel_id=1, source_target_pairs={{0,2},{2,0},{4,6},{6,4},{8,10},{10,8},{12,14},{14,12},{16,18},{18,... | collective-permute-start | bytes 1572872 | tf_op jit(solution)/shard_map/ppermute | solution.py:120
  74.0 17.4 %collective-permute-start.15 = (bf16[2,4,128,128]{3,2,1,0:T(8,128)(2,1)S(1)}, bf16[2,4,128,128]{3,2,1,0:T(8,128)(2,1)S(1)}, u32[]{:S(2)}, u32[]{:S(2)}) collective-permute-start(bf16[2,4,128,128]{3,2,1,0:T(8,128)(2,1)S(1)} %get-tuple-element.29), channel_id=1, source_target_pairs={{0,2},{2,0},{4,6},{6,4},{8,10},{10,8},{12,14},{14,12},{16,18},{18,... | collective-permute-start | bytes 786440 | tf_op jit(solution)/shard_map/ppermute | solution.py:120
  82.6 14.4 %collective-permute-start.23 = (bf16[128,1024]{1,0:T(8,128)(2,1)S(1)}, bf16[128,1024]{1,0:T(8,128)(2,1)S(1)}, u32[]{:S(2)}, u32[]{:S(2)}) collective-permute-start(bf16[128,1024]{1,0:T(8,128)(2,1)S(1)} %get-tuple-element.26), channel_id=1, source_target_pairs={{0,8},{2,10},{4,12},{6,14},{8,16},{10,18},{12,20},{14,22},{16,24},... | collective-permute-start | bytes 786440 | tf_op jit(solution)/shard_map/ppermute | solution.py:234
  83.8 22.9 %collective-permute-start.24 = (bf16[128,1024]{1,0:T(8,128)(2,1)S(1)}, bf16[128,1024]{1,0:T(8,128)(2,1)S(1)}, u32[]{:S(2)}, u32[]{:S(2)}) collective-permute-start(bf16[128,1024]{1,0:T(8,128)(2,1)S(1)} %get-tuple-element.28), channel_id=1, source_target_pairs={{0,16},{2,18},{4,20},{6,22},{8,24},{10,26},{12,28},{14,30},{16,0},... | collective-permute-start | bytes 786440 | tf_op jit(solution)/shard_map/ppermute | solution.py:234
  86.3 23.6 %collective-permute-start.25 = (bf16[128,1024]{1,0:T(8,128)(2,1)S(1)}, bf16[128,1024]{1,0:T(8,128)(2,1)S(1)}, u32[]{:S(2)}, u32[]{:S(2)}) collective-permute-start(bf16[128,1024]{1,0:T(8,128)(2,1)S(1)} %get-tuple-element.27), channel_id=1, source_target_pairs={{0,24},{2,26},{4,28},{6,30},{8,0},{10,2},{12,4},{14,6},{16,8},{18,... | collective-permute-start | bytes 786440 | tf_op jit(solution)/shard_map/ppermute | solution.py:234
  (18 other events, 106.9 us)

commit v2 on v1

v2 whole, which is shorter than its diff:
```python
import math

import jax
import jax.numpy as jnp
from jax import lax
from jax.experimental import pallas as pl
from jax.experimental.pallas import tpu as pltpu
from jax.sharding import PartitionSpec as P

HEADS = 16
HEAD_DIM = 128
BLOCK = 128
PLANE = 4
SLOTS = HEADS // PLANE
F32 = jnp.float32
BF16 = jnp.bfloat16
RAN = ((8, 128), F32)
VMEM_LIMIT = 16 * 1024 * 1024


def dot(a, b, contract_a, contract_b):
    dims = (((contract_a,), (contract_b,)), ((), ()))
    return lax.dot_general(a, b, dims, preferred_element_type=F32)


def call(kernel, ids, arrays, outs, after=()):
    vmem = pl.BlockSpec(memory_space=pltpu.VMEM)
    first, last = (1 + len(arrays), 1 + len(arrays) + len(after))

    def run(*refs):
        kernel(*refs[:first], *refs[last:])

    return pl.pallas_call(
        run,
        out_shape=[jax.ShapeDtypeStruct(shape, dtype) for shape, dtype in outs],
        in_specs=[pl.BlockSpec(memory_space=pltpu.SMEM)]
        + [vmem] * len(arrays)
        + [pl.BlockSpec(memory_space=pl.ANY)] * len(after),
        out_specs=[vmem] * len(outs),
        compiler_params=pltpu.CompilerParams(vmem_limit_bytes=VMEM_LIMIT),
    )(ids, *arrays, *after)


def columns(head):
    return pl.ds(pl.multiple_of(head * HEAD_DIM, HEAD_DIM), HEAD_DIM)


def each_head(ids, body):
    x, c = (ids[1], ids[2])
    for other in range(2):
        for far in range(2):
            for slot in range(SLOTS):
                head = 4 * slot + 2 * (x ^ far) + (c ^ other)
                body(other, far, slot, columns(head))


def state_kernel(ids, a_ref, b_ref, mine_ref, send_ref):
    def body(other, far, slot, cols):
        state = dot(a_ref[0, :, cols], b_ref[0, :, cols], 0, 0)
        out = (mine_ref, send_ref)[other]
        out[far, slot] = state.astype(out.dtype)

    each_head(ids, body)


def grad_state_kernel(pieces, ids, a_ref, *refs):
    whole_ref, mine_ref, send_ref = refs[pieces:]
    width = refs[0].shape[1]
    for r in range(pieces):
        at = lax.rem(ids[3] + r, pieces) * width
        whole_ref[0, :, pl.ds(pl.multiple_of(at, HEAD_DIM), width)] = refs[r][...]
    state_kernel(ids, a_ref, whole_ref, mine_ref, send_ref)


def masked(scores):
    rows = lax.broadcasted_iota(jnp.int32, (BLOCK, BLOCK), 0)
    cols = lax.broadcasted_iota(jnp.int32, (BLOCK, BLOCK), 1)
    return jnp.where(rows >= cols, scores, 0.0).astype(BF16)


def attended_kernel(pieces, factor, ids, q_ref, k_ref, v_ref, own_ref, got_ref, *outs):
    f, x, c = (ids[3], ids[1], ids[2])
    per = HEADS // pieces
    for r in range(pieces):
        for other, s_ref in ((0, own_ref), (1, got_ref)):
            for t in range(per // 2):
                inner = 2 * t + (c ^ other)
                head = lax.rem(f + r, pieces) * per + inner
                far = ((head >> 1) & 1) ^ x
                cols = columns(head)
                q, k, v = (q_ref[0, :, cols], k_ref[0, :, cols], v_ref[0, :, cols])
                scores = masked(dot(q, k, 1, 1))
                out = dot(q, s_ref[far, head >> 2], 1, 0) + dot(scores, v, 1, 0)
                outs[r][:, columns(inner)] = (factor * out).astype(BF16)


def block_kernel(
    factor,
    ids,
    q_ref,
    k_ref,
    v_ref,
    g_ref,
    own_ref,
    got_ref,
    query_ref,
    key_ref,
    value_ref,
    ran_ref,
):
    def body(other, far, slot, cols):
        q, k = (q_ref[0, :, cols], k_ref[0, :, cols])
        v, g = (v_ref[0, :, cols], g_ref[0, :, cols])
        mixing = masked(dot(g, v, 1, 1))
        scores = masked(dot(q, k, 1, 1))
        state = (own_ref, got_ref)[other][far, slot]
        query = dot(g, state, 1, 1) + dot(mixing, k, 1, 0)
        query_ref[0, :, cols] = (factor * query).astype(BF16)
        key_ref[:, cols] = dot(mixing, q, 0, 0)
        value_ref[:, cols] = dot(scores, g, 0, 0)

    each_head(ids, body)
    ran_ref[...] = jnp.zeros_like(ran_ref)


def later_kernel(
    factor, ids, k_ref, v_ref, key_in, value_in, own_ref, got_ref, key_ref, value_ref
):
    def body(other, far, slot, cols):
        k, v = (k_ref[0, :, cols], v_ref[0, :, cols])
        state = (own_ref, got_ref)[other][far, slot]
        key = dot(v, state, 1, 1) + key_in[:, cols]
        value = dot(k, state, 1, 0) + value_in[:, cols]
        key_ref[0, :, cols] = (factor * key).astype(BF16)
        value_ref[0, :, cols] = (factor * value).astype(BF16)

    each_head(ids, body)


def features_kernel(levels, ids, in_ref, here_ref, there_ref):
    z, member = (ids[0], 2 * ids[1] + ids[2])
    rows = in_ref.shape[1] // (levels * PLANE)
    for j in range(PLANE):
        out = (here_ref, there_ref)[j // 2]
        for step in range(levels):
            at = ((z ^ step) * PLANE + (member ^ j)) * rows
            block = in_ref[:, pl.ds(pl.multiple_of(at, HEAD_DIM), rows)]
            out[j % 2, :, step * rows : (step + 1) * rows] = block


def features(grads, ids, levels, after=()):
    tokens, width = grads.shape
    rows = width // (levels * PLANE)
    if rows % HEAD_DIM == 0:

        def run(ids, *refs):
            features_kernel(levels, ids, *refs)

        return call(run, ids, (grads,), [((2, tokens, levels * rows), BF16)] * 2, after)
    order = jnp.arange(levels) ^ ids[0]
    members = jnp.arange(PLANE) ^ (2 * ids[1] + ids[2])
    parts = jnp.take(grads.reshape(tokens, levels, PLANE, rows), order, axis=1)
    parts = jnp.take(parts, members, axis=2).transpose(2, 0, 1, 3)
    parts = parts.reshape(PLANE, tokens, levels * rows)
    return parts[:2], parts[2:]


def chip_rows_kernel(ids, here_ref, there_ref, *outs):
    tokens = here_ref.shape[1]
    for core, out in enumerate(outs):
        out[:tokens] = here_ref[core]
        out[tokens:] = there_ref[core]


def stack_kernel(ids, *refs):
    rows = refs[0].shape[0]
    for at, ref in enumerate(refs[:-1]):
        refs[-1][at * rows : (at + 1) * rows] = ref[...]


def swap(value, distance, count):
    return lax.ppermute(value, "seq", [(i, i ^ distance) for i in range(count)])


def shift(value, r, count):
    return lax.ppermute(value, "fsdp", [(i, (i + r) % count) for i in range(count)])


def shift_across(value, r, count, devices):
    route = [
        (i * count + f, (i ^ 2) * count + (f + r) % count) for i in range(devices) for f in range(count)
    ]
    return lax.ppermute(value, ("seq", "fsdp"), route)


def chip_kernel(ids, mine_ref, pair_ref, near_ref, send_ref):
    near_ref[...] = mine_ref[0] + pair_ref[0].astype(F32)
    send_ref[...] = (mine_ref[1] + pair_ref[1].astype(F32)).astype(BF16)


def sum_kernel(ids, a_ref, b_ref, out_ref):
    out_ref[...] = (a_ref[...].astype(F32) + b_ref[...].astype(F32)).astype(BF16)


def before_kernel(reverse, ids, chip_ref, across_ref, *refs):
    near_ref, send_ref = refs[-2:]
    before = refs[0][...].astype(F32)
    for ref in refs[1:-2]:
        before = before + ref[...].astype(F32)
    second = (1 - ids[1] if reverse else ids[1]) == 1
    near_ref[...] = before + jnp.where(second, across_ref[...].astype(F32), 0.0)
    send_ref[...] = (before + jnp.where(second, 0.0, chip_ref[...])).astype(BF16)


def core_kernel(reverse, ids, near_ref, far_ref, mine_ref, pair_ref, own_ref, send_ref):
    second = (1 - ids[2] if reverse else ids[2]) == 1
    for at, ref in ((0, near_ref), (1, far_ref)):
        before = ref[...].astype(F32)
        own = before + jnp.where(second, pair_ref[at].astype(F32), 0.0)
        send = before + jnp.where(second, 0.0, mine_ref[at])
        own_ref[at] = own.astype(BF16)
        send_ref[at] = send.astype(BF16)


class Scan:
    def __init__(self, mine, send, ids, count, reverse, doubling):
        self.mine, self.ids, self.count = (mine, ids, count)
        self.reverse, self.doubling = (reverse, doubling)
        self.quarter = (SLOTS, HEAD_DIM, HEAD_DIM)
        self.pair = swap(send, 1, count)

    def chip(self, after=()):
        outs = [(self.quarter, F32), (self.quarter, BF16)]
        self.total, to_x = call(chip_kernel, self.ids, (self.mine, self.pair), outs, after)
        self.across = swap(to_x, 2, self.count)
        return self.total

    def along(self, value, step):
        move = -PLANE * step if self.reverse else PLANE * step
        route = [(i, i + move) for i in range(self.count) if 0 <= i + move < self.count]
        return lax.ppermute(value, "seq", route)

    def plane(self, after=()):
        outs = [(self.quarter, BF16)]
        (self.summed,) = call(sum_kernel, self.ids, (self.total, self.across), outs, after)
        steps = [1] if self.doubling else range(1, self.count // PLANE)
        self.got = [self.along(self.summed, step) for step in steps]
        return self.summed

    def double(self, after=()):
        step = 2
        while step < self.count // PLANE:
            outs = [(self.quarter, BF16)]
            (self.summed,) = call(sum_kernel, self.ids, (self.summed, self.got[-1]), outs, after)
            self.got.append(self.along(self.summed, step))
            step *= 2
        return self.summed

    def before(self, after=()):
        def befores(ids, *refs):
            before_kernel(self.reverse, ids, *refs)

        outs = [(self.quarter, F32), (self.quarter, BF16)]
        arrays = (self.total, self.across, *self.got)
        self.near, to_x = call(befores, self.ids, arrays, outs, after)
        self.far = swap(to_x, 2, self.count)
        return self.near

    def core(self, after=()):
        def cores(ids, *refs):
            core_kernel(self.reverse, ids, *refs)

        outs = [((2, *self.quarter), BF16)] * 2
        arrays = (self.near, self.far, self.mine, self.pair)
        own, to_core = call(cores, self.ids, arrays, outs, after)
        return own, swap(to_core, 1, self.count)


def body(queries, key_vectors, value_vectors, out_grad, out_weight):
    seq_devices = lax.axis_size("seq")
    fsdp_devices = lax.axis_size("fsdp")
    batches, tokens, width = queries.shape
    rows = out_grad.shape[2] // seq_devices
    levels = seq_devices // PLANE
    piece = out_weight.shape[1]
    factor = 1.0 / math.sqrt(HEAD_DIM * tokens * seq_devices)
    grad_factor = 1.0 / math.sqrt(fsdp_devices * tokens * seq_devices)
    me = lax.axis_index("seq")
    ids = jnp.stack([me // PLANE, (me >> 1) & 1, me & 1, lax.axis_index("fsdp")]).astype(jnp.int32)
    half = (2, SLOTS, HEAD_DIM, HEAD_DIM)
    others = range(1, fsdp_devices)

    grads_own = out_grad[0]
    grads_got = [shift(grads_own, r, fsdp_devices) for r in others]
    mine, send = call(state_kernel, ids, (key_vectors, value_vectors), [(half, F32), (half, BF16)])
    s_scan = Scan(mine, send, ids, seq_devices, False, False)
    s_total = s_scan.chip()
    attn_own = dot(grads_own, out_weight, 1, 0).astype(BF16)
    here, there = features(grads_own, ids, levels, after=(s_total,))
    there = swap(there, 2, seq_devices)
    s_plane = s_scan.plane(after=(attn_own,))
    attn_got = [dot(grads, out_weight, 1, 0).astype(BF16) for grads in grads_got]
    attn_back = [shift(attn_got[r - 1], -r, fsdp_devices) for r in others]
    mine_rows, send_rows = call(
        chip_rows_kernel,
        ids,
        (here, there),
        [((2 * tokens, levels * rows), BF16)] * 2,
    )
    s_near = s_scan.before(after=(*attn_got, mine_rows))
    rows_own = jnp.stack([mine_rows, swap(send_rows, 1, seq_devices)])
    rows_all = [rows_own] + [shift(rows_own, r, fsdp_devices) for r in others]
    s_own, s_got = s_scan.core(after=attn_back)

    def grad_states(ids, *refs):
        grad_state_kernel(fsdp_devices, ids, *refs)

    grad_attn, g_mine, g_send = call(
        grad_states,
        ids,
        (queries, attn_own, *attn_back),
        [(queries.shape, BF16), (half, F32), (half, BF16)],
        after=(s_own,),
    )

    g_scan = Scan(g_mine, g_send, ids, seq_devices, True, True)
    g_scan.chip()

    def attended_heads(ids, *refs):
        attended_kernel(fsdp_devices, factor, ids, *refs)

    attended = call(
        attended_heads,
        ids,
        (queries, key_vectors, value_vectors, s_own, s_got),
        [((tokens, piece), BF16)] * fsdp_devices,
        after=(g_mine,),
    )
    near = [attended[0]] + [shift(attended[r], r, fsdp_devices) for r in others]
    across = [swap(attended[0], 2, seq_devices)]
    across += [shift_across(attended[r], r, fsdp_devices, seq_devices) for r in others]

    g_plane = g_scan.plane(after=(attended[0], *rows_all[1:]))

    def blocks(ids, *refs):
        block_kernel(factor, ids, *refs)

    flat = (tokens, width)
    query_grad, key_part, value_part, blocks_ran = call(
        blocks,
        ids,
        (queries, key_vectors, value_vectors, grad_attn, s_own, s_got),
        [(queries.shape, BF16), (flat, F32), (flat, F32), RAN],
        after=(g_plane,),
    )
    g_double = g_scan.double()
    g_near = g_scan.before()

    (near,) = call(
        stack_kernel,
        ids,
        [part for pair in zip(near, across) for part in pair],
        [((2 * fsdp_devices * tokens, piece), BF16)],
        after=(blocks_ran, g_double, *rows_all[1:]),
    )
    grads_rows = jnp.concatenate([part[core] for core in range(2) for part in rows_all])
    attended_all = jnp.concatenate([near, swap(near, 1, seq_devices)])
    partial = dot(grads_rows, attended_all, 0, 0)
    chunks = [partial[k * rows : (k + 1) * rows].astype(BF16) for k in range(levels)]
    got = [swap(chunks[k], PLANE * k, seq_devices) for k in range(1, levels)]
    g_own, g_got = g_scan.core(after=got[:1])

    def later(ids, *refs):
        later_kernel(factor, ids, *refs)

    key_grad, value_grad = call(
        later,
        ids,
        (key_vectors, value_vectors, key_part, value_part, g_own, g_got),
        [(queries.shape, BF16)] * 2,
    )
    weight_grad = partial[:rows]
    for chunk in got:
        weight_grad = weight_grad + chunk.astype(F32)
    return (query_grad, key_grad, value_grad, weight_grad * grad_factor)


def solution(mesh):
    in_specs = (
        P("fsdp", "seq", None),
        P("fsdp", "seq", None),
        P("fsdp", "seq", None),
        P("fsdp", "seq", None),
        P(None, "fsdp"),
    )
    out_specs = (
        P("fsdp", "seq", None),
        P("fsdp", "seq", None),
        P("fsdp", "seq", None),
        P("seq", "fsdp"),
    )
    return jax.shard_map(body, mesh=mesh, in_specs=in_specs, out_specs=out_specs, check_vma=False)
```

time: 111 us -> 95 us (0.86)
  waiting for transfers between devices: 52.4 us -> 31.6 us
  Pallas kernels: 12.3 us -> 18.3 us
  starting transfers between devices: 29.9 us -> 34.8 us
  local copies, waits for them, and re-layouts: 5.67 us -> 2.2 us
  other arithmetic: 4.52 us -> 1.07 us
    ppermute x9 -> x6, waiting for transfers between devices: 28 us -> 6.84 us  [the longest x5 6.84 us: along(): return lax.ppermute(value, 'seq', route)]
    pallas_call x5 -> x17, Pallas kernels: 12.3 us -> 18.3 us  [call(): pl.pallas_call(run, out_shape=[jax.ShapeDtypeStruct(shape, dtype) for sha...]
    ppermute x14 -> x15, waiting for transfers between devices: 18.9 us -> 24.7 us  [swap(): return lax.ppermute(value, 'seq', [(i, i ^ distance) for i in range(count)])]
    ppermute x3 -> x4, waiting for transfers between devices: 5.52 us -> 0.01 us  [shift(): lax.ppermute(value, 'fsdp', [(i, (i + r) % count) for i in range(count)])]
    ppermute x14 -> x15, starting transfers between devices: 9.2 us -> 12.9 us  [swap(): return lax.ppermute(value, 'seq', [(i, i ^ distance) for i in range(count)])]
    unnamed x36 -> x14, local copies, waits for them, and re-layouts: 4.75 us -> 2.11 us
    convert_element_type x4 -> x0, other arithmetic: 2.17 us -> none  [the longest x2 2.11 us: scan(): got = swap((chip_before + (1.0 - first_c) * mine).astype(BF16), 1, count)]
    ppermute x9 -> x6, starting transfers between devices: 15.9 us -> 16.7 us  [the longest x5 15.1 us: along(): return lax.ppermute(value, 'seq', route)]
  transfers between devices with their start and end apart: 26 -> 25, of which waited for: 14 -> 11; matrix products, arithmetic and copies ran while one was open for 9% -> 7% of each run, Pallas kernels for 10% -> 15%
where the time goes in v2:
time: 95 us; the launch traced here: 94.1 us
  starting transfers between devices  34.8 us (37%)
  waiting for transfers between devices  31.6 us (33%)
  Pallas kernels  18.3 us (19%)
  matrix products  5.24 us (6%)
  local copies, waits for them, and re-layouts  2.2 us (2%)
  other arithmetic  1.07 us (1%)
  between operations  0.97 us (1%)
    ppermute x15, waiting for transfers between devices, swap(): return lax.ppermute(value, 'seq', [(i, i ^ distance) for i in range(count)])  24.7 us
    pallas_call x17, Pallas kernels, call(): pl.pallas_call(run, out_shape=[jax.ShapeDtypeStruct(shape, dtype) for sha...  18.3 us
    ppermute x5, starting transfers between devices, along(): return lax.ppermute(value, 'seq', route)  15.1 us
    ppermute x15, starting transfers between devices, swap(): return lax.ppermute(value, 'seq', [(i, i ^ distance) for i in range(count)])  12.9 us
    ppermute x5, waiting for transfers between devices, along(): return lax.ppermute(value, 'seq', route)  6.84 us
    dot_general x3, matrix products, dot(): return lax.dot_general(a, b, dims, preferred_element_type=F32)  5.24 us
    ppermute x4, starting transfers between devices, shift(): lax.ppermute(value, 'fsdp', [(i, (i + r) % count) for i in range(count)])  5.2 us
    unnamed x14, local copies, waits for them, and re-layouts  2.11 us
  transfers between devices with their start and end apart: 25, of which 11 were waited for; matrix products, arithmetic and copies ran while one was open for 7% of the time, Pallas kernels for 15%

profile of v2, /device:TPU:8, one launch (start us, length us, event | category | flops | bytes accessed | tf_op | source)
XLA Modules:
  0.0 94.1 jit_solution(15163959641885867317)
XLA Ops:
  3.9 1.6 %collective-permute-start = (bf16[128,2048]{1,0:T(8,128)(2,1)}, bf16[128,2048]{1,0:T(8,128)(2,1)S(1)}, u32[]{:S(2)}, u32[]{:S(2)}) collective-permute-start(bf16[128,2048]{1,0:T(8,128)(2,1)} %bitcast.16), channel_id=1, source_target_pairs={{0,1},{1,0},{2,3},{3,2},{4,5},{5,4},{6,7},{7,6},{8,9},{9,8},{10,11... | collective-permute-start | bytes 1572872 | tf_op jit(solution)/shard_map/ppermute | solution.py:186
  6.1 1.6 %collective-permute-start.3 = (bf16[4,128,128]{2,1,0:T(8,128)(2,1)S(1)}, bf16[4,128,128]{2,1,0:T(8,128)(2,1)S(1)}, u32[]{:S(2)}, u32[]{:S(2)}) collective-permute-start(bf16[4,128,128]{2,1,0:T(8,128)(2,1)S(1)} %get-tuple-element.36), channel_id=1, source_target_pairs={{0,4},{2,6},{4,0},{6,2},{8,12},{10,14},{12,8},{14,10},{16,20},{18,... | collective-permute-start | bytes 393224 | tf_op jit(solution)/shard_map/ppermute | solution.py:182
  9.0 3.2 %convolution_convert_fusion.1.refs_3_.refs_2_ = bf16[128,1024]{1,0:T(8,128)(2,1)S(1)} fusion(bf16[2048,1024]{1,0:T(8,128)(2,1)} %param.9, bf16[1,128,2048]{2,1,0:T(8,128)(2,1)S(1)} %copy-done.5), kind=kOutput, calls=%fused_computation.5 | convolution fusion | flops 537001984 | bytes 4980736 | tf_op jit(solution)/shard_map/dot_general | solution.py:23
  13.8 5.1 %collective-permute-start.5 = (bf16[4,128,128]{2,1,0:T(8,128)(2,1)S(1)}, bf16[4,128,128]{2,1,0:T(8,128)(2,1)S(1)}, u32[]{:S(2)}, u32[]{:S(2)}) collective-permute-start(bf16[4,128,128]{2,1,0:T(8,128)(2,1)S(1)} %shard_map.86), channel_id=1, source_target_pairs={{0,16},{2,18},{4,20},{6,22},{8,24},{10,26},{12,28},{14,30},{1,17},... | collective-permute-start | bytes 393224 | tf_op jit(solution)/shard_map/ppermute | solution.py:241
  18.9 1.9 %collective-permute-start.4 = (bf16[4,128,128]{2,1,0:T(8,128)(2,1)S(1)}, bf16[4,128,128]{2,1,0:T(8,128)(2,1)S(1)}, u32[]{:S(2)}, u32[]{:S(2)}) collective-permute-start(bf16[4,128,128]{2,1,0:T(8,128)(2,1)S(1)} %shard_map.86), channel_id=1, source_target_pairs={{0,8},{2,10},{4,12},{6,14},{8,16},{10,18},{12,20},{14,22},{16,24},... | collective-permute-start | bytes 393224 | tf_op jit(solution)/shard_map/ppermute | solution.py:241
  22.3 1.5 %collective-permute-start.1 = (bf16[128,1024]{1,0:T(8,128)(2,1)S(1)}, bf16[128,1024]{1,0:T(8,128)(2,1)S(1)}, u32[]{:S(2)}, u32[]{:S(2)}) collective-permute-start(bf16[128,1024]{1,0:T(8,128)(2,1)S(1)} %convolution_convert_fusion.refs_6_), channel_id=1, source_target_pairs={{0,1},{1,0},{2,3},{3,2},{4,5},{5,4},{6,7},{7,6},{8,9},{9,8},{10,11... | collective-permute-start | bytes 786440 | tf_op jit(solution)/shard_map/ppermute | solution.py:186
  23.8 2.5 %collective-permute-done.5.refs_4_ = bf16[4,128,128]{2,1,0:T(8,128)(2,1)S(1)} collective-permute-done((bf16[4,128,128]{2,1,0:T(8,128)(2,1)S(1)}, bf16[4,128,128]{2,1,0:T(8,128)(2,1)S(1)}, u32[]{:S(2)}, u32[]{:S(2)}) %collective-permute-start.5) | collective-permute-done | bytes 131104 | tf_op jit(solution)/shard_map/ppermute | solution.py:241
  26.3 2.7 %collective-permute-done.4.refs_3_ = bf16[4,128,128]{2,1,0:T(8,128)(2,1)S(1)} collective-permute-done((bf16[4,128,128]{2,1,0:T(8,128)(2,1)S(1)}, bf16[4,128,128]{2,1,0:T(8,128)(2,1)S(1)}, u32[]{:S(2)}, u32[]{:S(2)}) %collective-permute-start.4) | collective-permute-done | bytes 131104 | tf_op jit(solution)/shard_map/ppermute | solution.py:241
  29.6 1.4 %collective-permute-start.8 = (bf16[4,128,128]{2,1,0:T(8,128)(2,1)S(1)}, bf16[4,128,128]{2,1,0:T(8,128)(2,1)S(1)}, u32[]{:S(2)}, u32[]{:S(2)}) collective-permute-start(bf16[4,128,128]{2,1,0:T(8,128)(2,1)S(1)} %get-tuple-element.41), channel_id=1, source_target_pairs={{0,4},{2,6},{4,0},{6,2},{8,12},{10,14},{12,8},{14,10},{16,20},{18,... | collective-permute-start | bytes 393224 | tf_op jit(solution)/shard_map/ppermute | solution.py:182
  31.1 1.5 %collective-permute-start.13 = (bf16[2,256,512]{2,1,0:T(8,128)(2,1)S(1)}, bf16[2,256,512]{2,1,0:T(8,128)(2,1)S(1)}, u32[]{:S(2)}, u32[]{:S(2)}) collective-permute-start(bf16[2,256,512]{2,1,0:T(8,128)(2,1)S(1)} %pad_maximum_fusion), channel_id=1, source_target_pairs={{0,1},{1,0},{2,3},{3,2},{4,5},{5,4},{6,7},{7,6},{8,9},{9,8},{10,11... | collective-permute-start | bytes 1572872 | tf_op jit(solution)/shard_map/ppermute | solution.py:186
  32.6 2.5 %collective-permute-done.8.refs_2_ = bf16[4,128,128]{2,1,0:T(8,128)(2,1)S(1)} collective-permute-done((bf16[4,128,128]{2,1,0:T(8,128)(2,1)S(1)}, bf16[4,128,128]{2,1,0:T(8,128)(2,1)S(1)}, u32[]{:S(2)}, u32[]{:S(2)}) %collective-permute-start.8) | collective-permute-done | bytes 131104 | tf_op jit(solution)/shard_map/ppermute | solution.py:182
  39.0 1.4 %collective-permute-start.11 = (bf16[4,128,128]{2,1,0:T(8,128)(2,1)S(1)}, bf16[4,128,128]{2,1,0:T(8,128)(2,1)S(1)}, u32[]{:S(2)}, u32[]{:S(2)}) collective-permute-start(bf16[4,128,128]{2,1,0:T(8,128)(2,1)S(1)} %get-tuple-element.48), channel_id=1, source_target_pairs={{0,4},{2,6},{4,0},{6,2},{8,12},{10,14},{12,8},{14,10},{16,20},{18,... | collective-permute-start | bytes 393224 | tf_op jit(solution)/shard_map/ppermute | solution.py:182
  40.5 1.5 %shard_map.93 = (bf16[128,1024]{1,0:T(8,128)(2,1)S(1)}, bf16[128,1024]{1,0:T(8,128)(2,1)S(1)}) custom-call(s32[4]{0:T(128)S(1)} %pad_add_fusion.refs_0_, bf16[1,128,2048]{2,1,0:T(8,128)(2,1)S(1)} %copy-done.4, bf16[1,128,2048]{2,1,0:T(8,128)(2,1)S(1)} %copy-done.1, bf16[1,128,2048]{2,1,0:T(8,128)(2,1)S(1)} %copy-done.3, ...), custom_call_target="tpu_custom_call" | custom-call | tf_op jit(solution)/shard_map/pallas_call | solution.py:33
  41.9 1.6 %collective-permute-start.19 = (bf16[128,1024]{1,0:T(8,128)(2,1)S(1)}, bf16[128,1024]{1,0:T(8,128)(2,1)S(1)}, u32[]{:S(2)}, u32[]{:S(2)}) collective-permute-start(bf16[128,1024]{1,0:T(8,128)(2,1)S(1)} %get-tuple-element.56), channel_id=1, source_target_pairs={{0,5},{1,4},{2,7},{3,6},{4,1},{5,0},{6,3},{7,2},{8,13},{9,12},{10,... | collective-permute-start | bytes 786440 | tf_op jit(solution)/shard_map/ppermute | solution.py:193
  44.1 1.4 %collective-permute-start.17 = (bf16[128,1024]{1,0:T(8,128)(2,1)S(1)}, bf16[128,1024]{1,0:T(8,128)(2,1)S(1)}, u32[]{:S(2)}, u32[]{:S(2)}) collective-permute-start(bf16[128,1024]{1,0:T(8,128)(2,1)S(1)} %get-tuple-element.49.refs_3_.refs_1_), channel_id=1, source_target_pairs={{0,4},{2,6},{4,0},{6,2},{8,12},{10,14},{12,8},{14,10},{16,20},{18,... | collective-permute-start | bytes 786440 | tf_op jit(solution)/shard_map/ppermute | solution.py:182
  46.1 6.1 %collective-permute-start.14 = (bf16[4,128,128]{2,1,0:T(8,128)(2,1)S(1)}, bf16[4,128,128]{2,1,0:T(8,128)(2,1)S(1)}, u32[]{:S(2)}, u32[]{:S(2)}) collective-permute-start(bf16[4,128,128]{2,1,0:T(8,128)(2,1)S(1)} %shard_map.94.refs_7_.refs_1_), channel_id=1, source_target_pairs={{8,0},{10,2},{12,4},{14,6},{16,8},{18,10},{20,12},{22,14},{24,16},... | collective-permute-start | bytes 393224 | tf_op jit(solution)/shard_map/ppermute | solution.py:241
  52.2 5.2 %shard_map.95 = (bf16[1,128,2048]{2,1,0:T(8,128)(2,1)}, f32[128,2048]{1,0:T(8,128)S(1)}, f32[128,2048]{1,0:T(8,128)S(1)}, f32[8,128]{1,0:T(8,128)S(1)}) custom-call(s32[4]{0:T(128)S(1)} %pad_add_fusion.refs_0_, bf16[1,128,2048]{2,1,0:T(8,128)(2,1)S(1)} %copy-done.4, bf16[1,128,2048]{2,1,0:T(8,128)(2,1)S(1)} %copy-done.1, ...), custom_call_target="tpu_custom_call" | custom-call | tf_op jit(solution)/shard_map/pallas_call | solution.py:33
  62.8 2.6 %collective-permute-start.23 = (bf16[128,1024]{1,0:T(8,128)(2,1)S(1)}, bf16[128,1024]{1,0:T(8,128)(2,1)S(1)}, u32[]{:S(2)}, u32[]{:S(2)}) collective-permute-start(bf16[128,1024]{1,0:T(8,128)(2,1)S(1)} %get-tuple-element.62), channel_id=1, source_target_pairs={{0,16},{2,18},{4,20},{6,22},{8,24},{10,26},{12,28},{14,30},{16,0},... | collective-permute-start | bytes 786440 | tf_op jit(solution)/shard_map/ppermute | solution.py:182
  66.3 1.6 %collective-permute-done.15.refs_4_ = bf16[4,128,128]{2,1,0:T(8,128)(2,1)S(1)} collective-permute-done((bf16[4,128,128]{2,1,0:T(8,128)(2,1)S(1)}, bf16[4,128,128]{2,1,0:T(8,128)(2,1)S(1)}, u32[]{:S(2)}, u32[]{:S(2)}) %collective-permute-start.15) | collective-permute-done | bytes 131104 | tf_op jit(solution)/shard_map/ppermute | solution.py:241
  68.5 2.2 %collective-permute-start.16 = (bf16[4,128,128]{2,1,0:T(8,128)(2,1)S(1)}, bf16[4,128,128]{2,1,0:T(8,128)(2,1)S(1)}, u32[]{:S(2)}, u32[]{:S(2)}) collective-permute-start(bf16[4,128,128]{2,1,0:T(8,128)(2,1)S(1)} %get-tuple-element.55), channel_id=1, source_target_pairs={{0,4},{2,6},{4,0},{6,2},{8,12},{10,14},{12,8},{14,10},{16,20},{18,... | collective-permute-start | bytes 393224 | tf_op jit(solution)/shard_map/ppermute | solution.py:182
  70.7 3.0 %collective-permute-done.16.refs_2_ = bf16[4,128,128]{2,1,0:T(8,128)(2,1)S(1)} collective-permute-done((bf16[4,128,128]{2,1,0:T(8,128)(2,1)S(1)}, bf16[4,128,128]{2,1,0:T(8,128)(2,1)S(1)}, u32[]{:S(2)}, u32[]{:S(2)}) %collective-permute-start.16) | collective-permute-done | bytes 131104 | tf_op jit(solution)/shard_map/ppermute | solution.py:182
  75.7 7.7 %collective-permute-done.23 = bf16[128,1024]{1,0:T(8,128)(2,1)S(1)} collective-permute-done((bf16[128,1024]{1,0:T(8,128)(2,1)S(1)}, bf16[128,1024]{1,0:T(8,128)(2,1)S(1)}, u32[]{:S(2)}, u32[]{:S(2)}) %collective-permute-start.23) | collective-permute-done | bytes 262176 | tf_op jit(solution)/shard_map/ppermute | solution.py:182
  83.4 7.6 %collective-permute-done.24 = bf16[128,1024]{1,0:T(8,128)(2,1)S(1)} collective-permute-done((bf16[128,1024]{1,0:T(8,128)(2,1)S(1)}, bf16[128,1024]{1,0:T(8,128)(2,1)S(1)}, u32[]{:S(2)}, u32[]{:S(2)}) %collective-permute-start.24) | collective-permute-done | bytes 262176 | tf_op jit(solution)/shard_map/ppermute | solution.py:182
  92.0 2.2 %shard_map.100 = (bf16[1,128,2048]{2,1,0:T(8,128)(2,1)}, bf16[1,128,2048]{2,1,0:T(8,128)(2,1)}) custom-call(s32[4]{0:T(128)S(1)} %pad_add_fusion.refs_0_, bf16[1,128,2048]{2,1,0:T(8,128)(2,1)S(1)} %copy-done.1, bf16[1,128,2048]{2,1,0:T(8,128)(2,1)S(1)} %copy-done.3, f32[128,2048]{1,0:T(8,128)S(1)} %get-tuple-element.52.refs_3_, ...), custom_call_target="tpu_custom_call" | custom-call | tf_op jit(solution)/shard_map/pallas_call | solution.py:33
  (65 shorter events, 23.6 us)
Async XLA Ops:
  3.8 1.7 %collective-permute-start.2 = (bf16[2,4,128,128]{3,2,1,0:T(8,128)(2,1)S(1)}, bf16[2,4,128,128]{3,2,1,0:T(8,128)(2,1)S(1)}, u32[]{:S(2)}, u32[]{:S(2)}) collective-permute-start(bf16[2,4,128,128]{3,2,1,0:T(8,128)(2,1)S(1)} %get-tuple-element.34), channel_id=1, source_target_pairs={{0,2},{2,0},{4,6},{6,4},{8,10},{10,8},{12,14},{14,12},{16,18},{18,... | collective-permute-start | bytes 786440 | tf_op jit(solution)/shard_map/ppermute | solution.py:182
  3.9 17.6 %collective-permute-start = (bf16[128,2048]{1,0:T(8,128)(2,1)}, bf16[128,2048]{1,0:T(8,128)(2,1)S(1)}, u32[]{:S(2)}, u32[]{:S(2)}) collective-permute-start(bf16[128,2048]{1,0:T(8,128)(2,1)} %bitcast.16), channel_id=1, source_target_pairs={{0,1},{1,0},{2,3},{3,2},{4,5},{5,4},{6,7},{7,6},{8,9},{9,8},{10,11... | collective-permute-start | bytes 1572872 | tf_op jit(solution)/shard_map/ppermute | solution.py:186
  6.1 6.4 %collective-permute-start.3 = (bf16[4,128,128]{2,1,0:T(8,128)(2,1)S(1)}, bf16[4,128,128]{2,1,0:T(8,128)(2,1)S(1)}, u32[]{:S(2)}, u32[]{:S(2)}) collective-permute-start(bf16[4,128,128]{2,1,0:T(8,128)(2,1)S(1)} %get-tuple-element.36), channel_id=1, source_target_pairs={{0,4},{2,6},{4,0},{6,2},{8,12},{10,14},{12,8},{14,10},{16,20},{18,... | collective-permute-start | bytes 393224 | tf_op jit(solution)/shard_map/ppermute | solution.py:182
  8.4 12.5 %collective-permute-start.7 = (bf16[2,128,512]{2,1,0:T(8,128)(2,1)S(1)}, bf16[2,128,512]{2,1,0:T(8,128)(2,1)S(1)}, u32[]{:S(2)}, u32[]{:S(2)}) collective-permute-start(bf16[2,128,512]{2,1,0:T(8,128)(2,1)S(1)} %get-tuple-element.38), channel_id=1, source_target_pairs={{0,4},{2,6},{4,0},{6,2},{8,12},{10,14},{12,8},{14,10},{16,20},{18,... | collective-permute-start | bytes 786440 | tf_op jit(solution)/shard_map/ppermute | solution.py:182
  13.1 10.7 %collective-permute-start.6 = (bf16[4,128,128]{2,1,0:T(8,128)(2,1)S(1)}, bf16[4,128,128]{2,1,0:T(8,128)(2,1)S(1)}, u32[]{:S(2)}, u32[]{:S(2)}) collective-permute-start(bf16[4,128,128]{2,1,0:T(8,128)(2,1)S(1)} %shard_map.86), channel_id=1, source_target_pairs={{0,24},{2,26},{4,28},{6,30},{1,25},{3,27},{5,29},{7,31}} | collective-permute-start | bytes 393224 | tf_op jit(solution)/shard_map/ppermute | solution.py:241
  13.8 12.5 %collective-permute-start.5 = (bf16[4,128,128]{2,1,0:T(8,128)(2,1)S(1)}, bf16[4,128,128]{2,1,0:T(8,128)(2,1)S(1)}, u32[]{:S(2)}, u32[]{:S(2)}) collective-permute-start(bf16[4,128,128]{2,1,0:T(8,128)(2,1)S(1)} %shard_map.86), channel_id=1, source_target_pairs={{0,16},{2,18},{4,20},{6,22},{8,24},{10,26},{12,28},{14,30},{1,17},... | collective-permute-start | bytes 393224 | tf_op jit(solution)/shard_map/ppermute | solution.py:241
  18.9 10.1 %collective-permute-start.4 = (bf16[4,128,128]{2,1,0:T(8,128)(2,1)S(1)}, bf16[4,128,128]{2,1,0:T(8,128)(2,1)S(1)}, u32[]{:S(2)}, u32[]{:S(2)}) collective-permute-start(bf16[4,128,128]{2,1,0:T(8,128)(2,1)S(1)} %shard_map.86), channel_id=1, source_target_pairs={{0,8},{2,10},{4,12},{6,14},{8,16},{10,18},{12,20},{14,22},{16,24},... | collective-permute-start | bytes 393224 | tf_op jit(solution)/shard_map/ppermute | solution.py:241
  21.4 9.6 %collective-permute-start.12 = (bf16[256,512]{1,0:T(8,128)(2,1)S(1)}, bf16[256,512]{1,0:T(8,128)(2,1)S(1)}, u32[]{:S(2)}, u32[]{:S(2)}) collective-permute-start(bf16[256,512]{1,0:T(8,128)(2,1)S(1)} %get-tuple-element.50), channel_id=1, source_target_pairs={{0,2},{2,0},{4,6},{6,4},{8,10},{10,8},{12,14},{14,12},{16,18},{18,... | collective-permute-start | bytes 786440 | tf_op jit(solution)/shard_map/ppermute | solution.py:182
  22.3 12.8 %collective-permute-start.1 = (bf16[128,1024]{1,0:T(8,128)(2,1)S(1)}, bf16[128,1024]{1,0:T(8,128)(2,1)S(1)}, u32[]{:S(2)}, u32[]{:S(2)}) collective-permute-start(bf16[128,1024]{1,0:T(8,128)(2,1)S(1)} %convolution_convert_fusion.refs_6_), channel_id=1, source_target_pairs={{0,1},{1,0},{2,3},{3,2},{4,5},{5,4},{6,7},{7,6},{8,9},{9,8},{10,11... | collective-permute-start | bytes 786440 | tf_op jit(solution)/shard_map/ppermute | solution.py:186
  29.6 5.5 %collective-permute-start.8 = (bf16[4,128,128]{2,1,0:T(8,128)(2,1)S(1)}, bf16[4,128,128]{2,1,0:T(8,128)(2,1)S(1)}, u32[]{:S(2)}, u32[]{:S(2)}) collective-permute-start(bf16[4,128,128]{2,1,0:T(8,128)(2,1)S(1)} %get-tuple-element.41), channel_id=1, source_target_pairs={{0,4},{2,6},{4,0},{6,2},{8,12},{10,14},{12,8},{14,10},{16,20},{18,... | collective-permute-start | bytes 393224 | tf_op jit(solution)/shard_map/ppermute | solution.py:182
  31.1 14.4 %collective-permute-start.13 = (bf16[2,256,512]{2,1,0:T(8,128)(2,1)S(1)}, bf16[2,256,512]{2,1,0:T(8,128)(2,1)S(1)}, u32[]{:S(2)}, u32[]{:S(2)}) collective-permute-start(bf16[2,256,512]{2,1,0:T(8,128)(2,1)S(1)} %pad_maximum_fusion), channel_id=1, source_target_pairs={{0,1},{1,0},{2,3},{3,2},{4,5},{5,4},{6,7},{7,6},{8,9},{9,8},{10,11... | collective-permute-start | bytes 1572872 | tf_op jit(solution)/shard_map/ppermute | solution.py:186
  36.9 3.5 %collective-permute-start.9 = (bf16[2,4,128,128]{3,2,1,0:T(8,128)(2,1)S(1)}, bf16[2,4,128,128]{3,2,1,0:T(8,128)(2,1)S(1)}, u32[]{:S(2)}, u32[]{:S(2)}) collective-permute-start(bf16[2,4,128,128]{3,2,1,0:T(8,128)(2,1)S(1)} %get-tuple-element.44), channel_id=1, source_target_pairs={{0,2},{2,0},{4,6},{6,4},{8,10},{10,8},{12,14},{14,12},{16,18},{18,... | collective-permute-start | bytes 786440 | tf_op jit(solution)/shard_map/ppermute | solution.py:182
  39.0 6.5 %collective-permute-start.11 = (bf16[4,128,128]{2,1,0:T(8,128)(2,1)S(1)}, bf16[4,128,128]{2,1,0:T(8,128)(2,1)S(1)}, u32[]{:S(2)}, u32[]{:S(2)}) collective-permute-start(bf16[4,128,128]{2,1,0:T(8,128)(2,1)S(1)} %get-tuple-element.48), channel_id=1, source_target_pairs={{0,4},{2,6},{4,0},{6,2},{8,12},{10,14},{12,8},{14,10},{16,20},{18,... | collective-permute-start | bytes 393224 | tf_op jit(solution)/shard_map/ppermute | solution.py:182
  41.9 16.1 %collective-permute-start.19 = (bf16[128,1024]{1,0:T(8,128)(2,1)S(1)}, bf16[128,1024]{1,0:T(8,128)(2,1)S(1)}, u32[]{:S(2)}, u32[]{:S(2)}) collective-permute-start(bf16[128,1024]{1,0:T(8,128)(2,1)S(1)} %get-tuple-element.56), channel_id=1, source_target_pairs={{0,5},{1,4},{2,7},{3,6},{4,1},{5,0},{6,3},{7,2},{8,13},{9,12},{10,... | collective-permute-start | bytes 786440 | tf_op jit(solution)/shard_map/ppermute | solution.py:193
  43.5 14.5 %collective-permute-start.18 = (bf16[128,1024]{1,0:T(8,128)(2,1)S(1)}, bf16[128,1024]{1,0:T(8,128)(2,1)S(1)}, u32[]{:S(2)}, u32[]{:S(2)}) collective-permute-start(bf16[128,1024]{1,0:T(8,128)(2,1)S(1)} %get-tuple-element.56), channel_id=1, source_target_pairs={{0,1},{1,0},{2,3},{3,2},{4,5},{5,4},{6,7},{7,6},{8,9},{9,8},{10,11... | collective-permute-start | bytes 786440 | tf_op jit(solution)/shard_map/ppermute | solution.py:186
  44.1 13.9 %collective-permute-start.17 = (bf16[128,1024]{1,0:T(8,128)(2,1)S(1)}, bf16[128,1024]{1,0:T(8,128)(2,1)S(1)}, u32[]{:S(2)}, u32[]{:S(2)}) collective-permute-start(bf16[128,1024]{1,0:T(8,128)(2,1)S(1)} %get-tuple-element.49.refs_3_.refs_1_), channel_id=1, source_target_pairs={{0,4},{2,6},{4,0},{6,2},{8,12},{10,14},{12,8},{14,10},{16,20},{18,... | collective-permute-start | bytes 786440 | tf_op jit(solution)/shard_map/ppermute | solution.py:182
  46.1 11.3 %collective-permute-start.14 = (bf16[4,128,128]{2,1,0:T(8,128)(2,1)S(1)}, bf16[4,128,128]{2,1,0:T(8,128)(2,1)S(1)}, u32[]{:S(2)}, u32[]{:S(2)}) collective-permute-start(bf16[4,128,128]{2,1,0:T(8,128)(2,1)S(1)} %shard_map.94.refs_7_.refs_1_), channel_id=1, source_target_pairs={{8,0},{10,2},{12,4},{14,6},{16,8},{18,10},{20,12},{22,14},{24,16},... | collective-permute-start | bytes 393224 | tf_op jit(solution)/shard_map/ppermute | solution.py:241
  58.7 2.7 %collective-permute-start.20 = (bf16[512,1024]{1,0:T(8,128)(2,1)S(1)}, bf16[512,1024]{1,0:T(8,128)(2,1)S(1)}, u32[]{:S(2)}, u32[]{:S(2)}) collective-permute-start(bf16[512,1024]{1,0:T(8,128)(2,1)S(1)} %shard_map.98), channel_id=1, source_target_pairs={{0,2},{2,0},{4,6},{6,4},{8,10},{10,8},{12,14},{14,12},{16,18},{18,... | collective-permute-start | bytes 3145736 | tf_op jit(solution)/shard_map/ppermute | solution.py:182
  58.8 9.1 %collective-permute-start.15 = (bf16[4,128,128]{2,1,0:T(8,128)(2,1)S(1)}, bf16[4,128,128]{2,1,0:T(8,128)(2,1)S(1)}, u32[]{:S(2)}, u32[]{:S(2)}) collective-permute-start(bf16[4,128,128]{2,1,0:T(8,128)(2,1)S(1)} %shard_map.96.refs_6_), channel_id=1, source_target_pairs={{16,0},{18,2},{20,4},{22,6},{24,8},{26,10},{28,12},{30,14},{17,1},... | collective-permute-start | bytes 393224 | tf_op jit(solution)/shard_map/ppermute | solution.py:241
  62.7 12.3 %collective-permute-start.21 = (bf16[128,1024]{1,0:T(8,128)(2,1)S(1)}, bf16[128,1024]{1,0:T(8,128)(2,1)S(1)}, u32[]{:S(2)}, u32[]{:S(2)}) collective-permute-start(bf16[128,1024]{1,0:T(8,128)(2,1)S(1)} %get-tuple-element.64), channel_id=1, source_target_pairs={{0,8},{2,10},{4,12},{6,14},{8,0},{10,2},{12,4},{14,6},{16,24},{18,... | collective-permute-start | bytes 786440 | tf_op jit(solution)/shard_map/ppermute | solution.py:182
  62.8 20.6 %collective-permute-start.23 = (bf16[128,1024]{1,0:T(8,128)(2,1)S(1)}, bf16[128,1024]{1,0:T(8,128)(2,1)S(1)}, u32[]{:S(2)}, u32[]{:S(2)}) collective-permute-start(bf16[128,1024]{1,0:T(8,128)(2,1)S(1)} %get-tuple-element.62), channel_id=1, source_target_pairs={{0,16},{2,18},{4,20},{6,22},{8,24},{10,26},{12,28},{14,30},{16,0},... | collective-permute-start | bytes 786440 | tf_op jit(solution)/shard_map/ppermute | solution.py:182
  65.4 25.6 %collective-permute-start.24 = (bf16[128,1024]{1,0:T(8,128)(2,1)S(1)}, bf16[128,1024]{1,0:T(8,128)(2,1)S(1)}, u32[]{:S(2)}, u32[]{:S(2)}) collective-permute-start(bf16[128,1024]{1,0:T(8,128)(2,1)S(1)} %get-tuple-element.63), channel_id=1, source_target_pairs={{0,24},{2,26},{4,28},{6,30},{8,16},{10,18},{12,20},{14,22},{16,8},... | collective-permute-start | bytes 786440 | tf_op jit(solution)/shard_map/ppermute | solution.py:182
  68.5 5.1 %collective-permute-start.16 = (bf16[4,128,128]{2,1,0:T(8,128)(2,1)S(1)}, bf16[4,128,128]{2,1,0:T(8,128)(2,1)S(1)}, u32[]{:S(2)}, u32[]{:S(2)}) collective-permute-start(bf16[4,128,128]{2,1,0:T(8,128)(2,1)S(1)} %get-tuple-element.55), channel_id=1, source_target_pairs={{0,4},{2,6},{4,0},{6,2},{8,12},{10,14},{12,8},{14,10},{16,20},{18,... | collective-permute-start | bytes 393224 | tf_op jit(solution)/shard_map/ppermute | solution.py:182
  75.6 16.3 %collective-permute-start.22 = (bf16[2,4,128,128]{3,2,1,0:T(8,128)(2,1)S(1)}, bf16[2,4,128,128]{3,2,1,0:T(8,128)(2,1)S(1)}, u32[]{:S(2)}, u32[]{:S(2)}) collective-permute-start(bf16[2,4,128,128]{3,2,1,0:T(8,128)(2,1)S(1)} %get-tuple-element.59), channel_id=1, source_target_pairs={{0,2},{2,0},{4,6},{6,4},{8,10},{10,8},{12,14},{14,12},{16,18},{18,... | collective-permute-start | bytes 786440 | tf_op jit(solution)/shard_map/ppermute | solution.py:182
  (8 other events, 54.1 us)

commit v3 on v2

--- a/solution.py
+++ b/solution.py
@@ -172,6 +172,11 @@
         out[tokens:] = there_ref[core]
 
 
+def chip_rows(here, there, ids):
+    shape = (2 * here.shape[1], here.shape[2])
+    return call(chip_rows_kernel, ids, (here, there), [(shape, BF16)] * 2)
+
+
 def stack_kernel(ids, *refs):
     rows = refs[0].shape[0]
     for at, ref in enumerate(refs[:-1]):
@@ -243,7 +248,7 @@
     def plane(self, after=()):
         outs = [(self.quarter, BF16)]
         (self.summed,) = call(sum_kernel, self.ids, (self.total, self.across), outs, after)
-        steps = [1] if self.doubling else range(1, self.count // PLANE)
+        steps = [1] if self.doubling else range(self.count // PLANE - 1, 0, -1)
         self.got = [self.along(self.summed, step) for step in steps]
         return self.summed
 
@@ -301,16 +306,11 @@
     s_plane = s_scan.plane(after=(attn_own,))
     attn_got = [dot(grads, out_weight, 1, 0).astype(BF16) for grads in grads_got]
     attn_back = [shift(attn_got[r - 1], -r, fsdp_devices) for r in others]
-    mine_rows, send_rows = call(
-        chip_rows_kernel,
-        ids,
-        (here, there),
-        [((2 * tokens, levels * rows), BF16)] * 2,
-    )
-    s_near = s_scan.before(after=(*attn_got, mine_rows))
-    rows_own = jnp.stack([mine_rows, swap(send_rows, 1, seq_devices)])
-    rows_all = [rows_own] + [shift(rows_own, r, fsdp_devices) for r in others]
-    s_own, s_got = s_scan.core(after=attn_back)
+    rows_own = chip_rows(here, there, ids)
+    s_near = s_scan.before(after=(*attn_got, rows_own[0]))
+    here_got, there_got = features(jnp.concatenate(grads_got), ids, levels, after=(s_near,))
+    there_got = swap(there_got, 2, seq_devices)
+    s_own, s_got = s_scan.core()
 
     def grad_states(ids, *refs):
         grad_state_kernel(fsdp_devices, ids, *refs)
@@ -324,7 +324,7 @@
     )
 
     g_scan = Scan(g_mine, g_send, ids, seq_devices, True, True)
-    g_scan.chip()
+    g_scan.chip(after=(there_got,))
 
     def attended_heads(ids, *refs):
         attended_kernel(fsdp_devices, factor, ids, *refs)
@@ -340,7 +340,7 @@
     across = [swap(attended[0], 2, seq_devices)]
     across += [shift_across(attended[r], r, fsdp_devices, seq_devices) for r in others]
 
-    g_plane = g_scan.plane(after=(attended[0], *rows_all[1:]))
+    g_plane = g_scan.plane(after=attended[:1])
 
     def blocks(ids, *refs):
         block_kernel(factor, ids, *refs)
@@ -353,17 +353,20 @@
         [(queries.shape, BF16), (flat, F32), (flat, F32), RAN],
         after=(g_plane,),
     )
+    rows_got = chip_rows(here_got, there_got, ids)
     g_double = g_scan.double()
     g_near = g_scan.before()
 
     (near,) = call(
         stack_kernel,
         ids,
-        [part for pair in zip(near, across) for part in pair],
+        (near[0], across[0], *near[1:], *across[1:]),
         [((2 * fsdp_devices * tokens, piece), BF16)],
-        after=(blocks_ran, g_double, *rows_all[1:]),
-    )
-    grads_rows = jnp.concatenate([part[core] for core in range(2) for part in rows_all])
+        after=(blocks_ran, g_double, rows_got[0]),
+    )
+    grads_rows = jnp.concatenate(
+        [rows_own[0], rows_got[0], swap(rows_own[1], 1, seq_devices), swap(rows_got[1], 1, seq_devices)]
+    )
     attended_all = jnp.concatenate([near, swap(near, 1, seq_devices)])
     partial = dot(grads_rows, attended_all, 0, 0)
     chunks = [partial[k * rows : (k + 1) * rows].astype(BF16) for k in range(levels)]

time: 95 us -> 92 us (0.968)
  starting transfers between devices: 34.8 us -> 28.3 us
  waiting for transfers between devices: 31.6 us -> 34.8 us
  Pallas kernels: 18.3 us -> 19.5 us
    ppermute x5, starting transfers between devices: 15.1 us -> 9.66 us  [along(): return lax.ppermute(value, 'seq', route)]
    ppermute x15 -> x17, waiting for transfers between devices: 24.7 us -> 27 us  [swap(): return lax.ppermute(value, 'seq', [(i, i ^ distance) for i in range(count)])]
    ppermute x4 -> x3, waiting for transfers between devices: 0.01 us -> 2.08 us  [shift(): lax.ppermute(value, 'fsdp', [(i, (i + r) % count) for i in range(count)])]
    ppermute x4 -> x3, starting transfers between devices: 5.2 us -> 3.75 us  [shift(): lax.ppermute(value, 'fsdp', [(i, (i + r) % count) for i in range(count)])]
    pallas_call x17 -> x19, Pallas kernels: 18.3 us -> 19.5 us  [call(): pl.pallas_call(run, out_shape=[jax.ShapeDtypeStruct(shape, dtype) for sha...]
    ppermute x5, waiting for transfers between devices: 6.84 us -> 5.72 us  [along(): return lax.ppermute(value, 'seq', route)]
    ppermute x15 -> x17, starting transfers between devices: 12.9 us -> 12.9 us  [swap(): return lax.ppermute(value, 'seq', [(i, i ^ distance) for i in range(count)])]
  transfers between devices with their start and end apart: 25 -> 26, of which waited for: 11 -> 11; matrix products, arithmetic and copies ran while one was open for 7% -> 6% of each run, Pallas kernels for 15% -> 17%
where the time goes in v3:
time: 92 us; the launch traced here: 91.7 us
  waiting for transfers between devices  34.8 us (38%)
  starting transfers between devices  28.3 us (31%)
  Pallas kernels  19.5 us (21%)
  matrix products  4.95 us (5%)
  local copies, waits for them, and re-layouts  2.16 us (2%)
  other arithmetic  1.02 us (1%)
  between operations  0.96 us (1%)
    ppermute x17, waiting for transfers between devices, swap(): return lax.ppermute(value, 'seq', [(i, i ^ distance) for i in range(count)])  27 us
    pallas_call x19, Pallas kernels, call(): pl.pallas_call(run, out_shape=[jax.ShapeDtypeStruct(shape, dtype) for sha...  19.5 us
    ppermute x17, starting transfers between devices, swap(): return lax.ppermute(value, 'seq', [(i, i ^ distance) for i in range(count)])  12.9 us
    ppermute x5, starting transfers between devices, along(): return lax.ppermute(value, 'seq', route)  9.66 us
    ppermute x5, waiting for transfers between devices, along(): return lax.ppermute(value, 'seq', route)  5.72 us
    dot_general x3, matrix products, dot(): return lax.dot_general(a, b, dims, preferred_element_type=F32)  4.95 us
    ppermute x3, starting transfers between devices, shift(): lax.ppermute(value, 'fsdp', [(i, (i + r) % count) for i in range(count)])  3.75 us
    unnamed x14, local copies, waits for them, and re-layouts  2.11 us
  transfers between devices with their start and end apart: 26, of which 11 were waited for; matrix products, arithmetic and copies ran while one was open for 6% of the time, Pallas kernels for 17%

profile of v3, /device:TPU:8, one launch (start us, length us, event | category | flops | bytes accessed | tf_op | source)
XLA Modules:
  0.0 91.7 jit_solution(15198273880961072124)
XLA Ops:
  3.9 1.6 %collective-permute-start = (bf16[128,2048]{1,0:T(8,128)(2,1)}, bf16[128,2048]{1,0:T(8,128)(2,1)S(1)}, u32[]{:S(2)}, u32[]{:S(2)}) collective-permute-start(bf16[128,2048]{1,0:T(8,128)(2,1)} %bitcast.10), channel_id=1, source_target_pairs={{0,1},{1,0},{2,3},{3,2},{4,5},{5,4},{6,7},{7,6},{8,9},{9,8},{10,11... | collective-permute-start | bytes 1572872 | tf_op jit(solution)/shard_map/ppermute | solution.py:191
  6.1 1.6 %collective-permute-start.3 = (bf16[4,128,128]{2,1,0:T(8,128)(2,1)S(1)}, bf16[4,128,128]{2,1,0:T(8,128)(2,1)S(1)}, u32[]{:S(2)}, u32[]{:S(2)}) collective-permute-start(bf16[4,128,128]{2,1,0:T(8,128)(2,1)S(1)} %get-tuple-element.40), channel_id=1, source_target_pairs={{0,4},{2,6},{4,0},{6,2},{8,12},{10,14},{12,8},{14,10},{16,20},{18,... | collective-permute-start | bytes 393224 | tf_op jit(solution)/shard_map/ppermute | solution.py:187
  7.7 2.9 %convolution_convert_fusion.1.refs_3_.refs_2_ = bf16[128,1024]{1,0:T(8,128)(2,1)S(1)} fusion(bf16[2048,1024]{1,0:T(8,128)(2,1)} %param.9, bf16[1,128,2048]{2,1,0:T(8,128)(2,1)S(1)} %copy-done.5), kind=kOutput, calls=%fused_computation.5 | convolution fusion | flops 537001984 | bytes 4980736 | tf_op jit(solution)/shard_map/dot_general | solution.py:23
  12.8 3.5 %collective-permute-start.6 = (bf16[4,128,128]{2,1,0:T(8,128)(2,1)S(1)}, bf16[4,128,128]{2,1,0:T(8,128)(2,1)S(1)}, u32[]{:S(2)}, u32[]{:S(2)}) collective-permute-start(bf16[4,128,128]{2,1,0:T(8,128)(2,1)S(1)} %shard_map.86), channel_id=1, source_target_pairs={{0,8},{2,10},{4,12},{6,14},{8,16},{10,18},{12,20},{14,22},{16,24},... | collective-permute-start | bytes 393224 | tf_op jit(solution)/shard_map/ppermute | solution.py:246
  16.3 2.3 %collective-permute-start.5 = (bf16[4,128,128]{2,1,0:T(8,128)(2,1)S(1)}, bf16[4,128,128]{2,1,0:T(8,128)(2,1)S(1)}, u32[]{:S(2)}, u32[]{:S(2)}) collective-permute-start(bf16[4,128,128]{2,1,0:T(8,128)(2,1)S(1)} %shard_map.86), channel_id=1, source_target_pairs={{0,16},{2,18},{4,20},{6,22},{8,24},{10,26},{12,28},{14,30},{1,17},... | collective-permute-start | bytes 393224 | tf_op jit(solution)/shard_map/ppermute | solution.py:246
  20.1 1.5 %collective-permute-start.1 = (bf16[128,1024]{1,0:T(8,128)(2,1)S(1)}, bf16[128,1024]{1,0:T(8,128)(2,1)S(1)}, u32[]{:S(2)}, u32[]{:S(2)}) collective-permute-start(bf16[128,1024]{1,0:T(8,128)(2,1)S(1)} %convolution_convert_fusion.refs_6_), channel_id=1, source_target_pairs={{0,1},{1,0},{2,3},{3,2},{4,5},{5,4},{6,7},{7,6},{8,9},{9,8},{10,11... | collective-permute-start | bytes 786440 | tf_op jit(solution)/shard_map/ppermute | solution.py:191
  22.2 5.0 %collective-permute-done.5.refs_4_ = bf16[4,128,128]{2,1,0:T(8,128)(2,1)S(1)} collective-permute-done((bf16[4,128,128]{2,1,0:T(8,128)(2,1)S(1)}, bf16[4,128,128]{2,1,0:T(8,128)(2,1)S(1)}, u32[]{:S(2)}, u32[]{:S(2)}) %collective-permute-start.5) | collective-permute-done | bytes 131104 | tf_op jit(solution)/shard_map/ppermute | solution.py:246
  27.8 1.3 %collective-permute-start.8 = (bf16[4,128,128]{2,1,0:T(8,128)(2,1)S(1)}, bf16[4,128,128]{2,1,0:T(8,128)(2,1)S(1)}, u32[]{:S(2)}, u32[]{:S(2)}) collective-permute-start(bf16[4,128,128]{2,1,0:T(8,128)(2,1)S(1)} %get-tuple-element.45), channel_id=1, source_target_pairs={{0,4},{2,6},{4,0},{6,2},{8,12},{10,14},{12,8},{14,10},{16,20},{18,... | collective-permute-start | bytes 393224 | tf_op jit(solution)/shard_map/ppermute | solution.py:187
  30.7 3.6 %collective-permute-done.8.refs_2_ = bf16[4,128,128]{2,1,0:T(8,128)(2,1)S(1)} collective-permute-done((bf16[4,128,128]{2,1,0:T(8,128)(2,1)S(1)}, bf16[4,128,128]{2,1,0:T(8,128)(2,1)S(1)}, u32[]{:S(2)}, u32[]{:S(2)}) %collective-permute-start.8) | collective-permute-done | bytes 131104 | tf_op jit(solution)/shard_map/ppermute | solution.py:187
  36.6 1.7 %collective-permute-done.11.refs_3_.refs_2_ = bf16[2,128,512]{2,1,0:T(8,128)(2,1)S(1)} collective-permute-done((bf16[2,128,512]{2,1,0:T(8,128)(2,1)S(1)}, bf16[2,128,512]{2,1,0:T(8,128)(2,1)S(1)}, u32[]{:S(2)}, u32[]{:S(2)}) %collective-permute-start.11) | collective-permute-done | bytes 262176 | tf_op jit(solution)/shard_map/ppermute | solution.py:187
  39.9 1.5 %shard_map.94 = (bf16[128,1024]{1,0:T(8,128)(2,1)S(1)}, bf16[128,1024]{1,0:T(8,128)(2,1)S(1)}) custom-call(s32[4]{0:T(128)S(1)} %pad_add_fusion.refs_0_, bf16[1,128,2048]{2,1,0:T(8,128)(2,1)S(1)} %copy-done.4, bf16[1,128,2048]{2,1,0:T(8,128)(2,1)S(1)} %copy-done.1, bf16[1,128,2048]{2,1,0:T(8,128)(2,1)S(1)} %copy-done.3, ...), custom_call_target="tpu_custom_call" | custom-call | tf_op jit(solution)/shard_map/pallas_call | solution.py:33
  41.3 2.0 %collective-permute-start.20 = (bf16[128,1024]{1,0:T(8,128)(2,1)S(1)}, bf16[128,1024]{1,0:T(8,128)(2,1)S(1)}, u32[]{:S(2)}, u32[]{:S(2)}) collective-permute-start(bf16[128,1024]{1,0:T(8,128)(2,1)S(1)} %get-tuple-element.64), channel_id=1, source_target_pairs={{0,5},{1,4},{2,7},{3,6},{4,1},{5,0},{6,3},{7,2},{8,13},{9,12},{10,... | collective-permute-start | bytes 786440 | tf_op jit(solution)/shard_map/ppermute | solution.py:198
  45.5 1.9 %collective-permute-start.13 = (bf16[4,128,128]{2,1,0:T(8,128)(2,1)S(1)}, bf16[4,128,128]{2,1,0:T(8,128)(2,1)S(1)}, u32[]{:S(2)}, u32[]{:S(2)}) collective-permute-start(bf16[4,128,128]{2,1,0:T(8,128)(2,1)S(1)} %shard_map.95.refs_7_.refs_1_), channel_id=1, source_target_pairs={{8,0},{10,2},{12,4},{14,6},{16,8},{18,10},{20,12},{22,14},{24,16},... | collective-permute-start | bytes 393224 | tf_op jit(solution)/shard_map/ppermute | solution.py:246
  48.0 5.2 %shard_map.96 = (bf16[1,128,2048]{2,1,0:T(8,128)(2,1)}, f32[128,2048]{1,0:T(8,128)S(1)}, f32[128,2048]{1,0:T(8,128)S(1)}, f32[8,128]{1,0:T(8,128)S(1)}) custom-call(s32[4]{0:T(128)S(1)} %pad_add_fusion.refs_0_, bf16[1,128,2048]{2,1,0:T(8,128)(2,1)S(1)} %copy-done.4, bf16[1,128,2048]{2,1,0:T(8,128)(2,1)S(1)} %copy-done.1, ...), custom_call_target="tpu_custom_call" | custom-call | tf_op jit(solution)/shard_map/pallas_call | solution.py:33
  53.8 2.1 %collective-permute-done.19.refs_3_ = bf16[128,1024]{1,0:T(8,128)(2,1)S(1)} collective-permute-done((bf16[128,1024]{1,0:T(8,128)(2,1)S(1)}, bf16[128,1024]{1,0:T(8,128)(2,1)S(1)}, u32[]{:S(2)}, u32[]{:S(2)}) %collective-permute-start.19) | collective-permute-done | bytes 262176 | tf_op jit(solution)/shard_map/ppermute | solution.py:191
  57.2 1.3 %collective-permute-start.14 = (bf16[4,128,128]{2,1,0:T(8,128)(2,1)S(1)}, bf16[4,128,128]{2,1,0:T(8,128)(2,1)S(1)}, u32[]{:S(2)}, u32[]{:S(2)}) collective-permute-start(bf16[4,128,128]{2,1,0:T(8,128)(2,1)S(1)} %shard_map.97.refs_6_), channel_id=1, source_target_pairs={{16,0},{18,2},{20,4},{22,6},{24,8},{26,10},{28,12},{30,14},{17,1},... | collective-permute-start | bytes 393224 | tf_op jit(solution)/shard_map/ppermute | solution.py:246
  58.5 1.2 %collective-permute-done.16 = bf16[256,512]{1,0:T(8,128)(2,1)S(1)} collective-permute-done((bf16[256,512]{1,0:T(8,128)(2,1)S(1)}, bf16[256,512]{1,0:T(8,128)(2,1)S(1)}, u32[]{:S(2)}, u32[]{:S(2)}) %collective-permute-start.16) | collective-permute-done | bytes 262176 | tf_op jit(solution)/shard_map/ppermute | solution.py:187
  60.0 1.3 %fusion.17 = (bf16[512,1024]{1,0:T(8,128)(2,1)S(1)}, f32[512,1024]{1,0:T(8,128)S(1)}) fusion(bf16[512,1024]{1,0:T(8,128)(2,1)S(1)} %collective-permute-done.21, bf16[512,1024]{1,0:T(8,128)(2,1)S(1)} %shard_map.100, bf16[256,512]{1,0:T(8,128)(2,1)S(1)} %collective-permute-done.17, bf16[256,512]{1,0:T(8,128)(2,1)S(1)} %collective-permute-done.16, ...), kind=kOutput, calls=%fused_computation.21 | convolution fusion | flops 1082654720 | bytes 6291456 | tf_op jit(solution)/shard_map/dot_general | solution.py:23
  61.4 3.4 %collective-permute-start.24 = (bf16[128,1024]{1,0:T(8,128)(2,1)S(1)}, bf16[128,1024]{1,0:T(8,128)(2,1)S(1)}, u32[]{:S(2)}, u32[]{:S(2)}) collective-permute-start(bf16[128,1024]{1,0:T(8,128)(2,1)S(1)} %get-tuple-element.70), channel_id=1, source_target_pairs={{0,16},{2,18},{4,20},{6,22},{8,24},{10,26},{12,28},{14,30},{16,0},... | collective-permute-start | bytes 786440 | tf_op jit(solution)/shard_map/ppermute | solution.py:187
  67.7 4.1 %collective-permute-done.15.refs_2_ = bf16[4,128,128]{2,1,0:T(8,128)(2,1)S(1)} collective-permute-done((bf16[4,128,128]{2,1,0:T(8,128)(2,1)S(1)}, bf16[4,128,128]{2,1,0:T(8,128)(2,1)S(1)}, u32[]{:S(2)}, u32[]{:S(2)}) %collective-permute-start.15) | collective-permute-done | bytes 131104 | tf_op jit(solution)/shard_map/ppermute | solution.py:187
  71.8 1.3 %collective-permute-done.22.refs_5_ = bf16[128,1024]{1,0:T(8,128)(2,1)S(1)} collective-permute-done((bf16[128,1024]{1,0:T(8,128)(2,1)S(1)}, bf16[128,1024]{1,0:T(8,128)(2,1)S(1)}, u32[]{:S(2)}, u32[]{:S(2)}) %collective-permute-start.22) | collective-permute-done | bytes 262176 | tf_op jit(solution)/shard_map/ppermute | solution.py:187
  73.8 9.0 %collective-permute-done.24 = bf16[128,1024]{1,0:T(8,128)(2,1)S(1)} collective-permute-done((bf16[128,1024]{1,0:T(8,128)(2,1)S(1)}, bf16[128,1024]{1,0:T(8,128)(2,1)S(1)}, u32[]{:S(2)}, u32[]{:S(2)}) %collective-permute-start.24) | collective-permute-done | bytes 262176 | tf_op jit(solution)/shard_map/ppermute | solution.py:187
  82.8 5.8 %collective-permute-done.25 = bf16[128,1024]{1,0:T(8,128)(2,1)S(1)} collective-permute-done((bf16[128,1024]{1,0:T(8,128)(2,1)S(1)}, bf16[128,1024]{1,0:T(8,128)(2,1)S(1)}, u32[]{:S(2)}, u32[]{:S(2)}) %collective-permute-start.25) | collective-permute-done | bytes 262176 | tf_op jit(solution)/shard_map/ppermute | solution.py:187
  89.6 2.2 %shard_map.102 = (bf16[1,128,2048]{2,1,0:T(8,128)(2,1)}, bf16[1,128,2048]{2,1,0:T(8,128)(2,1)}) custom-call(s32[4]{0:T(128)S(1)} %pad_add_fusion.refs_0_, bf16[1,128,2048]{2,1,0:T(8,128)(2,1)S(1)} %copy-done.1, bf16[1,128,2048]{2,1,0:T(8,128)(2,1)S(1)} %copy-done.3, f32[128,2048]{1,0:T(8,128)S(1)} %get-tuple-element.56.refs_3_, ...), custom_call_target="tpu_custom_call" | custom-call | tf_op jit(solution)/shard_map/pallas_call | solution.py:33
  (67 shorter events, 23.7 us)
Async XLA Ops:
  3.9 15.4 %collective-permute-start = (bf16[128,2048]{1,0:T(8,128)(2,1)}, bf16[128,2048]{1,0:T(8,128)(2,1)S(1)}, u32[]{:S(2)}, u32[]{:S(2)}) collective-permute-start(bf16[128,2048]{1,0:T(8,128)(2,1)} %bitcast.10), channel_id=1, source_target_pairs={{0,1},{1,0},{2,3},{3,2},{4,5},{5,4},{6,7},{7,6},{8,9},{9,8},{10,11... | collective-permute-start | bytes 1572872 | tf_op jit(solution)/shard_map/ppermute | solution.py:191
  6.1 6.1 %collective-permute-start.3 = (bf16[4,128,128]{2,1,0:T(8,128)(2,1)S(1)}, bf16[4,128,128]{2,1,0:T(8,128)(2,1)S(1)}, u32[]{:S(2)}, u32[]{:S(2)}) collective-permute-start(bf16[4,128,128]{2,1,0:T(8,128)(2,1)S(1)} %get-tuple-element.40), channel_id=1, source_target_pairs={{0,4},{2,6},{4,0},{6,2},{8,12},{10,14},{12,8},{14,10},{16,20},{18,... | collective-permute-start | bytes 393224 | tf_op jit(solution)/shard_map/ppermute | solution.py:187
  11.3 10.3 %collective-permute-start.7 = (bf16[2,128,512]{2,1,0:T(8,128)(2,1)S(1)}, bf16[2,128,512]{2,1,0:T(8,128)(2,1)S(1)}, u32[]{:S(2)}, u32[]{:S(2)}) collective-permute-start(bf16[2,128,512]{2,1,0:T(8,128)(2,1)S(1)} %get-tuple-element.42), channel_id=1, source_target_pairs={{0,4},{2,6},{4,0},{6,2},{8,12},{10,14},{12,8},{14,10},{16,20},{18,... | collective-permute-start | bytes 786440 | tf_op jit(solution)/shard_map/ppermute | solution.py:187
  12.8 9.4 %collective-permute-start.6 = (bf16[4,128,128]{2,1,0:T(8,128)(2,1)S(1)}, bf16[4,128,128]{2,1,0:T(8,128)(2,1)S(1)}, u32[]{:S(2)}, u32[]{:S(2)}) collective-permute-start(bf16[4,128,128]{2,1,0:T(8,128)(2,1)S(1)} %shard_map.86), channel_id=1, source_target_pairs={{0,8},{2,10},{4,12},{6,14},{8,16},{10,18},{12,20},{14,22},{16,24},... | collective-permute-start | bytes 393224 | tf_op jit(solution)/shard_map/ppermute | solution.py:246
  16.3 10.9 %collective-permute-start.5 = (bf16[4,128,128]{2,1,0:T(8,128)(2,1)S(1)}, bf16[4,128,128]{2,1,0:T(8,128)(2,1)S(1)}, u32[]{:S(2)}, u32[]{:S(2)}) collective-permute-start(bf16[4,128,128]{2,1,0:T(8,128)(2,1)S(1)} %shard_map.86), channel_id=1, source_target_pairs={{0,16},{2,18},{4,20},{6,22},{8,24},{10,26},{12,28},{14,30},{1,17},... | collective-permute-start | bytes 393224 | tf_op jit(solution)/shard_map/ppermute | solution.py:246
  18.6 8.6 %collective-permute-start.4 = (bf16[4,128,128]{2,1,0:T(8,128)(2,1)S(1)}, bf16[4,128,128]{2,1,0:T(8,128)(2,1)S(1)}, u32[]{:S(2)}, u32[]{:S(2)}) collective-permute-start(bf16[4,128,128]{2,1,0:T(8,128)(2,1)S(1)} %shard_map.86), channel_id=1, source_target_pairs={{0,24},{2,26},{4,28},{6,30},{1,25},{3,27},{5,29},{7,31}} | collective-permute-start | bytes 393224 | tf_op jit(solution)/shard_map/ppermute | solution.py:246
  20.1 14.8 %collective-permute-start.1 = (bf16[128,1024]{1,0:T(8,128)(2,1)S(1)}, bf16[128,1024]{1,0:T(8,128)(2,1)S(1)}, u32[]{:S(2)}, u32[]{:S(2)}) collective-permute-start(bf16[128,1024]{1,0:T(8,128)(2,1)S(1)} %convolution_convert_fusion.refs_6_), channel_id=1, source_target_pairs={{0,1},{1,0},{2,3},{3,2},{4,5},{5,4},{6,7},{7,6},{8,9},{9,8},{10,11... | collective-permute-start | bytes 786440 | tf_op jit(solution)/shard_map/ppermute | solution.py:191
  27.8 6.4 %collective-permute-start.8 = (bf16[4,128,128]{2,1,0:T(8,128)(2,1)S(1)}, bf16[4,128,128]{2,1,0:T(8,128)(2,1)S(1)}, u32[]{:S(2)}, u32[]{:S(2)}) collective-permute-start(bf16[4,128,128]{2,1,0:T(8,128)(2,1)S(1)} %get-tuple-element.45), channel_id=1, source_target_pairs={{0,4},{2,6},{4,0},{6,2},{8,12},{10,14},{12,8},{14,10},{16,20},{18,... | collective-permute-start | bytes 393224 | tf_op jit(solution)/shard_map/ppermute | solution.py:187
  29.8 8.5 %collective-permute-start.11 = (bf16[2,128,512]{2,1,0:T(8,128)(2,1)S(1)}, bf16[2,128,512]{2,1,0:T(8,128)(2,1)S(1)}, u32[]{:S(2)}, u32[]{:S(2)}) collective-permute-start(bf16[2,128,512]{2,1,0:T(8,128)(2,1)S(1)} %get-tuple-element.51), channel_id=1, source_target_pairs={{0,4},{2,6},{4,0},{6,2},{8,12},{10,14},{12,8},{14,10},{16,20},{18,... | collective-permute-start | bytes 786440 | tf_op jit(solution)/shard_map/ppermute | solution.py:187
  36.1 3.8 %collective-permute-start.9 = (bf16[2,4,128,128]{3,2,1,0:T(8,128)(2,1)S(1)}, bf16[2,4,128,128]{3,2,1,0:T(8,128)(2,1)S(1)}, u32[]{:S(2)}, u32[]{:S(2)}) collective-permute-start(bf16[2,4,128,128]{3,2,1,0:T(8,128)(2,1)S(1)} %get-tuple-element.48), channel_id=1, source_target_pairs={{0,2},{2,0},{4,6},{6,4},{8,10},{10,8},{12,14},{14,12},{16,18},{18,... | collective-permute-start | bytes 786440 | tf_op jit(solution)/shard_map/ppermute | solution.py:187
  38.9 6.0 %collective-permute-start.12 = (bf16[4,128,128]{2,1,0:T(8,128)(2,1)S(1)}, bf16[4,128,128]{2,1,0:T(8,128)(2,1)S(1)}, u32[]{:S(2)}, u32[]{:S(2)}) collective-permute-start(bf16[4,128,128]{2,1,0:T(8,128)(2,1)S(1)} %get-tuple-element.53), channel_id=1, source_target_pairs={{0,4},{2,6},{4,0},{6,2},{8,12},{10,14},{12,8},{14,10},{16,20},{18,... | collective-permute-start | bytes 393224 | tf_op jit(solution)/shard_map/ppermute | solution.py:187
  41.3 12.5 %collective-permute-start.20 = (bf16[128,1024]{1,0:T(8,128)(2,1)S(1)}, bf16[128,1024]{1,0:T(8,128)(2,1)S(1)}, u32[]{:S(2)}, u32[]{:S(2)}) collective-permute-start(bf16[128,1024]{1,0:T(8,128)(2,1)S(1)} %get-tuple-element.64), channel_id=1, source_target_pairs={{0,5},{1,4},{2,7},{3,6},{4,1},{5,0},{6,3},{7,2},{8,13},{9,12},{10,... | collective-permute-start | bytes 786440 | tf_op jit(solution)/shard_map/ppermute | solution.py:198
  43.3 12.6 %collective-permute-start.19 = (bf16[128,1024]{1,0:T(8,128)(2,1)S(1)}, bf16[128,1024]{1,0:T(8,128)(2,1)S(1)}, u32[]{:S(2)}, u32[]{:S(2)}) collective-permute-start(bf16[128,1024]{1,0:T(8,128)(2,1)S(1)} %get-tuple-element.64), channel_id=1, source_target_pairs={{0,1},{1,0},{2,3},{3,2},{4,5},{5,4},{6,7},{7,6},{8,9},{9,8},{10,11... | collective-permute-start | bytes 786440 | tf_op jit(solution)/shard_map/ppermute | solution.py:191
  44.0 11.9 %collective-permute-start.18 = (bf16[128,1024]{1,0:T(8,128)(2,1)S(1)}, bf16[128,1024]{1,0:T(8,128)(2,1)S(1)}, u32[]{:S(2)}, u32[]{:S(2)}) collective-permute-start(bf16[128,1024]{1,0:T(8,128)(2,1)S(1)} %get-tuple-element.54.refs_3_.refs_1_), channel_id=1, source_target_pairs={{0,4},{2,6},{4,0},{6,2},{8,12},{10,14},{12,8},{14,10},{16,20},{18,... | collective-permute-start | bytes 786440 | tf_op jit(solution)/shard_map/ppermute | solution.py:187
  45.5 7.8 %collective-permute-start.13 = (bf16[4,128,128]{2,1,0:T(8,128)(2,1)S(1)}, bf16[4,128,128]{2,1,0:T(8,128)(2,1)S(1)}, u32[]{:S(2)}, u32[]{:S(2)}) collective-permute-start(bf16[4,128,128]{2,1,0:T(8,128)(2,1)S(1)} %shard_map.95.refs_7_.refs_1_), channel_id=1, source_target_pairs={{8,0},{10,2},{12,4},{14,6},{16,8},{18,10},{20,12},{22,14},{24,16},... | collective-permute-start | bytes 393224 | tf_op jit(solution)/shard_map/ppermute | solution.py:246
  56.5 3.5 %collective-permute-start.21 = (bf16[512,1024]{1,0:T(8,128)(2,1)S(1)}, bf16[512,1024]{1,0:T(8,128)(2,1)S(1)}, u32[]{:S(2)}, u32[]{:S(2)}) collective-permute-start(bf16[512,1024]{1,0:T(8,128)(2,1)S(1)} %shard_map.100), channel_id=1, source_target_pairs={{0,2},{2,0},{4,6},{6,4},{8,10},{10,8},{12,14},{14,12},{16,18},{18,... | collective-permute-start | bytes 3145736 | tf_op jit(solution)/shard_map/ppermute | solution.py:187
  56.6 3.0 %collective-permute-start.16 = (bf16[256,512]{1,0:T(8,128)(2,1)S(1)}, bf16[256,512]{1,0:T(8,128)(2,1)S(1)}, u32[]{:S(2)}, u32[]{:S(2)}) collective-permute-start(bf16[256,512]{1,0:T(8,128)(2,1)S(1)} %get-tuple-element.62), channel_id=1, source_target_pairs={{0,2},{2,0},{4,6},{6,4},{8,10},{10,8},{12,14},{14,12},{16,18},{18,... | collective-permute-start | bytes 786440 | tf_op jit(solution)/shard_map/ppermute | solution.py:187
  57.1 2.9 %collective-permute-start.17 = (bf16[256,512]{1,0:T(8,128)(2,1)S(1)}, bf16[256,512]{1,0:T(8,128)(2,1)S(1)}, u32[]{:S(2)}, u32[]{:S(2)}) collective-permute-start(bf16[256,512]{1,0:T(8,128)(2,1)S(1)} %get-tuple-element.63), channel_id=1, source_target_pairs={{0,2},{2,0},{4,6},{6,4},{8,10},{10,8},{12,14},{14,12},{16,18},{18,... | collective-permute-start | bytes 786440 | tf_op jit(solution)/shard_map/ppermute | solution.py:187
  57.2 8.9 %collective-permute-start.14 = (bf16[4,128,128]{2,1,0:T(8,128)(2,1)S(1)}, bf16[4,128,128]{2,1,0:T(8,128)(2,1)S(1)}, u32[]{:S(2)}, u32[]{:S(2)}) collective-permute-start(bf16[4,128,128]{2,1,0:T(8,128)(2,1)S(1)} %shard_map.97.refs_6_), channel_id=1, source_target_pairs={{16,0},{18,2},{20,4},{22,6},{24,8},{26,10},{28,12},{30,14},{17,1},... | collective-permute-start | bytes 393224 | tf_op jit(solution)/shard_map/ppermute | solution.py:246
  61.3 11.7 %collective-permute-start.22 = (bf16[128,1024]{1,0:T(8,128)(2,1)S(1)}, bf16[128,1024]{1,0:T(8,128)(2,1)S(1)}, u32[]{:S(2)}, u32[]{:S(2)}) collective-permute-start(bf16[128,1024]{1,0:T(8,128)(2,1)S(1)} %get-tuple-element.72), channel_id=1, source_target_pairs={{0,8},{2,10},{4,12},{6,14},{8,0},{10,2},{12,4},{14,6},{16,24},{18,... | collective-permute-start | bytes 786440 | tf_op jit(solution)/shard_map/ppermute | solution.py:187
  61.4 21.4 %collective-permute-start.24 = (bf16[128,1024]{1,0:T(8,128)(2,1)S(1)}, bf16[128,1024]{1,0:T(8,128)(2,1)S(1)}, u32[]{:S(2)}, u32[]{:S(2)}) collective-permute-start(bf16[128,1024]{1,0:T(8,128)(2,1)S(1)} %get-tuple-element.70), channel_id=1, source_target_pairs={{0,16},{2,18},{4,20},{6,22},{8,24},{10,26},{12,28},{14,30},{16,0},... | collective-permute-start | bytes 786440 | tf_op jit(solution)/shard_map/ppermute | solution.py:187
  64.8 23.8 %collective-permute-start.25 = (bf16[128,1024]{1,0:T(8,128)(2,1)S(1)}, bf16[128,1024]{1,0:T(8,128)(2,1)S(1)}, u32[]{:S(2)}, u32[]{:S(2)}) collective-permute-start(bf16[128,1024]{1,0:T(8,128)(2,1)S(1)} %get-tuple-element.71), channel_id=1, source_target_pairs={{0,24},{2,26},{4,28},{6,30},{8,16},{10,18},{12,20},{14,22},{16,8},... | collective-permute-start | bytes 786440 | tf_op jit(solution)/shard_map/ppermute | solution.py:187
  66.7 5.1 %collective-permute-start.15 = (bf16[4,128,128]{2,1,0:T(8,128)(2,1)S(1)}, bf16[4,128,128]{2,1,0:T(8,128)(2,1)S(1)}, u32[]{:S(2)}, u32[]{:S(2)}) collective-permute-start(bf16[4,128,128]{2,1,0:T(8,128)(2,1)S(1)} %get-tuple-element.59), channel_id=1, source_target_pairs={{0,4},{2,6},{4,0},{6,2},{8,12},{10,14},{12,8},{14,10},{16,20},{18,... | collective-permute-start | bytes 393224 | tf_op jit(solution)/shard_map/ppermute | solution.py:187
  73.7 15.8 %collective-permute-start.23 = (bf16[2,4,128,128]{3,2,1,0:T(8,128)(2,1)S(1)}, bf16[2,4,128,128]{3,2,1,0:T(8,128)(2,1)S(1)}, u32[]{:S(2)}, u32[]{:S(2)}) collective-permute-start(bf16[2,4,128,128]{3,2,1,0:T(8,128)(2,1)S(1)} %get-tuple-element.67), channel_id=1, source_target_pairs={{0,2},{2,0},{4,6},{6,4},{8,10},{10,8},{12,14},{14,12},{16,18},{18,... | collective-permute-start | bytes 786440 | tf_op jit(solution)/shard_map/ppermute | solution.py:187
  (9 other events, 60.4 us)

commit v4 on v3

--- a/solution.py
+++ b/solution.py
@@ -307,6 +307,7 @@
     attn_got = [dot(grads, out_weight, 1, 0).astype(BF16) for grads in grads_got]
     attn_back = [shift(attn_got[r - 1], -r, fsdp_devices) for r in others]
     rows_own = chip_rows(here, there, ids)
+    rows_own_other = swap(rows_own[1], 1, seq_devices)
     s_near = s_scan.before(after=(*attn_got, rows_own[0]))
     here_got, there_got = features(jnp.concatenate(grads_got), ids, levels, after=(s_near,))
     there_got = swap(there_got, 2, seq_devices)
@@ -324,7 +325,7 @@
     )
 
     g_scan = Scan(g_mine, g_send, ids, seq_devices, True, True)
-    g_scan.chip(after=(there_got,))
+    g_total = g_scan.chip(after=(there_got,))
 
     def attended_heads(ids, *refs):
         attended_kernel(fsdp_devices, factor, ids, *refs)
@@ -334,7 +335,7 @@
         ids,
         (queries, key_vectors, value_vectors, s_own, s_got),
         [((tokens, piece), BF16)] * fsdp_devices,
-        after=(g_mine,),
+        after=(g_total, rows_own_other),
     )
     near = [attended[0]] + [shift(attended[r], r, fsdp_devices) for r in others]
     across = [swap(attended[0], 2, seq_devices)]
@@ -354,7 +355,7 @@
         after=(g_plane,),
     )
     rows_got = chip_rows(here_got, there_got, ids)
-    g_double = g_scan.double()
+    g_double = g_scan.double(after=rows_got[:1])
     g_near = g_scan.before()
 
     (near,) = call(
@@ -365,13 +366,13 @@
         after=(blocks_ran, g_double, rows_got[0]),
     )
     grads_rows = jnp.concatenate(
-        [rows_own[0], rows_got[0], swap(rows_own[1], 1, seq_devices), swap(rows_got[1], 1, seq_devices)]
+        [rows_own[0], rows_got[0], rows_own_other, swap(rows_got[1], 1, seq_devices)]
     )
     attended_all = jnp.concatenate([near, swap(near, 1, seq_devices)])
     partial = dot(grads_rows, attended_all, 0, 0)
     chunks = [partial[k * rows : (k + 1) * rows].astype(BF16) for k in range(levels)]
     got = [swap(chunks[k], PLANE * k, seq_devices) for k in range(1, levels)]
-    g_own, g_got = g_scan.core(after=got[:1])
+    g_own, g_got = g_scan.core(after=got[:2])
 
     def later(ids, *refs):
         later_kernel(factor, ids, *refs)

time: 92 us -> 91.6 us (level)
  transfers between devices with their start and end apart: 26 -> 26, of which waited for: 11 -> 10; matrix products, arithmetic and copies ran while one was open for 6% -> 6% of each run, Pallas kernels for 17% -> 17%
where the time goes in v4:
time: 91.6 us; the launch traced here: 91.3 us
  waiting for transfers between devices  34.3 us (37%)
  starting transfers between devices  28.4 us (31%)
  Pallas kernels  19.5 us (21%)
  matrix products  4.93 us (5%)
  local copies, waits for them, and re-layouts  2.16 us (2%)
  other arithmetic  1.02 us (1%)
  between operations  0.96 us (1%)
    ppermute x17, waiting for transfers between devices, swap(): return lax.ppermute(value, 'seq', [(i, i ^ distance) for i in range(count)])  26.6 us
    pallas_call x19, Pallas kernels, call(): pl.pallas_call(run, out_shape=[jax.ShapeDtypeStruct(shape, dtype) for sha...  19.5 us
    ppermute x17, starting transfers between devices, swap(): return lax.ppermute(value, 'seq', [(i, i ^ distance) for i in range(count)])  13 us
    ppermute x5, starting transfers between devices, along(): return lax.ppermute(value, 'seq', route)  9.65 us
    ppermute x5, waiting for transfers between devices, along(): return lax.ppermute(value, 'seq', route)  5.6 us
    dot_general x3, matrix products, dot(): return lax.dot_general(a, b, dims, preferred_element_type=F32)  4.93 us
    ppermute x3, starting transfers between devices, shift(): lax.ppermute(value, 'fsdp', [(i, (i + r) % count) for i in range(count)])  3.74 us
    unnamed x14, local copies, waits for them, and re-layouts  2.11 us
  transfers between devices with their start and end apart: 26, of which 10 were waited for; matrix products, arithmetic and copies ran while one was open for 6% of the time, Pallas kernels for 17%

profile of v4, /device:TPU:8, one launch (start us, length us, event | category | flops | bytes accessed | tf_op | source)
XLA Modules:
  0.0 91.3 jit_solution(14884623607873952083)
XLA Ops:
  3.9 1.6 %collective-permute-start = (bf16[128,2048]{1,0:T(8,128)(2,1)}, bf16[128,2048]{1,0:T(8,128)(2,1)S(1)}, u32[]{:S(2)}, u32[]{:S(2)}) collective-permute-start(bf16[128,2048]{1,0:T(8,128)(2,1)} %bitcast.10), channel_id=1, source_target_pairs={{0,1},{1,0},{2,3},{3,2},{4,5},{5,4},{6,7},{7,6},{8,9},{9,8},{10,11... | collective-permute-start | bytes 1572872 | tf_op jit(solution)/shard_map/ppermute | solution.py:191
  6.1 1.6 %collective-permute-start.3 = (bf16[4,128,128]{2,1,0:T(8,128)(2,1)S(1)}, bf16[4,128,128]{2,1,0:T(8,128)(2,1)S(1)}, u32[]{:S(2)}, u32[]{:S(2)}) collective-permute-start(bf16[4,128,128]{2,1,0:T(8,128)(2,1)S(1)} %get-tuple-element.40), channel_id=1, source_target_pairs={{0,4},{2,6},{4,0},{6,2},{8,12},{10,14},{12,8},{14,10},{16,20},{18,... | collective-permute-start | bytes 393224 | tf_op jit(solution)/shard_map/ppermute | solution.py:187
  7.7 2.9 %convolution_convert_fusion.1.refs_3_.refs_2_ = bf16[128,1024]{1,0:T(8,128)(2,1)S(1)} fusion(bf16[2048,1024]{1,0:T(8,128)(2,1)} %param.9, bf16[1,128,2048]{2,1,0:T(8,128)(2,1)S(1)} %copy-done.5), kind=kOutput, calls=%fused_computation.5 | convolution fusion | flops 537001984 | bytes 4980736 | tf_op jit(solution)/shard_map/dot_general | solution.py:23
  12.8 3.5 %collective-permute-start.6 = (bf16[4,128,128]{2,1,0:T(8,128)(2,1)S(1)}, bf16[4,128,128]{2,1,0:T(8,128)(2,1)S(1)}, u32[]{:S(2)}, u32[]{:S(2)}) collective-permute-start(bf16[4,128,128]{2,1,0:T(8,128)(2,1)S(1)} %shard_map.86), channel_id=1, source_target_pairs={{0,8},{2,10},{4,12},{6,14},{8,16},{10,18},{12,20},{14,22},{16,24},... | collective-permute-start | bytes 393224 | tf_op jit(solution)/shard_map/ppermute | solution.py:246
  16.3 2.3 %collective-permute-start.5 = (bf16[4,128,128]{2,1,0:T(8,128)(2,1)S(1)}, bf16[4,128,128]{2,1,0:T(8,128)(2,1)S(1)}, u32[]{:S(2)}, u32[]{:S(2)}) collective-permute-start(bf16[4,128,128]{2,1,0:T(8,128)(2,1)S(1)} %shard_map.86), channel_id=1, source_target_pairs={{0,16},{2,18},{4,20},{6,22},{8,24},{10,26},{12,28},{14,30},{1,17},... | collective-permute-start | bytes 393224 | tf_op jit(solution)/shard_map/ppermute | solution.py:246
  20.0 1.5 %collective-permute-start.1 = (bf16[128,1024]{1,0:T(8,128)(2,1)S(1)}, bf16[128,1024]{1,0:T(8,128)(2,1)S(1)}, u32[]{:S(2)}, u32[]{:S(2)}) collective-permute-start(bf16[128,1024]{1,0:T(8,128)(2,1)S(1)} %convolution_convert_fusion.refs_6_), channel_id=1, source_target_pairs={{0,1},{1,0},{2,3},{3,2},{4,5},{5,4},{6,7},{7,6},{8,9},{9,8},{10,11... | collective-permute-start | bytes 786440 | tf_op jit(solution)/shard_map/ppermute | solution.py:191
  22.1 5.0 %collective-permute-done.5.refs_4_ = bf16[4,128,128]{2,1,0:T(8,128)(2,1)S(1)} collective-permute-done((bf16[4,128,128]{2,1,0:T(8,128)(2,1)S(1)}, bf16[4,128,128]{2,1,0:T(8,128)(2,1)S(1)}, u32[]{:S(2)}, u32[]{:S(2)}) %collective-permute-start.5) | collective-permute-done | bytes 131104 | tf_op jit(solution)/shard_map/ppermute | solution.py:246
  27.8 1.3 %collective-permute-start.8 = (bf16[4,128,128]{2,1,0:T(8,128)(2,1)S(1)}, bf16[4,128,128]{2,1,0:T(8,128)(2,1)S(1)}, u32[]{:S(2)}, u32[]{:S(2)}) collective-permute-start(bf16[4,128,128]{2,1,0:T(8,128)(2,1)S(1)} %get-tuple-element.45), channel_id=1, source_target_pairs={{0,4},{2,6},{4,0},{6,2},{8,12},{10,14},{12,8},{14,10},{16,20},{18,... | collective-permute-start | bytes 393224 | tf_op jit(solution)/shard_map/ppermute | solution.py:187
  30.7 3.6 %collective-permute-done.8.refs_2_ = bf16[4,128,128]{2,1,0:T(8,128)(2,1)S(1)} collective-permute-done((bf16[4,128,128]{2,1,0:T(8,128)(2,1)S(1)}, bf16[4,128,128]{2,1,0:T(8,128)(2,1)S(1)}, u32[]{:S(2)}, u32[]{:S(2)}) %collective-permute-start.8) | collective-permute-done | bytes 131104 | tf_op jit(solution)/shard_map/ppermute | solution.py:187
  36.6 1.6 %collective-permute-done.11.refs_3_.refs_2_ = bf16[2,128,512]{2,1,0:T(8,128)(2,1)S(1)} collective-permute-done((bf16[2,128,512]{2,1,0:T(8,128)(2,1)S(1)}, bf16[2,128,512]{2,1,0:T(8,128)(2,1)S(1)}, u32[]{:S(2)}, u32[]{:S(2)}) %collective-permute-start.11) | collective-permute-done | bytes 262176 | tf_op jit(solution)/shard_map/ppermute | solution.py:187
  39.9 1.5 %shard_map.94 = (bf16[128,1024]{1,0:T(8,128)(2,1)S(1)}, bf16[128,1024]{1,0:T(8,128)(2,1)S(1)}) custom-call(s32[4]{0:T(128)S(1)} %pad_add_fusion.refs_0_, bf16[1,128,2048]{2,1,0:T(8,128)(2,1)S(1)} %copy-done.4, bf16[1,128,2048]{2,1,0:T(8,128)(2,1)S(1)} %copy-done.1, bf16[1,128,2048]{2,1,0:T(8,128)(2,1)S(1)} %copy-done.3, ...), custom_call_target="tpu_custom_call" | custom-call | tf_op jit(solution)/shard_map/pallas_call | solution.py:33
  41.3 2.0 %collective-permute-start.20 = (bf16[128,1024]{1,0:T(8,128)(2,1)S(1)}, bf16[128,1024]{1,0:T(8,128)(2,1)S(1)}, u32[]{:S(2)}, u32[]{:S(2)}) collective-permute-start(bf16[128,1024]{1,0:T(8,128)(2,1)S(1)} %get-tuple-element.64), channel_id=1, source_target_pairs={{0,5},{1,4},{2,7},{3,6},{4,1},{5,0},{6,3},{7,2},{8,13},{9,12},{10,... | collective-permute-start | bytes 786440 | tf_op jit(solution)/shard_map/ppermute | solution.py:198
  45.4 1.9 %collective-permute-start.14 = (bf16[4,128,128]{2,1,0:T(8,128)(2,1)S(1)}, bf16[4,128,128]{2,1,0:T(8,128)(2,1)S(1)}, u32[]{:S(2)}, u32[]{:S(2)}) collective-permute-start(bf16[4,128,128]{2,1,0:T(8,128)(2,1)S(1)} %shard_map.95.refs_7_.refs_1_), channel_id=1, source_target_pairs={{8,0},{10,2},{12,4},{14,6},{16,8},{18,10},{20,12},{22,14},{24,16},... | collective-permute-start | bytes 393224 | tf_op jit(solution)/shard_map/ppermute | solution.py:246
  48.0 5.2 %shard_map.96 = (bf16[1,128,2048]{2,1,0:T(8,128)(2,1)}, f32[128,2048]{1,0:T(8,128)S(1)}, f32[128,2048]{1,0:T(8,128)S(1)}, f32[8,128]{1,0:T(8,128)S(1)}) custom-call(s32[4]{0:T(128)S(1)} %pad_add_fusion.refs_0_, bf16[1,128,2048]{2,1,0:T(8,128)(2,1)S(1)} %copy-done.4, bf16[1,128,2048]{2,1,0:T(8,128)(2,1)S(1)} %copy-done.1, ...), custom_call_target="tpu_custom_call" | custom-call | tf_op jit(solution)/shard_map/pallas_call | solution.py:33
  53.8 2.1 %collective-permute-done.19.refs_3_ = bf16[128,1024]{1,0:T(8,128)(2,1)S(1)} collective-permute-done((bf16[128,1024]{1,0:T(8,128)(2,1)S(1)}, bf16[128,1024]{1,0:T(8,128)(2,1)S(1)}, u32[]{:S(2)}, u32[]{:S(2)}) %collective-permute-start.19) | collective-permute-done | bytes 262176 | tf_op jit(solution)/shard_map/ppermute | solution.py:191
  57.1 1.3 %collective-permute-start.15 = (bf16[4,128,128]{2,1,0:T(8,128)(2,1)S(1)}, bf16[4,128,128]{2,1,0:T(8,128)(2,1)S(1)}, u32[]{:S(2)}, u32[]{:S(2)}) collective-permute-start(bf16[4,128,128]{2,1,0:T(8,128)(2,1)S(1)} %shard_map.98.refs_6_), channel_id=1, source_target_pairs={{16,0},{18,2},{20,4},{22,6},{24,8},{26,10},{28,12},{30,14},{17,1},... | collective-permute-start | bytes 393224 | tf_op jit(solution)/shard_map/ppermute | solution.py:246
  58.4 1.2 %collective-permute-done.17 = bf16[256,512]{1,0:T(8,128)(2,1)S(1)} collective-permute-done((bf16[256,512]{1,0:T(8,128)(2,1)S(1)}, bf16[256,512]{1,0:T(8,128)(2,1)S(1)}, u32[]{:S(2)}, u32[]{:S(2)}) %collective-permute-start.17) | collective-permute-done | bytes 262176 | tf_op jit(solution)/shard_map/ppermute | solution.py:187
  59.6 1.3 %fusion.17 = (bf16[512,1024]{1,0:T(8,128)(2,1)S(1)}, f32[512,1024]{1,0:T(8,128)S(1)}) fusion(bf16[512,1024]{1,0:T(8,128)(2,1)S(1)} %collective-permute-done.21, bf16[512,1024]{1,0:T(8,128)(2,1)S(1)} %shard_map.100, bf16[256,512]{1,0:T(8,128)(2,1)S(1)} %collective-permute-done.17, bf16[256,512]{1,0:T(8,128)(2,1)S(1)} %collective-permute-done.13.refs_7_, ...), kind=kOutput, calls=%fused_computation.21 | convolution fusion | flops 1082654720 | bytes 6291456 | tf_op jit(solution)/shard_map/dot_general | solution.py:23
  61.0 3.4 %collective-permute-start.23 = (bf16[128,1024]{1,0:T(8,128)(2,1)S(1)}, bf16[128,1024]{1,0:T(8,128)(2,1)S(1)}, u32[]{:S(2)}, u32[]{:S(2)}) collective-permute-start(bf16[128,1024]{1,0:T(8,128)(2,1)S(1)} %get-tuple-element.71), channel_id=1, source_target_pairs={{0,16},{2,18},{4,20},{6,22},{8,24},{10,26},{12,28},{14,30},{16,0},... | collective-permute-start | bytes 786440 | tf_op jit(solution)/shard_map/ppermute | solution.py:187
  67.3 4.0 %collective-permute-done.16.refs_2_ = bf16[4,128,128]{2,1,0:T(8,128)(2,1)S(1)} collective-permute-done((bf16[4,128,128]{2,1,0:T(8,128)(2,1)S(1)}, bf16[4,128,128]{2,1,0:T(8,128)(2,1)S(1)}, u32[]{:S(2)}, u32[]{:S(2)}) %collective-permute-start.16) | collective-permute-done | bytes 131104 | tf_op jit(solution)/shard_map/ppermute | solution.py:187
  71.3 2.8 %collective-permute-done.23.refs_6_ = bf16[128,1024]{1,0:T(8,128)(2,1)S(1)} collective-permute-done((bf16[128,1024]{1,0:T(8,128)(2,1)S(1)}, bf16[128,1024]{1,0:T(8,128)(2,1)S(1)}, u32[]{:S(2)}, u32[]{:S(2)}) %collective-permute-start.23) | collective-permute-done | bytes 262176 | tf_op jit(solution)/shard_map/ppermute | solution.py:187
  74.1 1.2 %collective-permute-done.22.refs_5_ = bf16[128,1024]{1,0:T(8,128)(2,1)S(1)} collective-permute-done((bf16[128,1024]{1,0:T(8,128)(2,1)S(1)}, bf16[128,1024]{1,0:T(8,128)(2,1)S(1)}, u32[]{:S(2)}, u32[]{:S(2)}) %collective-permute-start.22) | collective-permute-done | bytes 262176 | tf_op jit(solution)/shard_map/ppermute | solution.py:187
  76.0 12.2 %collective-permute-done.25 = bf16[128,1024]{1,0:T(8,128)(2,1)S(1)} collective-permute-done((bf16[128,1024]{1,0:T(8,128)(2,1)S(1)}, bf16[128,1024]{1,0:T(8,128)(2,1)S(1)}, u32[]{:S(2)}, u32[]{:S(2)}) %collective-permute-start.25) | collective-permute-done | bytes 262176 | tf_op jit(solution)/shard_map/ppermute | solution.py:187
  89.1 2.2 %shard_map.102 = (bf16[1,128,2048]{2,1,0:T(8,128)(2,1)}, bf16[1,128,2048]{2,1,0:T(8,128)(2,1)}) custom-call(s32[4]{0:T(128)S(1)} %pad_add_fusion.refs_0_, bf16[1,128,2048]{2,1,0:T(8,128)(2,1)S(1)} %copy-done.1, bf16[1,128,2048]{2,1,0:T(8,128)(2,1)S(1)} %copy-done.3, f32[128,2048]{1,0:T(8,128)S(1)} %get-tuple-element.57.refs_3_, ...), custom_call_target="tpu_custom_call" | custom-call | tf_op jit(solution)/shard_map/pallas_call | solution.py:33
  (67 shorter events, 23.2 us)
Async XLA Ops:
  3.9 15.3 %collective-permute-start = (bf16[128,2048]{1,0:T(8,128)(2,1)}, bf16[128,2048]{1,0:T(8,128)(2,1)S(1)}, u32[]{:S(2)}, u32[]{:S(2)}) collective-permute-start(bf16[128,2048]{1,0:T(8,128)(2,1)} %bitcast.10), channel_id=1, source_target_pairs={{0,1},{1,0},{2,3},{3,2},{4,5},{5,4},{6,7},{7,6},{8,9},{9,8},{10,11... | collective-permute-start | bytes 1572872 | tf_op jit(solution)/shard_map/ppermute | solution.py:191
  6.1 6.1 %collective-permute-start.3 = (bf16[4,128,128]{2,1,0:T(8,128)(2,1)S(1)}, bf16[4,128,128]{2,1,0:T(8,128)(2,1)S(1)}, u32[]{:S(2)}, u32[]{:S(2)}) collective-permute-start(bf16[4,128,128]{2,1,0:T(8,128)(2,1)S(1)} %get-tuple-element.40), channel_id=1, source_target_pairs={{0,4},{2,6},{4,0},{6,2},{8,12},{10,14},{12,8},{14,10},{16,20},{18,... | collective-permute-start | bytes 393224 | tf_op jit(solution)/shard_map/ppermute | solution.py:187
  11.3 10.3 %collective-permute-start.7 = (bf16[2,128,512]{2,1,0:T(8,128)(2,1)S(1)}, bf16[2,128,512]{2,1,0:T(8,128)(2,1)S(1)}, u32[]{:S(2)}, u32[]{:S(2)}) collective-permute-start(bf16[2,128,512]{2,1,0:T(8,128)(2,1)S(1)} %get-tuple-element.42), channel_id=1, source_target_pairs={{0,4},{2,6},{4,0},{6,2},{8,12},{10,14},{12,8},{14,10},{16,20},{18,... | collective-permute-start | bytes 786440 | tf_op jit(solution)/shard_map/ppermute | solution.py:187
  12.8 9.3 %collective-permute-start.6 = (bf16[4,128,128]{2,1,0:T(8,128)(2,1)S(1)}, bf16[4,128,128]{2,1,0:T(8,128)(2,1)S(1)}, u32[]{:S(2)}, u32[]{:S(2)}) collective-permute-start(bf16[4,128,128]{2,1,0:T(8,128)(2,1)S(1)} %shard_map.86), channel_id=1, source_target_pairs={{0,8},{2,10},{4,12},{6,14},{8,16},{10,18},{12,20},{14,22},{16,24},... | collective-permute-start | bytes 393224 | tf_op jit(solution)/shard_map/ppermute | solution.py:246
  16.3 10.9 %collective-permute-start.5 = (bf16[4,128,128]{2,1,0:T(8,128)(2,1)S(1)}, bf16[4,128,128]{2,1,0:T(8,128)(2,1)S(1)}, u32[]{:S(2)}, u32[]{:S(2)}) collective-permute-start(bf16[4,128,128]{2,1,0:T(8,128)(2,1)S(1)} %shard_map.86), channel_id=1, source_target_pairs={{0,16},{2,18},{4,20},{6,22},{8,24},{10,26},{12,28},{14,30},{1,17},... | collective-permute-start | bytes 393224 | tf_op jit(solution)/shard_map/ppermute | solution.py:246
  18.6 8.6 %collective-permute-start.4 = (bf16[4,128,128]{2,1,0:T(8,128)(2,1)S(1)}, bf16[4,128,128]{2,1,0:T(8,128)(2,1)S(1)}, u32[]{:S(2)}, u32[]{:S(2)}) collective-permute-start(bf16[4,128,128]{2,1,0:T(8,128)(2,1)S(1)} %shard_map.86), channel_id=1, source_target_pairs={{0,24},{2,26},{4,28},{6,30},{1,25},{3,27},{5,29},{7,31}} | collective-permute-start | bytes 393224 | tf_op jit(solution)/shard_map/ppermute | solution.py:246
  20.0 14.9 %collective-permute-start.1 = (bf16[128,1024]{1,0:T(8,128)(2,1)S(1)}, bf16[128,1024]{1,0:T(8,128)(2,1)S(1)}, u32[]{:S(2)}, u32[]{:S(2)}) collective-permute-start(bf16[128,1024]{1,0:T(8,128)(2,1)S(1)} %convolution_convert_fusion.refs_6_), channel_id=1, source_target_pairs={{0,1},{1,0},{2,3},{3,2},{4,5},{5,4},{6,7},{7,6},{8,9},{9,8},{10,11... | collective-permute-start | bytes 786440 | tf_op jit(solution)/shard_map/ppermute | solution.py:191
  27.8 6.4 %collective-permute-start.8 = (bf16[4,128,128]{2,1,0:T(8,128)(2,1)S(1)}, bf16[4,128,128]{2,1,0:T(8,128)(2,1)S(1)}, u32[]{:S(2)}, u32[]{:S(2)}) collective-permute-start(bf16[4,128,128]{2,1,0:T(8,128)(2,1)S(1)} %get-tuple-element.45), channel_id=1, source_target_pairs={{0,4},{2,6},{4,0},{6,2},{8,12},{10,14},{12,8},{14,10},{16,20},{18,... | collective-permute-start | bytes 393224 | tf_op jit(solution)/shard_map/ppermute | solution.py:187
  29.8 8.5 %collective-permute-start.11 = (bf16[2,128,512]{2,1,0:T(8,128)(2,1)S(1)}, bf16[2,128,512]{2,1,0:T(8,128)(2,1)S(1)}, u32[]{:S(2)}, u32[]{:S(2)}) collective-permute-start(bf16[2,128,512]{2,1,0:T(8,128)(2,1)S(1)} %get-tuple-element.51), channel_id=1, source_target_pairs={{0,4},{2,6},{4,0},{6,2},{8,12},{10,14},{12,8},{14,10},{16,20},{18,... | collective-permute-start | bytes 786440 | tf_op jit(solution)/shard_map/ppermute | solution.py:187
  36.1 3.8 %collective-permute-start.13 = (bf16[256,512]{1,0:T(8,128)(2,1)S(1)}, bf16[256,512]{1,0:T(8,128)(2,1)S(1)}, u32[]{:S(2)}, u32[]{:S(2)}) collective-permute-start(bf16[256,512]{1,0:T(8,128)(2,1)S(1)} %get-tuple-element.54), channel_id=1, source_target_pairs={{0,2},{2,0},{4,6},{6,4},{8,10},{10,8},{12,14},{14,12},{16,18},{18,... | collective-permute-start | bytes 786440 | tf_op jit(solution)/shard_map/ppermute | solution.py:187
  36.5 3.3 %collective-permute-start.9 = (bf16[2,4,128,128]{3,2,1,0:T(8,128)(2,1)S(1)}, bf16[2,4,128,128]{3,2,1,0:T(8,128)(2,1)S(1)}, u32[]{:S(2)}, u32[]{:S(2)}) collective-permute-start(bf16[2,4,128,128]{3,2,1,0:T(8,128)(2,1)S(1)} %get-tuple-element.48), channel_id=1, source_target_pairs={{0,2},{2,0},{4,6},{6,4},{8,10},{10,8},{12,14},{14,12},{16,18},{18,... | collective-permute-start | bytes 786440 | tf_op jit(solution)/shard_map/ppermute | solution.py:187
  38.8 6.0 %collective-permute-start.12 = (bf16[4,128,128]{2,1,0:T(8,128)(2,1)S(1)}, bf16[4,128,128]{2,1,0:T(8,128)(2,1)S(1)}, u32[]{:S(2)}, u32[]{:S(2)}) collective-permute-start(bf16[4,128,128]{2,1,0:T(8,128)(2,1)S(1)} %get-tuple-element.53), channel_id=1, source_target_pairs={{0,4},{2,6},{4,0},{6,2},{8,12},{10,14},{12,8},{14,10},{16,20},{18,... | collective-permute-start | bytes 393224 | tf_op jit(solution)/shard_map/ppermute | solution.py:187
  41.3 12.5 %collective-permute-start.20 = (bf16[128,1024]{1,0:T(8,128)(2,1)S(1)}, bf16[128,1024]{1,0:T(8,128)(2,1)S(1)}, u32[]{:S(2)}, u32[]{:S(2)}) collective-permute-start(bf16[128,1024]{1,0:T(8,128)(2,1)S(1)} %get-tuple-element.64), channel_id=1, source_target_pairs={{0,5},{1,4},{2,7},{3,6},{4,1},{5,0},{6,3},{7,2},{8,13},{9,12},{10,... | collective-permute-start | bytes 786440 | tf_op jit(solution)/shard_map/ppermute | solution.py:198
  43.3 12.6 %collective-permute-start.19 = (bf16[128,1024]{1,0:T(8,128)(2,1)S(1)}, bf16[128,1024]{1,0:T(8,128)(2,1)S(1)}, u32[]{:S(2)}, u32[]{:S(2)}) collective-permute-start(bf16[128,1024]{1,0:T(8,128)(2,1)S(1)} %get-tuple-element.64), channel_id=1, source_target_pairs={{0,1},{1,0},{2,3},{3,2},{4,5},{5,4},{6,7},{7,6},{8,9},{9,8},{10,11... | collective-permute-start | bytes 786440 | tf_op jit(solution)/shard_map/ppermute | solution.py:191
  43.9 11.9 %collective-permute-start.18 = (bf16[128,1024]{1,0:T(8,128)(2,1)S(1)}, bf16[128,1024]{1,0:T(8,128)(2,1)S(1)}, u32[]{:S(2)}, u32[]{:S(2)}) collective-permute-start(bf16[128,1024]{1,0:T(8,128)(2,1)S(1)} %get-tuple-element.55.refs_3_.refs_1_), channel_id=1, source_target_pairs={{0,4},{2,6},{4,0},{6,2},{8,12},{10,14},{12,8},{14,10},{16,20},{18,... | collective-permute-start | bytes 786440 | tf_op jit(solution)/shard_map/ppermute | solution.py:187
  45.4 7.8 %collective-permute-start.14 = (bf16[4,128,128]{2,1,0:T(8,128)(2,1)S(1)}, bf16[4,128,128]{2,1,0:T(8,128)(2,1)S(1)}, u32[]{:S(2)}, u32[]{:S(2)}) collective-permute-start(bf16[4,128,128]{2,1,0:T(8,128)(2,1)S(1)} %shard_map.95.refs_7_.refs_1_), channel_id=1, source_target_pairs={{8,0},{10,2},{12,4},{14,6},{16,8},{18,10},{20,12},{22,14},{24,16},... | collective-permute-start | bytes 393224 | tf_op jit(solution)/shard_map/ppermute | solution.py:246
  56.5 3.1 %collective-permute-start.21 = (bf16[512,1024]{1,0:T(8,128)(2,1)S(1)}, bf16[512,1024]{1,0:T(8,128)(2,1)S(1)}, u32[]{:S(2)}, u32[]{:S(2)}) collective-permute-start(bf16[512,1024]{1,0:T(8,128)(2,1)S(1)} %shard_map.100), channel_id=1, source_target_pairs={{0,2},{2,0},{4,6},{6,4},{8,10},{10,8},{12,14},{14,12},{16,18},{18,... | collective-permute-start | bytes 3145736 | tf_op jit(solution)/shard_map/ppermute | solution.py:187
  56.6 3.0 %collective-permute-start.17 = (bf16[256,512]{1,0:T(8,128)(2,1)S(1)}, bf16[256,512]{1,0:T(8,128)(2,1)S(1)}, u32[]{:S(2)}, u32[]{:S(2)}) collective-permute-start(bf16[256,512]{1,0:T(8,128)(2,1)S(1)} %get-tuple-element.63), channel_id=1, source_target_pairs={{0,2},{2,0},{4,6},{6,4},{8,10},{10,8},{12,14},{14,12},{16,18},{18,... | collective-permute-start | bytes 786440 | tf_op jit(solution)/shard_map/ppermute | solution.py:187
  57.1 8.5 %collective-permute-start.15 = (bf16[4,128,128]{2,1,0:T(8,128)(2,1)S(1)}, bf16[4,128,128]{2,1,0:T(8,128)(2,1)S(1)}, u32[]{:S(2)}, u32[]{:S(2)}) collective-permute-start(bf16[4,128,128]{2,1,0:T(8,128)(2,1)S(1)} %shard_map.98.refs_6_), channel_id=1, source_target_pairs={{16,0},{18,2},{20,4},{22,6},{24,8},{26,10},{28,12},{30,14},{17,1},... | collective-permute-start | bytes 393224 | tf_op jit(solution)/shard_map/ppermute | solution.py:246
  61.0 13.1 %collective-permute-start.23 = (bf16[128,1024]{1,0:T(8,128)(2,1)S(1)}, bf16[128,1024]{1,0:T(8,128)(2,1)S(1)}, u32[]{:S(2)}, u32[]{:S(2)}) collective-permute-start(bf16[128,1024]{1,0:T(8,128)(2,1)S(1)} %get-tuple-element.71), channel_id=1, source_target_pairs={{0,16},{2,18},{4,20},{6,22},{8,24},{10,26},{12,28},{14,30},{16,0},... | collective-permute-start | bytes 786440 | tf_op jit(solution)/shard_map/ppermute | solution.py:187
  64.4 10.8 %collective-permute-start.22 = (bf16[128,1024]{1,0:T(8,128)(2,1)S(1)}, bf16[128,1024]{1,0:T(8,128)(2,1)S(1)}, u32[]{:S(2)}, u32[]{:S(2)}) collective-permute-start(bf16[128,1024]{1,0:T(8,128)(2,1)S(1)} %get-tuple-element.72), channel_id=1, source_target_pairs={{0,8},{2,10},{4,12},{6,14},{8,0},{10,2},{12,4},{14,6},{16,24},{18,... | collective-permute-start | bytes 786440 | tf_op jit(solution)/shard_map/ppermute | solution.py:187
  64.4 23.8 %collective-permute-start.25 = (bf16[128,1024]{1,0:T(8,128)(2,1)S(1)}, bf16[128,1024]{1,0:T(8,128)(2,1)S(1)}, u32[]{:S(2)}, u32[]{:S(2)}) collective-permute-start(bf16[128,1024]{1,0:T(8,128)(2,1)S(1)} %get-tuple-element.70), channel_id=1, source_target_pairs={{0,24},{2,26},{4,28},{6,30},{8,16},{10,18},{12,20},{14,22},{16,8},... | collective-permute-start | bytes 786440 | tf_op jit(solution)/shard_map/ppermute | solution.py:187
  66.2 5.0 %collective-permute-start.16 = (bf16[4,128,128]{2,1,0:T(8,128)(2,1)S(1)}, bf16[4,128,128]{2,1,0:T(8,128)(2,1)S(1)}, u32[]{:S(2)}, u32[]{:S(2)}) collective-permute-start(bf16[4,128,128]{2,1,0:T(8,128)(2,1)S(1)} %get-tuple-element.62), channel_id=1, source_target_pairs={{0,4},{2,6},{4,0},{6,2},{8,12},{10,14},{12,8},{14,10},{16,20},{18,... | collective-permute-start | bytes 393224 | tf_op jit(solution)/shard_map/ppermute | solution.py:187
  75.9 13.2 %collective-permute-start.24 = (bf16[2,4,128,128]{3,2,1,0:T(8,128)(2,1)S(1)}, bf16[2,4,128,128]{3,2,1,0:T(8,128)(2,1)S(1)}, u32[]{:S(2)}, u32[]{:S(2)}) collective-permute-start(bf16[2,4,128,128]{3,2,1,0:T(8,128)(2,1)S(1)} %get-tuple-element.67), channel_id=1, source_target_pairs={{0,2},{2,0},{4,6},{6,4},{8,10},{10,8},{12,14},{14,12},{16,18},{18,... | collective-permute-start | bytes 786440 | tf_op jit(solution)/shard_map/ppermute | solution.py:187
  (9 other events, 60.4 us)

commit v5 on v4

--- a/solution.py
+++ b/solution.py
@@ -23,7 +23,7 @@
     return lax.dot_general(a, b, dims, preferred_element_type=F32)
 
 
-def call(kernel, ids, arrays, outs, after=()):
+def call(kernel, ids, arrays, outs, after=(), stored=False, scratch=()):
     vmem = pl.BlockSpec(memory_space=pltpu.VMEM)
     first, last = (1 + len(arrays), 1 + len(arrays) + len(after))
 
@@ -36,7 +36,8 @@
         in_specs=[pl.BlockSpec(memory_space=pltpu.SMEM)]
         + [vmem] * len(arrays)
         + [pl.BlockSpec(memory_space=pl.ANY)] * len(after),
-        out_specs=[vmem] * len(outs),
+        out_specs=[pl.BlockSpec(memory_space=pl.ANY) if stored else vmem] * len(outs),
+        scratch_shapes=scratch,
         compiler_params=pltpu.CompilerParams(vmem_limit_bytes=VMEM_LIMIT),
     )(ids, *arrays, *after)
 
@@ -124,17 +125,28 @@
 
 
 def later_kernel(
-    factor, ids, k_ref, v_ref, key_in, value_in, own_ref, got_ref, key_ref, value_ref
+    factor, ids, k_ref, v_ref, key_in, value_in, own_ref, got_ref, key_out, value_out, key_ref, value_ref, sems
 ):
-    def body(other, far, slot, cols):
-        k, v = (k_ref[0, :, cols], v_ref[0, :, cols])
-        state = (own_ref, got_ref)[other][far, slot]
-        key = dot(v, state, 1, 1) + key_in[:, cols]
-        value = dot(k, state, 1, 0) + value_in[:, cols]
-        key_ref[0, :, cols] = (factor * key).astype(BF16)
-        value_ref[0, :, cols] = (factor * value).astype(BF16)
-
-    each_head(ids, body)
+    x, c = (ids[1], ids[2])
+    width = PLANE * HEAD_DIM
+    copies = []
+    for slot in range(SLOTS):
+        for other in range(2):
+            for far in range(2):
+                cols = columns(4 * slot + 2 * (x ^ far) + (c ^ other))
+                k, v = (k_ref[0, :, cols], v_ref[0, :, cols])
+                state = (own_ref, got_ref)[other][far, slot]
+                key = dot(v, state, 1, 1) + key_in[:, cols]
+                value = dot(k, state, 1, 0) + value_in[:, cols]
+                key_ref[0, :, cols] = (factor * key).astype(BF16)
+                value_ref[0, :, cols] = (factor * value).astype(BF16)
+        done = pl.ds(slot * width, width)
+        for at, (ref, out) in enumerate(((key_ref, key_out), (value_ref, value_out))):
+            copy = pltpu.make_async_copy(ref.at[:, :, done], out.at[:, :, done], sems.at[at, slot])
+            copy.start()
+            copies.append(copy)
+    for copy in copies:
+        copy.wait()
 
 
 def features_kernel(levels, ids, in_ref, here_ref, there_ref):
@@ -363,7 +375,7 @@
         ids,
         (near[0], across[0], *near[1:], *across[1:]),
         [((2 * fsdp_devices * tokens, piece), BF16)],
-        after=(blocks_ran, g_double, rows_got[0]),
+        after=(g_double, rows_got[0]),
     )
     grads_rows = jnp.concatenate(
         [rows_own[0], rows_got[0], rows_own_other, swap(rows_got[1], 1, seq_devices)]
@@ -382,6 +394,12 @@
         ids,
         (key_vectors, value_vectors, key_part, value_part, g_own, g_got),
         [(queries.shape, BF16)] * 2,
+        stored=True,
+        scratch=[
+            pltpu.VMEM(queries.shape, BF16),
+            pltpu.VMEM(queries.shape, BF16),
+            pltpu.SemaphoreType.DMA((2, SLOTS)),
+        ],
     )
     weight_grad = partial[:rows]
     for chunk in got:

time: 91.6 us -> 91.4 us (level)
    ppermute x17, waiting for transfers between devices: 26.6 us -> 21.3 us  [swap(): return lax.ppermute(value, 'seq', [(i, i ^ distance) for i in range(count)])]
    ppermute x5, waiting for transfers between devices: 5.6 us -> 9.94 us  [along(): return lax.ppermute(value, 'seq', route)]
  transfers between devices with their start and end apart: 26 -> 26, of which waited for: 10 -> 10; matrix products, arithmetic and copies ran while one was open for 6% -> 7% of each run, Pallas kernels for 17% -> 17%
where the time goes in v5:
time: 91.4 us; the launch traced here: 91.1 us
  waiting for transfers between devices  34.3 us (38%)
  starting transfers between devices  28.4 us (31%)
  Pallas kernels  19.3 us (21%)
  matrix products  4.95 us (5%)
  local copies, waits for them, and re-layouts  2.16 us (2%)
  other arithmetic  1.02 us (1%)
  between operations  0.96 us (1%)
    ppermute x17, waiting for transfers between devices, swap(): return lax.ppermute(value, 'seq', [(i, i ^ distance) for i in range(count)])  21.3 us
    pallas_call x19, Pallas kernels, call(): pl.pallas_call(run, out_shape=[jax.ShapeDtypeStruct(shape, dtype) for sha...  19.3 us
    ppermute x17, starting transfers between devices, swap(): return lax.ppermute(value, 'seq', [(i, i ^ distance) for i in range(count)])  13 us
    ppermute x5, waiting for transfers between devices, along(): return lax.ppermute(value, 'seq', route)  9.94 us
    ppermute x5, starting transfers between devices, along(): return lax.ppermute(value, 'seq', route)  9.65 us
    dot_general x3, matrix products, dot(): return lax.dot_general(a, b, dims, preferred_element_type=F32)  4.95 us
    ppermute x3, starting transfers between devices, shift(): lax.ppermute(value, 'fsdp', [(i, (i + r) % count) for i in range(count)])  3.74 us
    ppermute x3, waiting for transfers between devices, shift(): lax.ppermute(value, 'fsdp', [(i, (i + r) % count) for i in range(count)])  2.99 us
  transfers between devices with their start and end apart: 26, of which 10 were waited for; matrix products, arithmetic and copies ran while one was open for 7% of the time, Pallas kernels for 17%

profile of v5, /device:TPU:8, one launch (start us, length us, event | category | flops | bytes accessed | tf_op | source)
XLA Modules:
  0.0 91.1 jit_solution(17847707176109102807)
XLA Ops:
  3.9 1.6 %collective-permute-start = (bf16[128,2048]{1,0:T(8,128)(2,1)}, bf16[128,2048]{1,0:T(8,128)(2,1)S(1)}, u32[]{:S(2)}, u32[]{:S(2)}) collective-permute-start(bf16[128,2048]{1,0:T(8,128)(2,1)} %bitcast.10), channel_id=1, source_target_pairs={{0,1},{1,0},{2,3},{3,2},{4,5},{5,4},{6,7},{7,6},{8,9},{9,8},{10,11... | collective-permute-start | bytes 1572872 | tf_op jit(solution)/shard_map/ppermute | solution.py:203
  6.1 1.6 %collective-permute-start.3 = (bf16[4,128,128]{2,1,0:T(8,128)(2,1)S(1)}, bf16[4,128,128]{2,1,0:T(8,128)(2,1)S(1)}, u32[]{:S(2)}, u32[]{:S(2)}) collective-permute-start(bf16[4,128,128]{2,1,0:T(8,128)(2,1)S(1)} %get-tuple-element.39), channel_id=1, source_target_pairs={{0,4},{2,6},{4,0},{6,2},{8,12},{10,14},{12,8},{14,10},{16,20},{18,... | collective-permute-start | bytes 393224 | tf_op jit(solution)/shard_map/ppermute | solution.py:199
  7.7 2.9 %convolution_convert_fusion.1.refs_3_.refs_2_ = bf16[128,1024]{1,0:T(8,128)(2,1)S(1)} fusion(bf16[2048,1024]{1,0:T(8,128)(2,1)} %param.9, bf16[1,128,2048]{2,1,0:T(8,128)(2,1)S(1)} %copy-done.5), kind=kOutput, calls=%fused_computation.5 | convolution fusion | flops 537001984 | bytes 4980736 | tf_op jit(solution)/shard_map/dot_general | solution.py:23
  12.8 3.5 %collective-permute-start.6 = (bf16[4,128,128]{2,1,0:T(8,128)(2,1)S(1)}, bf16[4,128,128]{2,1,0:T(8,128)(2,1)S(1)}, u32[]{:S(2)}, u32[]{:S(2)}) collective-permute-start(bf16[4,128,128]{2,1,0:T(8,128)(2,1)S(1)} %shard_map.86), channel_id=1, source_target_pairs={{0,8},{2,10},{4,12},{6,14},{8,16},{10,18},{12,20},{14,22},{16,24},... | collective-permute-start | bytes 393224 | tf_op jit(solution)/shard_map/ppermute | solution.py:258
  16.3 2.3 %collective-permute-start.5 = (bf16[4,128,128]{2,1,0:T(8,128)(2,1)S(1)}, bf16[4,128,128]{2,1,0:T(8,128)(2,1)S(1)}, u32[]{:S(2)}, u32[]{:S(2)}) collective-permute-start(bf16[4,128,128]{2,1,0:T(8,128)(2,1)S(1)} %shard_map.86), channel_id=1, source_target_pairs={{0,16},{2,18},{4,20},{6,22},{8,24},{10,26},{12,28},{14,30},{1,17},... | collective-permute-start | bytes 393224 | tf_op jit(solution)/shard_map/ppermute | solution.py:258
  20.0 1.5 %collective-permute-start.1 = (bf16[128,1024]{1,0:T(8,128)(2,1)S(1)}, bf16[128,1024]{1,0:T(8,128)(2,1)S(1)}, u32[]{:S(2)}, u32[]{:S(2)}) collective-permute-start(bf16[128,1024]{1,0:T(8,128)(2,1)S(1)} %convolution_convert_fusion.refs_6_), channel_id=1, source_target_pairs={{0,1},{1,0},{2,3},{3,2},{4,5},{5,4},{6,7},{7,6},{8,9},{9,8},{10,11... | collective-permute-start | bytes 786440 | tf_op jit(solution)/shard_map/ppermute | solution.py:203
  22.2 5.0 %collective-permute-done.5.refs_4_ = bf16[4,128,128]{2,1,0:T(8,128)(2,1)S(1)} collective-permute-done((bf16[4,128,128]{2,1,0:T(8,128)(2,1)S(1)}, bf16[4,128,128]{2,1,0:T(8,128)(2,1)S(1)}, u32[]{:S(2)}, u32[]{:S(2)}) %collective-permute-start.5) | collective-permute-done | bytes 131104 | tf_op jit(solution)/shard_map/ppermute | solution.py:258
  27.8 1.3 %collective-permute-start.8 = (bf16[4,128,128]{2,1,0:T(8,128)(2,1)S(1)}, bf16[4,128,128]{2,1,0:T(8,128)(2,1)S(1)}, u32[]{:S(2)}, u32[]{:S(2)}) collective-permute-start(bf16[4,128,128]{2,1,0:T(8,128)(2,1)S(1)} %get-tuple-element.44), channel_id=1, source_target_pairs={{0,4},{2,6},{4,0},{6,2},{8,12},{10,14},{12,8},{14,10},{16,20},{18,... | collective-permute-start | bytes 393224 | tf_op jit(solution)/shard_map/ppermute | solution.py:199
  30.7 3.6 %collective-permute-done.8.refs_2_ = bf16[4,128,128]{2,1,0:T(8,128)(2,1)S(1)} collective-permute-done((bf16[4,128,128]{2,1,0:T(8,128)(2,1)S(1)}, bf16[4,128,128]{2,1,0:T(8,128)(2,1)S(1)}, u32[]{:S(2)}, u32[]{:S(2)}) %collective-permute-start.8) | collective-permute-done | bytes 131104 | tf_op jit(solution)/shard_map/ppermute | solution.py:199
  36.6 1.6 %collective-permute-done.11.refs_3_.refs_2_ = bf16[2,128,512]{2,1,0:T(8,128)(2,1)S(1)} collective-permute-done((bf16[2,128,512]{2,1,0:T(8,128)(2,1)S(1)}, bf16[2,128,512]{2,1,0:T(8,128)(2,1)S(1)}, u32[]{:S(2)}, u32[]{:S(2)}) %collective-permute-start.11) | collective-permute-done | bytes 262176 | tf_op jit(solution)/shard_map/ppermute | solution.py:199
  39.9 1.5 %shard_map.94 = (bf16[128,1024]{1,0:T(8,128)(2,1)S(1)}, bf16[128,1024]{1,0:T(8,128)(2,1)S(1)}) custom-call(s32[4]{0:T(128)S(1)} %pad_add_fusion.refs_0_, bf16[1,128,2048]{2,1,0:T(8,128)(2,1)S(1)} %copy-done.4, bf16[1,128,2048]{2,1,0:T(8,128)(2,1)S(1)} %copy-done.1, bf16[1,128,2048]{2,1,0:T(8,128)(2,1)S(1)} %copy-done.3, ...), custom_call_target="tpu_custom_call" | custom-call | tf_op jit(solution)/shard_map/pallas_call | solution.py:33
  41.3 2.0 %collective-permute-start.20 = (bf16[128,1024]{1,0:T(8,128)(2,1)S(1)}, bf16[128,1024]{1,0:T(8,128)(2,1)S(1)}, u32[]{:S(2)}, u32[]{:S(2)}) collective-permute-start(bf16[128,1024]{1,0:T(8,128)(2,1)S(1)} %get-tuple-element.63), channel_id=1, source_target_pairs={{0,5},{1,4},{2,7},{3,6},{4,1},{5,0},{6,3},{7,2},{8,13},{9,12},{10,... | collective-permute-start | bytes 786440 | tf_op jit(solution)/shard_map/ppermute | solution.py:210
  45.4 1.9 %collective-permute-start.14 = (bf16[4,128,128]{2,1,0:T(8,128)(2,1)S(1)}, bf16[4,128,128]{2,1,0:T(8,128)(2,1)S(1)}, u32[]{:S(2)}, u32[]{:S(2)}) collective-permute-start(bf16[4,128,128]{2,1,0:T(8,128)(2,1)S(1)} %shard_map.95.refs_7_.refs_1_), channel_id=1, source_target_pairs={{8,0},{10,2},{12,4},{14,6},{16,8},{18,10},{20,12},{22,14},{24,16},... | collective-permute-start | bytes 393224 | tf_op jit(solution)/shard_map/ppermute | solution.py:258
  48.0 4.3 %collective-permute-done.14.refs_2_.refs_3_ = bf16[4,128,128]{2,1,0:T(8,128)(2,1)S(1)} collective-permute-done((bf16[4,128,128]{2,1,0:T(8,128)(2,1)S(1)}, bf16[4,128,128]{2,1,0:T(8,128)(2,1)S(1)}, u32[]{:S(2)}, u32[]{:S(2)}) %collective-permute-start.14) | collective-permute-done | bytes 131104 | tf_op jit(solution)/shard_map/ppermute | solution.py:258
  52.9 3.0 %collective-permute-done.19.refs_3_ = bf16[128,1024]{1,0:T(8,128)(2,1)S(1)} collective-permute-done((bf16[128,1024]{1,0:T(8,128)(2,1)S(1)}, bf16[128,1024]{1,0:T(8,128)(2,1)S(1)}, u32[]{:S(2)}, u32[]{:S(2)}) %collective-permute-start.19) | collective-permute-done | bytes 262176 | tf_op jit(solution)/shard_map/ppermute | solution.py:203
  57.1 1.3 %collective-permute-start.15 = (bf16[4,128,128]{2,1,0:T(8,128)(2,1)S(1)}, bf16[4,128,128]{2,1,0:T(8,128)(2,1)S(1)}, u32[]{:S(2)}, u32[]{:S(2)}) collective-permute-start(bf16[4,128,128]{2,1,0:T(8,128)(2,1)S(1)} %shard_map.98.refs_5_), channel_id=1, source_target_pairs={{16,0},{18,2},{20,4},{22,6},{24,8},{26,10},{28,12},{30,14},{17,1},... | collective-permute-start | bytes 393224 | tf_op jit(solution)/shard_map/ppermute | solution.py:258
  58.4 1.2 %collective-permute-done.17 = bf16[256,512]{1,0:T(8,128)(2,1)S(1)} collective-permute-done((bf16[256,512]{1,0:T(8,128)(2,1)S(1)}, bf16[256,512]{1,0:T(8,128)(2,1)S(1)}, u32[]{:S(2)}, u32[]{:S(2)}) %collective-permute-start.17) | collective-permute-done | bytes 262176 | tf_op jit(solution)/shard_map/ppermute | solution.py:199
  59.6 1.3 %fusion.17 = (bf16[512,1024]{1,0:T(8,128)(2,1)S(1)}, f32[512,1024]{1,0:T(8,128)S(1)}) fusion(bf16[512,1024]{1,0:T(8,128)(2,1)S(1)} %collective-permute-done.21, bf16[512,1024]{1,0:T(8,128)(2,1)S(1)} %shard_map.100, bf16[256,512]{1,0:T(8,128)(2,1)S(1)} %collective-permute-done.17, bf16[256,512]{1,0:T(8,128)(2,1)S(1)} %collective-permute-done.13.refs_7_, ...), kind=kOutput, calls=%fused_computation.21 | convolution fusion | flops 1082654720 | bytes 6291456 | tf_op jit(solution)/shard_map/dot_general | solution.py:23
  61.0 3.4 %collective-permute-start.23 = (bf16[128,1024]{1,0:T(8,128)(2,1)S(1)}, bf16[128,1024]{1,0:T(8,128)(2,1)S(1)}, u32[]{:S(2)}, u32[]{:S(2)}) collective-permute-start(bf16[128,1024]{1,0:T(8,128)(2,1)S(1)} %get-tuple-element.69), channel_id=1, source_target_pairs={{0,16},{2,18},{4,20},{6,22},{8,24},{10,26},{12,28},{14,30},{16,0},... | collective-permute-start | bytes 786440 | tf_op jit(solution)/shard_map/ppermute | solution.py:199
  67.3 5.2 %shard_map.96 = (bf16[1,128,2048]{2,1,0:T(8,128)(2,1)}, f32[128,2048]{1,0:T(8,128)S(1)}, f32[128,2048]{1,0:T(8,128)S(1)}, f32[8,128]{1,0:T(8,128)}) custom-call(s32[4]{0:T(128)S(1)} %pad_add_fusion.refs_0_, bf16[1,128,2048]{2,1,0:T(8,128)(2,1)S(1)} %copy-done.4, bf16[1,128,2048]{2,1,0:T(8,128)(2,1)S(1)} %copy-done.1, bf16[1,128,2048]{2,1,0:T(8,128)(2,1)S(1)} %copy-done.3, ...), custom_call_target="tpu_custom_call" | custom-call | tf_op jit(solution)/shard_map/pallas_call | solution.py:33
  72.5 1.5 %collective-permute-done.23.refs_6_ = bf16[128,1024]{1,0:T(8,128)(2,1)S(1)} collective-permute-done((bf16[128,1024]{1,0:T(8,128)(2,1)S(1)}, bf16[128,1024]{1,0:T(8,128)(2,1)S(1)}, u32[]{:S(2)}, u32[]{:S(2)}) %collective-permute-start.23) | collective-permute-done | bytes 262176 | tf_op jit(solution)/shard_map/ppermute | solution.py:199
  74.0 1.1 %collective-permute-done.22.refs_5_ = bf16[128,1024]{1,0:T(8,128)(2,1)S(1)} collective-permute-done((bf16[128,1024]{1,0:T(8,128)(2,1)S(1)}, bf16[128,1024]{1,0:T(8,128)(2,1)S(1)}, u32[]{:S(2)}, u32[]{:S(2)}) %collective-permute-start.22) | collective-permute-done | bytes 262176 | tf_op jit(solution)/shard_map/ppermute | solution.py:199
  75.8 12.3 %collective-permute-done.25 = bf16[128,1024]{1,0:T(8,128)(2,1)S(1)} collective-permute-done((bf16[128,1024]{1,0:T(8,128)(2,1)S(1)}, bf16[128,1024]{1,0:T(8,128)(2,1)S(1)}, u32[]{:S(2)}, u32[]{:S(2)}) %collective-permute-start.25) | collective-permute-done | bytes 262176 | tf_op jit(solution)/shard_map/ppermute | solution.py:199
  89.1 2.0 %shard_map.102 = (bf16[1,128,2048]{2,1,0:T(8,128)(2,1)}, bf16[1,128,2048]{2,1,0:T(8,128)(2,1)}) custom-call(s32[4]{0:T(128)S(1)} %pad_add_fusion.refs_0_, bf16[1,128,2048]{2,1,0:T(8,128)(2,1)S(1)} %copy-done.1, bf16[1,128,2048]{2,1,0:T(8,128)(2,1)S(1)} %copy-done.3, f32[128,2048]{1,0:T(8,128)S(1)} %get-tuple-element.56.refs_3_, ...), custom_call_target="tpu_custom_call" | custom-call | tf_op jit(solution)/shard_map/pallas_call | solution.py:33
  (67 shorter events, 23.2 us)
Async XLA Ops:
  3.9 15.3 %collective-permute-start = (bf16[128,2048]{1,0:T(8,128)(2,1)}, bf16[128,2048]{1,0:T(8,128)(2,1)S(1)}, u32[]{:S(2)}, u32[]{:S(2)}) collective-permute-start(bf16[128,2048]{1,0:T(8,128)(2,1)} %bitcast.10), channel_id=1, source_target_pairs={{0,1},{1,0},{2,3},{3,2},{4,5},{5,4},{6,7},{7,6},{8,9},{9,8},{10,11... | collective-permute-start | bytes 1572872 | tf_op jit(solution)/shard_map/ppermute | solution.py:203
  6.1 6.1 %collective-permute-start.3 = (bf16[4,128,128]{2,1,0:T(8,128)(2,1)S(1)}, bf16[4,128,128]{2,1,0:T(8,128)(2,1)S(1)}, u32[]{:S(2)}, u32[]{:S(2)}) collective-permute-start(bf16[4,128,128]{2,1,0:T(8,128)(2,1)S(1)} %get-tuple-element.39), channel_id=1, source_target_pairs={{0,4},{2,6},{4,0},{6,2},{8,12},{10,14},{12,8},{14,10},{16,20},{18,... | collective-permute-start | bytes 393224 | tf_op jit(solution)/shard_map/ppermute | solution.py:199
  11.3 10.3 %collective-permute-start.7 = (bf16[2,128,512]{2,1,0:T(8,128)(2,1)S(1)}, bf16[2,128,512]{2,1,0:T(8,128)(2,1)S(1)}, u32[]{:S(2)}, u32[]{:S(2)}) collective-permute-start(bf16[2,128,512]{2,1,0:T(8,128)(2,1)S(1)} %get-tuple-element.41), channel_id=1, source_target_pairs={{0,4},{2,6},{4,0},{6,2},{8,12},{10,14},{12,8},{14,10},{16,20},{18,... | collective-permute-start | bytes 786440 | tf_op jit(solution)/shard_map/ppermute | solution.py:199
  12.8 9.4 %collective-permute-start.6 = (bf16[4,128,128]{2,1,0:T(8,128)(2,1)S(1)}, bf16[4,128,128]{2,1,0:T(8,128)(2,1)S(1)}, u32[]{:S(2)}, u32[]{:S(2)}) collective-permute-start(bf16[4,128,128]{2,1,0:T(8,128)(2,1)S(1)} %shard_map.86), channel_id=1, source_target_pairs={{0,8},{2,10},{4,12},{6,14},{8,16},{10,18},{12,20},{14,22},{16,24},... | collective-permute-start | bytes 393224 | tf_op jit(solution)/shard_map/ppermute | solution.py:258
  16.3 10.9 %collective-permute-start.5 = (bf16[4,128,128]{2,1,0:T(8,128)(2,1)S(1)}, bf16[4,128,128]{2,1,0:T(8,128)(2,1)S(1)}, u32[]{:S(2)}, u32[]{:S(2)}) collective-permute-start(bf16[4,128,128]{2,1,0:T(8,128)(2,1)S(1)} %shard_map.86), channel_id=1, source_target_pairs={{0,16},{2,18},{4,20},{6,22},{8,24},{10,26},{12,28},{14,30},{1,17},... | collective-permute-start | bytes 393224 | tf_op jit(solution)/shard_map/ppermute | solution.py:258
  18.6 8.6 %collective-permute-start.4 = (bf16[4,128,128]{2,1,0:T(8,128)(2,1)S(1)}, bf16[4,128,128]{2,1,0:T(8,128)(2,1)S(1)}, u32[]{:S(2)}, u32[]{:S(2)}) collective-permute-start(bf16[4,128,128]{2,1,0:T(8,128)(2,1)S(1)} %shard_map.86), channel_id=1, source_target_pairs={{0,24},{2,26},{4,28},{6,30},{1,25},{3,27},{5,29},{7,31}} | collective-permute-start | bytes 393224 | tf_op jit(solution)/shard_map/ppermute | solution.py:258
  20.0 14.9 %collective-permute-start.1 = (bf16[128,1024]{1,0:T(8,128)(2,1)S(1)}, bf16[128,1024]{1,0:T(8,128)(2,1)S(1)}, u32[]{:S(2)}, u32[]{:S(2)}) collective-permute-start(bf16[128,1024]{1,0:T(8,128)(2,1)S(1)} %convolution_convert_fusion.refs_6_), channel_id=1, source_target_pairs={{0,1},{1,0},{2,3},{3,2},{4,5},{5,4},{6,7},{7,6},{8,9},{9,8},{10,11... | collective-permute-start | bytes 786440 | tf_op jit(solution)/shard_map/ppermute | solution.py:203
  27.8 6.4 %collective-permute-start.8 = (bf16[4,128,128]{2,1,0:T(8,128)(2,1)S(1)}, bf16[4,128,128]{2,1,0:T(8,128)(2,1)S(1)}, u32[]{:S(2)}, u32[]{:S(2)}) collective-permute-start(bf16[4,128,128]{2,1,0:T(8,128)(2,1)S(1)} %get-tuple-element.44), channel_id=1, source_target_pairs={{0,4},{2,6},{4,0},{6,2},{8,12},{10,14},{12,8},{14,10},{16,20},{18,... | collective-permute-start | bytes 393224 | tf_op jit(solution)/shard_map/ppermute | solution.py:199
  29.8 8.5 %collective-permute-start.11 = (bf16[2,128,512]{2,1,0:T(8,128)(2,1)S(1)}, bf16[2,128,512]{2,1,0:T(8,128)(2,1)S(1)}, u32[]{:S(2)}, u32[]{:S(2)}) collective-permute-start(bf16[2,128,512]{2,1,0:T(8,128)(2,1)S(1)} %get-tuple-element.50), channel_id=1, source_target_pairs={{0,4},{2,6},{4,0},{6,2},{8,12},{10,14},{12,8},{14,10},{16,20},{18,... | collective-permute-start | bytes 786440 | tf_op jit(solution)/shard_map/ppermute | solution.py:199
  36.1 3.8 %collective-permute-start.13 = (bf16[256,512]{1,0:T(8,128)(2,1)S(1)}, bf16[256,512]{1,0:T(8,128)(2,1)S(1)}, u32[]{:S(2)}, u32[]{:S(2)}) collective-permute-start(bf16[256,512]{1,0:T(8,128)(2,1)S(1)} %get-tuple-element.53), channel_id=1, source_target_pairs={{0,2},{2,0},{4,6},{6,4},{8,10},{10,8},{12,14},{14,12},{16,18},{18,... | collective-permute-start | bytes 786440 | tf_op jit(solution)/shard_map/ppermute | solution.py:199
  36.5 3.3 %collective-permute-start.9 = (bf16[2,4,128,128]{3,2,1,0:T(8,128)(2,1)S(1)}, bf16[2,4,128,128]{3,2,1,0:T(8,128)(2,1)S(1)}, u32[]{:S(2)}, u32[]{:S(2)}) collective-permute-start(bf16[2,4,128,128]{3,2,1,0:T(8,128)(2,1)S(1)} %get-tuple-element.47), channel_id=1, source_target_pairs={{0,2},{2,0},{4,6},{6,4},{8,10},{10,8},{12,14},{14,12},{16,18},{18,... | collective-permute-start | bytes 786440 | tf_op jit(solution)/shard_map/ppermute | solution.py:199
  38.8 6.0 %collective-permute-start.12 = (bf16[4,128,128]{2,1,0:T(8,128)(2,1)S(1)}, bf16[4,128,128]{2,1,0:T(8,128)(2,1)S(1)}, u32[]{:S(2)}, u32[]{:S(2)}) collective-permute-start(bf16[4,128,128]{2,1,0:T(8,128)(2,1)S(1)} %get-tuple-element.52), channel_id=1, source_target_pairs={{0,4},{2,6},{4,0},{6,2},{8,12},{10,14},{12,8},{14,10},{16,20},{18,... | collective-permute-start | bytes 393224 | tf_op jit(solution)/shard_map/ppermute | solution.py:199
  41.3 11.6 %collective-permute-start.20 = (bf16[128,1024]{1,0:T(8,128)(2,1)S(1)}, bf16[128,1024]{1,0:T(8,128)(2,1)S(1)}, u32[]{:S(2)}, u32[]{:S(2)}) collective-permute-start(bf16[128,1024]{1,0:T(8,128)(2,1)S(1)} %get-tuple-element.63), channel_id=1, source_target_pairs={{0,5},{1,4},{2,7},{3,6},{4,1},{5,0},{6,3},{7,2},{8,13},{9,12},{10,... | collective-permute-start | bytes 786440 | tf_op jit(solution)/shard_map/ppermute | solution.py:210
  43.3 12.6 %collective-permute-start.19 = (bf16[128,1024]{1,0:T(8,128)(2,1)S(1)}, bf16[128,1024]{1,0:T(8,128)(2,1)S(1)}, u32[]{:S(2)}, u32[]{:S(2)}) collective-permute-start(bf16[128,1024]{1,0:T(8,128)(2,1)S(1)} %get-tuple-element.63), channel_id=1, source_target_pairs={{0,1},{1,0},{2,3},{3,2},{4,5},{5,4},{6,7},{7,6},{8,9},{9,8},{10,11... | collective-permute-start | bytes 786440 | tf_op jit(solution)/shard_map/ppermute | solution.py:203
  43.9 11.9 %collective-permute-start.18 = (bf16[128,1024]{1,0:T(8,128)(2,1)S(1)}, bf16[128,1024]{1,0:T(8,128)(2,1)S(1)}, u32[]{:S(2)}, u32[]{:S(2)}) collective-permute-start(bf16[128,1024]{1,0:T(8,128)(2,1)S(1)} %get-tuple-element.54.refs_3_.refs_1_), channel_id=1, source_target_pairs={{0,4},{2,6},{4,0},{6,2},{8,12},{10,14},{12,8},{14,10},{16,20},{18,... | collective-permute-start | bytes 786440 | tf_op jit(solution)/shard_map/ppermute | solution.py:199
  45.4 6.9 %collective-permute-start.14 = (bf16[4,128,128]{2,1,0:T(8,128)(2,1)S(1)}, bf16[4,128,128]{2,1,0:T(8,128)(2,1)S(1)}, u32[]{:S(2)}, u32[]{:S(2)}) collective-permute-start(bf16[4,128,128]{2,1,0:T(8,128)(2,1)S(1)} %shard_map.95.refs_7_.refs_1_), channel_id=1, source_target_pairs={{8,0},{10,2},{12,4},{14,6},{16,8},{18,10},{20,12},{22,14},{24,16},... | collective-permute-start | bytes 393224 | tf_op jit(solution)/shard_map/ppermute | solution.py:258
  56.5 3.1 %collective-permute-start.21 = (bf16[512,1024]{1,0:T(8,128)(2,1)S(1)}, bf16[512,1024]{1,0:T(8,128)(2,1)S(1)}, u32[]{:S(2)}, u32[]{:S(2)}) collective-permute-start(bf16[512,1024]{1,0:T(8,128)(2,1)S(1)} %shard_map.100), channel_id=1, source_target_pairs={{0,2},{2,0},{4,6},{6,4},{8,10},{10,8},{12,14},{14,12},{16,18},{18,... | collective-permute-start | bytes 3145736 | tf_op jit(solution)/shard_map/ppermute | solution.py:199
  56.6 3.0 %collective-permute-start.17 = (bf16[256,512]{1,0:T(8,128)(2,1)S(1)}, bf16[256,512]{1,0:T(8,128)(2,1)S(1)}, u32[]{:S(2)}, u32[]{:S(2)}) collective-permute-start(bf16[256,512]{1,0:T(8,128)(2,1)S(1)} %get-tuple-element.62), channel_id=1, source_target_pairs={{0,2},{2,0},{4,6},{6,4},{8,10},{10,8},{12,14},{14,12},{16,18},{18,... | collective-permute-start | bytes 786440 | tf_op jit(solution)/shard_map/ppermute | solution.py:199
  57.1 8.5 %collective-permute-start.15 = (bf16[4,128,128]{2,1,0:T(8,128)(2,1)S(1)}, bf16[4,128,128]{2,1,0:T(8,128)(2,1)S(1)}, u32[]{:S(2)}, u32[]{:S(2)}) collective-permute-start(bf16[4,128,128]{2,1,0:T(8,128)(2,1)S(1)} %shard_map.98.refs_5_), channel_id=1, source_target_pairs={{16,0},{18,2},{20,4},{22,6},{24,8},{26,10},{28,12},{30,14},{17,1},... | collective-permute-start | bytes 393224 | tf_op jit(solution)/shard_map/ppermute | solution.py:258
  61.0 13.1 %collective-permute-start.23 = (bf16[128,1024]{1,0:T(8,128)(2,1)S(1)}, bf16[128,1024]{1,0:T(8,128)(2,1)S(1)}, u32[]{:S(2)}, u32[]{:S(2)}) collective-permute-start(bf16[128,1024]{1,0:T(8,128)(2,1)S(1)} %get-tuple-element.69), channel_id=1, source_target_pairs={{0,16},{2,18},{4,20},{6,22},{8,24},{10,26},{12,28},{14,30},{16,0},... | collective-permute-start | bytes 786440 | tf_op jit(solution)/shard_map/ppermute | solution.py:199
  64.4 10.7 %collective-permute-start.22 = (bf16[128,1024]{1,0:T(8,128)(2,1)S(1)}, bf16[128,1024]{1,0:T(8,128)(2,1)S(1)}, u32[]{:S(2)}, u32[]{:S(2)}) collective-permute-start(bf16[128,1024]{1,0:T(8,128)(2,1)S(1)} %get-tuple-element.70), channel_id=1, source_target_pairs={{0,8},{2,10},{4,12},{6,14},{8,0},{10,2},{12,4},{14,6},{16,24},{18,... | collective-permute-start | bytes 786440 | tf_op jit(solution)/shard_map/ppermute | solution.py:199
  64.4 23.8 %collective-permute-start.25 = (bf16[128,1024]{1,0:T(8,128)(2,1)S(1)}, bf16[128,1024]{1,0:T(8,128)(2,1)S(1)}, u32[]{:S(2)}, u32[]{:S(2)}) collective-permute-start(bf16[128,1024]{1,0:T(8,128)(2,1)S(1)} %get-tuple-element.68), channel_id=1, source_target_pairs={{0,24},{2,26},{4,28},{6,30},{8,16},{10,18},{12,20},{14,22},{16,8},... | collective-permute-start | bytes 786440 | tf_op jit(solution)/shard_map/ppermute | solution.py:199
  66.2 6.3 %collective-permute-start.16 = (bf16[4,128,128]{2,1,0:T(8,128)(2,1)S(1)}, bf16[4,128,128]{2,1,0:T(8,128)(2,1)S(1)}, u32[]{:S(2)}, u32[]{:S(2)}) collective-permute-start(bf16[4,128,128]{2,1,0:T(8,128)(2,1)S(1)} %get-tuple-element.61), channel_id=1, source_target_pairs={{0,4},{2,6},{4,0},{6,2},{8,12},{10,14},{12,8},{14,10},{16,20},{18,... | collective-permute-start | bytes 393224 | tf_op jit(solution)/shard_map/ppermute | solution.py:199
  75.7 13.4 %collective-permute-start.24 = (bf16[2,4,128,128]{3,2,1,0:T(8,128)(2,1)S(1)}, bf16[2,4,128,128]{3,2,1,0:T(8,128)(2,1)S(1)}, u32[]{:S(2)}, u32[]{:S(2)}) collective-permute-start(bf16[2,4,128,128]{3,2,1,0:T(8,128)(2,1)S(1)} %get-tuple-element.65), channel_id=1, source_target_pairs={{0,2},{2,0},{4,6},{6,4},{8,10},{10,8},{12,14},{14,12},{16,18},{18,... | collective-permute-start | bytes 786440 | tf_op jit(solution)/shard_map/ppermute | solution.py:199
  (9 other events, 60.4 us)
